TPU v7x, 32 devices: a whole 2x2x4 slice. The times are simulated.
32 devices in a mesh: item: 8 (over y, x, core), week: 4 (over z).
Axes of the slice: x: 2, y: 2, z: 4, core: 2. Of those that a mesh axis runs over, the one named last changes fastest.
Arguments:
- counts: int32 [128, 256, 16384], P(None, 'week', 'item'), may hold values from 0 to 7, as said below
- user_factor: float32 [128, 64], replicated, may hold values from 0.3 to 1.5
- item_factor: float32 [16384, 64], P('item'), may hold values from 0.001 to 12, as said below
- week_factor: float32 [256, 64], P('week'), may hold values from 0.001 to 1.5, as said below
Outputs:
- updated_users: float32 [128, 64], replicated
Inputs may be any that keep to these rules, and one draw needn't show every extreme that they name: `counts`: every user has at least one positive count. `item_factor`: positive entries. `week_factor`: positive entries.
All inputs are finite; a program needn't handle non-finite values.
Results may differ from a plain program's by a relative error of at most 0.0003.
Values sent between devices are 32-bit elements; how exact they have to be, the bound alone decides.
No kernel may reach another device: no remote copies, remote signals or barrier semaphores. Data moves between devices by JAX's collectives and lax.ppermute only.
A program may use at most 320 MiB of HBM per device.

v0:
```python
import jax
import jax.numpy as jnp
from jax import lax
from jax.sharding import PartitionSpec as P

ITERS = 3


def combine(partials):
    return lax.psum(partials, ("item", "week"))


def per_device(counts, user_factor, item_factor, week_factor):
    rank_width = user_factor.shape[1]
    user_rows = user_factor.shape[0]
    khatri_rao = (week_factor[:, None, :] * item_factor[None, :, :]).reshape(-1, rank_width)
    flat_counts = counts.reshape(user_rows, -1)
    local_items = jnp.sum(item_factor, axis=0)
    local_weeks = jnp.sum(week_factor, axis=0)
    denominator = None
    item_totals = lax.psum(local_items, "item")
    week_totals = lax.psum(local_weeks, "week")
    denominator = item_totals * week_totals
    factor = user_factor
    for iteration in range(ITERS):
        model = jnp.dot(factor, khatri_rao.T, precision=lax.Precision.HIGHEST)
        ratio = flat_counts.astype(jnp.float32) / model
        partial_phi = jnp.dot(ratio, khatri_rao, precision=lax.Precision.HIGHEST)
        summed = combine((partial_phi,))[0]
        factor = factor * summed / denominator[None, :]
    return factor


def solution(mesh):
    placed = (P(None, "week", "item"), P(), P("item", None), P("week", None))
    return jax.shard_map(per_device, mesh=mesh, in_specs=placed, out_specs=P(), check_vma=False)
```

profile of v0, /device:TPU:0, one launch (start us, length us, event | category | flops | bytes accessed | tf_op | source)
XLA Modules:
  0.0 766.5 jit_solution(12086018615631632185)
XLA Ops:
  0.0 1.2 reduce_sum.18
  1.2 15.1 %psum.36 = f32[64]{0:T(128)S(1)} all-reduce(f32[64]{0:T(128)S(1)} %reduce_sum.18), channel_id=1, replica_groups=mesh['item'=8,'week'=4] {'item'}, use_global_device_ids=true, to_apply=%region_2.0 | all-reduce | flops 64 | bytes 512 | tf_op jit(solution)/shard_map/psum | solution.py:21
  16.3 0.8 reduce_sum.19
  17.1 12.0 %psum.37 = f32[64]{0:T(128)S(1)} all-reduce(f32[64]{0:T(128)S(1)} %reduce_sum.19), channel_id=1, replica_groups=mesh['item'=8,'week'=4] {'week'}, use_global_device_ids=true, to_apply=%region_4.0 | all-reduce | flops 64 | bytes 512 | tf_op jit(solution)/shard_map/psum | solution.py:22
  29.0 0.5 mul.34
  29.6 4.0 multiply_bitcast_fusion
  33.6 11.0 %copy.12 = f32[64,8,8,2048]{3,2,0,1:T(8,128)} copy(f32[64,8,8,2048]{3,2,1,0:T(8,128)S(1)} %multiply_bitcast_fusion) | data formatting | bytes 67108864 | tf_op jit(solution)/shard_map/mul | solution.py:16
  44.6 43.4 %convert_element_type.8 = f32[128,64,2048]{2,1,0:T(8,128)} convert(s32[128,64,2048]{2,1,0:T(8,128)} %param.4) | non-fusion elementwise | flops 16777216 | bytes 134217728 | tf_op jit(solution)/shard_map/convert_element_type | solution.py:27
  88.0 0.0 copy-start
  88.0 70.4 %copy.6 = f32[128,64,2048]{0,2,1:T(8,128)} copy(f32[128,64,2048]{2,1,0:T(8,128)} %convert_element_type.8) | data formatting | bytes 134217728 | tf_op jit(solution)/shard_map/convert_element_type | solution.py:27
  158.5 0.0 copy-done
  158.5 113.7 %fusion = f32[128,131072]{0,1:T(8,128)} fusion(f32[128,131072]{0,1:T(8,128)} %bitcast, f32[131072,64]{0,1:T(8,128)} %bitcast.20, f32[128,64]{0,1:T(8,128)S(1)} %copy-done), kind=kOutput, calls=%fused_computation.1 | convolution fusion | flops 12901679104 | bytes 167804928 | tf_op jit(solution)/shard_map/dot_general | solution.py:26
  272.2 0.0 copy-start.1
  272.2 48.9 %fusion.1 = f32[128,64]{0,1:T(8,128)S(1)} fusion(f32[128,131072]{0,1:T(8,128)} %fusion, f32[131072,64]{0,1:T(8,128)} %bitcast.21), kind=kOutput, calls=%fused_computation.8 | convolution fusion | flops 12884901888 | bytes 100696064 | tf_op jit(solution)/shard_map/dot_general | solution.py:28
  321.2 37.0 %psum.35 = f32[128,64]{0,1:T(8,128)S(1)} all-reduce(f32[128,64]{0,1:T(8,128)S(1)} %fusion.1), channel_id=1, replica_groups=mesh['item'=8,'week'=4] {'item','week'}, use_global_device_ids=true, to_apply=%region_0.0 | all-reduce | flops 8192 | bytes 65536 | tf_op jit(solution)/shard_map/psum | solution.py:10
  358.2 0.0 copy-done.1
  358.2 114.4 %convolution_divide_fusion.1 = f32[128,131072]{0,1:T(8,128)} fusion(f32[128,131072]{0,1:T(8,128)} %bitcast, f32[131072,64]{0,1:T(8,128)} %bitcast.22, f32[128,64]{0,1:T(8,128)S(1)} %copy-done, f32[128,64]{0,1:T(8,128)S(1)} %psum.35, f32[64]{0:T(128)S(1)} %copy-done.1), kind=kOutput, calls=%fused_computation.3 | convolution fusion | flops 12901695488 | bytes 167837952 | tf_op jit(solution)/shard_map/dot_general | solution.py:26
  472.6 48.9 %fusion.2 = f32[128,64]{0,1:T(8,128)S(1)} fusion(f32[128,131072]{0,1:T(8,128)} %convolution_divide_fusion.1, f32[131072,64]{0,1:T(8,128)} %bitcast.23), kind=kOutput, calls=%fused_computation.9 | convolution fusion | flops 12884901888 | bytes 100696064 | tf_op jit(solution)/shard_map/dot_general | solution.py:28
  521.5 41.5 %psum.38 = f32[128,64]{0,1:T(8,128)S(1)} all-reduce(f32[128,64]{0,1:T(8,128)S(1)} %fusion.2), channel_id=1, replica_groups=mesh['item'=8,'week'=4] {'item','week'}, use_global_device_ids=true, to_apply=%region_5.0 | all-reduce | flops 8192 | bytes 65536 | tf_op jit(solution)/shard_map/psum | solution.py:10
  563.0 0.1 multiply_divide_fusion.1
  563.1 113.8 %convolution_divide_fusion = f32[128,131072]{0,1:T(8,128)} fusion(f32[128,131072]{0,1:T(8,128)} %bitcast, f32[128,64]{0,1:T(8,128)S(1)} %multiply_divide_fusion.1, f32[131072,64]{0,1:T(8,128)} %bitcast.24), kind=kOutput, calls=%fused_computation.2 | convolution fusion | flops 12901679104 | bytes 167804928 | tf_op jit(solution)/shard_map/dot_general | solution.py:26
  676.9 48.9 %fusion.3 = f32[128,64]{0,1:T(8,128)S(1)} fusion(f32[128,131072]{0,1:T(8,128)} %convolution_divide_fusion, f32[131072,64]{0,1:T(8,128)} %bitcast.25), kind=kOutput, calls=%fused_computation.10 | convolution fusion | flops 12884901888 | bytes 100696064 | tf_op jit(solution)/shard_map/dot_general | solution.py:28
  725.9 39.6 %psum.39 = f32[128,64]{0,1:T(8,128)S(1)} all-reduce(f32[128,64]{0,1:T(8,128)S(1)} %fusion.3), channel_id=1, replica_groups=mesh['item'=8,'week'=4] {'item','week'}, use_global_device_ids=true, to_apply=%region_6.0 | all-reduce | flops 8192 | bytes 65536 | tf_op jit(solution)/shard_map/psum | solution.py:10
  765.4 0.7 multiply_divide_fusion
Async XLA Ops:
  88.0 70.4 %copy-start = (f32[128,64]{0,1:T(8,128)S(1)}, f32[128,64]{0,1:T(8,128)}, u32[]{:S(2)}) copy-start(f32[128,64]{0,1:T(8,128)} %param.5) | copy-start | bytes 98308
  272.2 86.0 %copy-start.1 = (f32[64]{0:T(128)S(1)}, f32[64]{0:T(128)}, u32[]{:S(2)}) copy-start(f32[64]{0:T(128)} %mul.34) | copy-start | bytes 772
where the time goes:
time: 779 us; the launch traced here: 767 us
  matrix products  489 us (63%)
  blocking collectives  145 us (19%)
  local copies, waits for them, and re-layouts  81.4 us (10%)
  other arithmetic  50.7 us (7%)
    dot_general x3, matrix products, per_device(): model = jnp.dot(factor, khatri_rao.T, precision=lax.Precision.HIGHEST)  342 us
    dot_general x3, matrix products, per_device(): partial_phi = jnp.dot(ratio, khatri_rao, precision=lax.Precision.HIGHEST)  147 us
    psum x3, blocking collectives, combine(): return lax.psum(partials, ('item', 'week'))  118 us
    convert_element_type x1, local copies, waits for them, and re-layouts, per_device(): ratio = flat_counts.astype(jnp.float32) / model  70.4 us
    convert_element_type x1, other arithmetic, per_device(): ratio = flat_counts.astype(jnp.float32) / model  43.4 us

commit v1 on v0

v1 whole, which is shorter than its diff:
```python
import functools

import jax
import jax.numpy as jnp
from jax import lax
from jax.experimental import pallas as pl
from jax.experimental.pallas import tpu as pltpu
from jax.sharding import PartitionSpec as P

ITERS = 3
CHUNKS = 2
BLOCK_USERS = 8
COLUMNS = 256
AXES = ("item", "week")
F32, BF16 = jnp.float32, jnp.bfloat16


def split(x):
    high = x.astype(BF16)
    low = (x - high.astype(F32)).astype(BF16)
    return high, low


def pack(x):
    half = x.shape[0] // 2
    return jnp.concatenate([x[:half], x[half:]], axis=1)


def unpack(x):
    rank = x.shape[1] // 2
    return jnp.concatenate([x[:, :rank], x[:, rank:]], axis=0)


def prepare(item_t, model_w, phi_w):
    high, low = split(item_t)
    model_w[...] = jnp.concatenate([high, high, low, low], axis=0)
    phi_w[...] = jnp.concatenate([high.astype(F32), low.astype(F32)], axis=0).T.astype(BF16)


def column_sums(phi_w, week, n_item, n_week):
    rank = week.shape[1]
    ones = jnp.ones((8, phi_w.shape[0]), BF16)
    both = jnp.dot(ones, phi_w[...], preferred_element_type=F32)
    items = (both[:, :rank] + both[:, rank:]) * (1.0 / n_week)
    weeks = jnp.broadcast_to(jnp.sum(week, axis=0, keepdims=True), items.shape) * (1.0 / n_item)
    return jnp.concatenate([items, weeks], axis=1)


def phi_block(counts, factor, week, model_w, phi_w):
    users, weeks, items = counts.shape
    rank = factor.shape[1]
    rows = users * weeks
    scaled = (factor[:, None, :] * week[None, :, :]).reshape(rows, rank)
    high, low = split(scaled)
    lhs = jnp.concatenate([high, low, high, low], axis=1)
    total = None
    for start in range(0, items, COLUMNS):
        at = slice(start, start + COLUMNS)
        model = jnp.dot(lhs, model_w[:, at], preferred_element_type=F32)
        count = counts[:, :, at].reshape(rows, COLUMNS).astype(F32)
        ratio = count * pltpu.reciprocal(model, approx=True)
        rhs = phi_w[at, :]
        part = jnp.dot(
            jnp.concatenate(split(ratio), axis=1),
            jnp.concatenate([rhs, rhs], axis=0),
            preferred_element_type=F32,
        )
        total = part if total is None else total + part
    total = (total[:, :rank] + total[:, rank:]).reshape(users, weeks, rank)
    return jnp.sum(total * week[None, :, :], axis=1)


def step(counts, week, model_w, phi_w, factor_s, phi_s):
    i = pl.program_id(0)
    block = pl.ds(pl.multiple_of(i * BLOCK_USERS, BLOCK_USERS), BLOCK_USERS)
    phi_s[block, :] = phi_block(counts, factor_s[block, :], week[...], model_w, phi_w)


def first_kernel(chunk, n_item, n_week, prep, *refs):
    if prep:
        counts, factor_t, week, item_t, out, model_w, phi_w, factor_s, phi_s = refs
    else:
        counts, factor_t, week, model_w, phi_w, out, factor_s, phi_s = refs
    users = phi_s.shape[0]

    @pl.when(pl.program_id(0) == 0)
    def _():
        if prep:
            prepare(item_t[...], model_w, phi_w)
        factor_s[...] = factor_t[...].T[chunk * users:(chunk + 1) * users, :]

    step(counts, week, model_w, phi_w, factor_s, phi_s)

    @pl.when(pl.program_id(0) == pl.num_programs(0) - 1)
    def _():
        out[: users // 2, :] = pack(phi_s[...])
        out[users // 2:, :] = column_sums(phi_w, week[...], n_item, n_week)


def denominators(sums):
    rank = sums.shape[1] // 2
    return sums[:, :rank] * sums[:, rank:]


def second_kernel(chunk, counts, factor_t, gathered, week, model_w, phi_w, out, factor_s, den, phi_s):
    users = phi_s.shape[0]

    @pl.when(pl.program_id(0) == 0)
    def _():
        summed = jnp.sum(gathered[...], axis=0)
        den[...] = denominators(summed[users // 2:])
        old = factor_t[...].T[chunk * users:(chunk + 1) * users, :]
        factor_s[...] = old * unpack(summed[: users // 2]) / den[0:1, :]

    step(counts, week, model_w, phi_w, factor_s, phi_s)

    @pl.when(pl.program_id(0) == pl.num_programs(0) - 1)
    def _():
        out[...] = pack(phi_s[...])


def third_kernel(counts, factor, gathered, den, week, model_w, phi_w, out, factor_s, phi_s):
    @pl.when(pl.program_id(0) == 0)
    def _():
        summed = jnp.sum(gathered[...], axis=0)
        factor_s[...] = factor[...] * unpack(summed) / den[0:1, :]

    step(counts, week, model_w, phi_w, factor_s, phi_s)

    @pl.when(pl.program_id(0) == pl.num_programs(0) - 1)
    def _():
        out[...] = pack(phi_s[...])


def last_kernel(*refs):
    out = refs[-1]
    parts = []
    for factor, gathered, den in zip(refs[0:-1:3], refs[1:-1:3], refs[2:-1:3]):
        summed = jnp.sum(gathered[...], axis=0)
        parts.append(factor[...] * unpack(summed) / den[0:1, :])
    out[...] = jnp.concatenate(parts, axis=0).T


def whole(x):
    shape = x.shape
    return pl.BlockSpec(shape, lambda i: (0,) * len(shape))


def per_device(n_item, n_week, counts, user_factor, item_factor, week_factor):
    all_users, rank = user_factor.shape
    weeks, items = counts.shape[1:]
    users = all_users // CHUNKS
    factor_t, item_t = user_factor.T, item_factor.T

    def shape(dims, dtype=F32):
        return jax.ShapeDtypeStruct(dims, dtype)

    def run(kernel, chunk, operands, outs, scratch):
        steps = users // BLOCK_USERS
        return pl.pallas_call(
            kernel,
            grid=(steps,),
            in_specs=[pl.BlockSpec((BLOCK_USERS, weeks, items), lambda i: (chunk * steps + i, 0, 0))]
            + [whole(x) for x in operands],
            out_specs=[whole(x) for x in outs],
            out_shape=outs,
            scratch_shapes=[pltpu.VMEM((users, rank), F32) for _ in range(scratch)],
            compiler_params=pltpu.CompilerParams(vmem_limit_bytes=40 * 1024 * 1024),
            cost_estimate=pl.CostEstimate(
                flops=2 * 3 * users * weeks * items * 256,
                bytes_accessed=4 * users * weeks * items,
                transcendentals=0,
            ),
        )(counts, *operands)

    def gather(x):
        return lax.all_gather(x, AXES)

    packed = shape((users // 2, 2 * rank))
    packed_sums = shape((users // 2 + 8, 2 * rank))
    weights = [shape((4 * rank, items), BF16), shape((items, 2 * rank), BF16)]

    arrived, factors, dens = [], [], []
    model_w = phi_w = None
    for chunk in range(CHUNKS):
        kernel = functools.partial(first_kernel, chunk, n_item, n_week, chunk == 0)
        if chunk == 0:
            out, model_w, phi_w = run(
                kernel, chunk, (factor_t, week_factor, item_t), [packed_sums] + weights, 2
            )
        else:
            (out,) = run(kernel, chunk, (factor_t, week_factor, model_w, phi_w), [packed_sums], 2)
        arrived.append(gather(out))
    for chunk in range(CHUNKS):
        kernel = functools.partial(second_kernel, chunk)
        out, factor, den = run(
            kernel, chunk, (factor_t, arrived[chunk], week_factor, model_w, phi_w),
            [packed, shape((users, rank)), shape((8, rank))], 1,
        )
        factors.append(factor)
        dens.append(den)
        arrived[chunk] = gather(out)
    for chunk in range(CHUNKS):
        out, factors[chunk] = run(
            third_kernel, chunk,
            (factors[chunk], arrived[chunk], dens[chunk], week_factor, model_w, phi_w),
            [packed, shape((users, rank))], 1,
        )
        arrived[chunk] = gather(out)
    final = pl.pallas_call(last_kernel, out_shape=shape((rank, all_users)))(
        *[x for group in zip(factors, arrived, dens) for x in group]
    )
    return final.T


def solution(mesh):
    sizes = dict(zip(mesh.axis_names, mesh.devices.shape))
    placed = (P(None, "week", "item"), P(), P("item", None), P("week", None))
    run = functools.partial(per_device, sizes["item"], sizes["week"])
    return jax.shard_map(run, mesh=mesh, in_specs=placed, out_specs=P(), check_vma=False)
```

time: 779 us -> 588 us (0.75); the launches traced: 767 us -> 588 us
  matrix products: 489 us -> 0 us
  blocking collectives: 145 us -> 430 us
  Pallas kernels: 0 us -> 155 us
  local copies, waits for them, and re-layouts: 81.4 us -> 3.17 us
  other arithmetic: 50.7 us -> 0 us
    dot_general x6 -> x0, matrix products: 489 us -> none  [the longest x3 342 us: per_device(): model = jnp.dot(factor, khatri_rao.T, precision=lax.Precision.HIGHEST)]
    all_gather x0 -> x6, blocking collectives: none -> 430 us  [gather(): return lax.all_gather(x, AXES)]
    pallas_call x0 -> x7, Pallas kernels: none -> 155 us  [the longest x6 153 us: run(): pl.pallas_call(kernel, grid=(steps,), in_specs=[pl.BlockSpec((BLOCK_USERS...]
    psum x5 -> x0, blocking collectives: 145 us -> none  [the longest x3 118 us: combine(): return lax.psum(partials, ('item', 'week'))]
    convert_element_type x1 -> x0, local copies, waits for them, and re-layouts: 70.4 us -> none  [per_device(): ratio = flat_counts.astype(jnp.float32) / model]
    convert_element_type x1 -> x0, other arithmetic: 43.4 us -> none  [per_device(): ratio = flat_counts.astype(jnp.float32) / model]
    mul x1 -> x0, local copies, waits for them, and re-layouts: 11 us -> none  [per_device(): week_factor[:, None, :] * item_factor[None, :, :]]
where the time goes in v1:
time: 588 us
  blocking collectives  430 us (73%)
  Pallas kernels  155 us (26%)
    all_gather x6, blocking collectives, gather(): return lax.all_gather(x, AXES)  430 us
    pallas_call x6, Pallas kernels, run(): pl.pallas_call(kernel, grid=(steps,), in_specs=[pl.BlockSpec((BLOCK_USERS...  153 us

profile of v1, /device:TPU:0, one launch (start us, length us, event | category | flops | bytes accessed | tf_op | source)
XLA Modules:
  0.0 587.9 jit_solution(16994972279037745675)
XLA Ops:
  0.0 0.0 copy-start
  0.0 0.8 copy-done
  0.8 0.0 copy-start.1
  0.8 0.8 copy-done.1
  1.5 0.0 copy-start.2
  1.5 1.0 copy-done.2
  2.6 25.7 %shard_map.46 = (f32[40,128]{1,0:T(8,128)S(1)}, bf16[256,2048]{1,0:T(8,128)(2,1)S(1)}, bf16[2048,128]{1,0:T(8,128)(2,1)S(1)}) custom-call(s32[128,64,2048]{2,1,0:T(8,128)} %counts.7, f32[64,128]{1,0:T(8,128)S(1)} %bitcast.13, f32[64,64]{1,0:T(8,128)S(1)} %copy-done, f32[64,2048]{1,0:T(8,128)S(1)} %bitcast.17), custom_call_target="tpu_custom_call" | custom-call | flops 12884901888 | bytes 33554432 | tf_op jit(solution)/shard_map/pallas_call | solution.py:160
  28.3 25.6 %shard_map.49 = f32[40,128]{1,0:T(8,128)S(1)} custom-call(s32[128,64,2048]{2,1,0:T(8,128)} %counts.7, f32[64,128]{1,0:T(8,128)S(1)} %bitcast.14, f32[64,64]{1,0:T(8,128)S(1)} %copy-done, bf16[256,2048]{1,0:T(8,128)(2,1)S(1)} %get-tuple-element.19.model_w.refs_3_, bf16[2048,128]{1,0:T(8,128)(2,1)S(1)} %get-tuple-element.20.phi_w.refs_4_), custom_call_target="tpu_custom_call" | custom-call | flops 12884901888 | bytes 33554432 | tf_op jit(solution)/shard_map/pallas_call | solution.py:160
  53.9 75.2 %all-gather.3 = f32[1280,128]{1,0:T(8,128)S(1)} all-gather(f32[40,128]{1,0:T(8,128)S(1)} %shard_map.49), channel_id=5, replica_groups=mesh['item'=8,'week'=4] {'item','week'}, dimensions={0}, use_global_device_ids=true | all-gather | bytes 675840 | tf_op jit(solution)/shard_map/all_gather | solution.py:177
  129.0 25.5 %shard_map.50 = (f32[32,128]{1,0:T(8,128)S(1)}, f32[64,64]{1,0:T(8,128)S(1)}, f32[8,64]{1,0:T(8,128)S(1)}) custom-call(s32[128,64,2048]{2,1,0:T(8,128)} %counts.7, f32[64,128]{1,0:T(8,128)S(1)} %bitcast.15, f32[32,40,128]{2,1,0:T(8,128)S(1)} %bitcast.9, f32[64,64]{1,0:T(8,128)S(1)} %copy-done, bf16[256,2048]{1,0:T(8,128)(2,1)S(1)} %get-tuple-element.19.model_w.refs_3_, ...), custom_call_target="tpu_custom_call" | custom-call | flops 12884901888 | bytes 33554432 | tf_op jit(solution)/shard_map/pallas_call | solution.py:160
  154.5 0.0 copy-start.5
  154.5 67.8 %all-gather.4 = f32[1024,128]{1,0:T(8,128)S(1)} all-gather(f32[32,128]{1,0:T(8,128)S(1)} %get-tuple-element.27), channel_id=6, replica_groups=mesh['item'=8,'week'=4] {'item','week'}, dimensions={0}, use_global_device_ids=true | all-gather | bytes 540672 | tf_op jit(solution)/shard_map/all_gather | solution.py:177
  222.3 25.4 %shard_map.51 = (f32[32,128]{1,0:T(8,128)S(1)}, f32[64,64]{1,0:T(8,128)S(1)}) custom-call(s32[128,64,2048]{2,1,0:T(8,128)} %counts.7, f32[64,64]{1,0:T(8,128)S(1)} %get-tuple-element.26.factor, f32[32,32,128]{2,1,0:T(8,128)S(1)} %bitcast.12, f32[8,64]{1,0:T(8,128)S(1)} %get-tuple-element.28.den.refs_5_, f32[64,64]{1,0:T(8,128)S(1)} %copy-done, ...), custom_call_target="tpu_custom_call" | custom-call | flops 12884901888 | bytes 33554432 | tf_op jit(solution)/shard_map/pallas_call | solution.py:160
  247.7 0.0 copy-start.3
  247.7 74.3 %all-gather.5 = f32[1024,128]{1,0:T(8,128)} all-gather(f32[32,128]{1,0:T(8,128)S(1)} %get-tuple-element.30), channel_id=7, replica_groups=mesh['item'=8,'week'=4] {'item','week'}, dimensions={0}, use_global_device_ids=true | all-gather | bytes 540672 | tf_op jit(solution)/shard_map/all_gather | solution.py:177
  322.0 69.7 %all-gather = f32[1280,128]{1,0:T(8,128)S(1)} all-gather(f32[40,128]{1,0:T(8,128)S(1)} %get-tuple-element.18), channel_id=2, replica_groups=mesh['item'=8,'week'=4] {'item','week'}, dimensions={0}, use_global_device_ids=true | all-gather | bytes 675840 | tf_op jit(solution)/shard_map/all_gather | solution.py:177
  391.7 25.4 %shard_map.47 = (f32[32,128]{1,0:T(8,128)S(1)}, f32[64,64]{1,0:T(8,128)S(1)}, f32[8,64]{1,0:T(8,128)S(1)}) custom-call(s32[128,64,2048]{2,1,0:T(8,128)} %counts.7, f32[64,128]{1,0:T(8,128)S(1)} %bitcast.16, f32[32,40,128]{2,1,0:T(8,128)S(1)} %bitcast.10, f32[64,64]{1,0:T(8,128)S(1)} %copy-done, bf16[256,2048]{1,0:T(8,128)(2,1)S(1)} %get-tuple-element.19.model_w.refs_3_, ...), custom_call_target="tpu_custom_call" | custom-call | flops 12884901888 | bytes 33554432 | tf_op jit(solution)/shard_map/pallas_call | solution.py:160
  417.2 0.0 copy-done.5
  417.2 0.0 copy-start.6
  417.2 0.0 copy-done.3
  417.2 69.4 %all-gather.1 = f32[1024,128]{1,0:T(8,128)S(1)} all-gather(f32[32,128]{1,0:T(8,128)S(1)} %get-tuple-element.22), channel_id=3, replica_groups=mesh['item'=8,'week'=4] {'item','week'}, dimensions={0}, use_global_device_ids=true | all-gather | bytes 540672 | tf_op jit(solution)/shard_map/all_gather | solution.py:177
  486.6 25.4 %shard_map.48 = (f32[32,128]{1,0:T(8,128)S(1)}, f32[64,64]{1,0:T(8,128)S(1)}) custom-call(s32[128,64,2048]{2,1,0:T(8,128)} %counts.7, f32[64,64]{1,0:T(8,128)S(1)} %get-tuple-element.21.factor, f32[32,32,128]{2,1,0:T(8,128)S(1)} %bitcast.11, f32[8,64]{1,0:T(8,128)S(1)} %get-tuple-element.23.den.refs_2_, f32[64,64]{1,0:T(8,128)S(1)} %copy-done, ...), custom_call_target="tpu_custom_call" | custom-call | flops 12884901888 | bytes 33554432 | tf_op jit(solution)/shard_map/pallas_call | solution.py:160
  512.0 0.0 copy-start.4
  512.0 0.6 copy-done.4
  512.6 73.3 %all-gather.2 = f32[1024,128]{1,0:T(8,128)} all-gather(f32[32,128]{1,0:T(8,128)S(1)} %get-tuple-element.25), channel_id=4, replica_groups=mesh['item'=8,'week'=4] {'item','week'}, dimensions={0}, use_global_device_ids=true | all-gather | bytes 540672 | tf_op jit(solution)/shard_map/all_gather | solution.py:177
  585.9 0.0 copy-done.6
  585.9 2.0 shard_map.52
Async XLA Ops:
  0.0 0.8 copy-start
  0.8 0.8 copy-start.1
  1.5 1.0 copy-start.2
  154.5 262.7 %copy-start.5 = (f32[8,64]{1,0:T(8,128)}, f32[8,64]{1,0:T(8,128)S(1)}, u32[]{:S(2)}) copy-start(f32[8,64]{1,0:T(8,128)S(1)} %get-tuple-element.28.den.refs_5_) | copy-start | bytes 6148
  247.7 169.5 %copy-start.3 = (f32[64,64]{1,0:T(8,128)}, f32[64,64]{1,0:T(8,128)S(1)}, u32[]{:S(2)}) copy-start(f32[64,64]{1,0:T(8,128)S(1)} %get-tuple-element.29.refs_3_) | copy-start | bytes 49156
  417.2 168.7 %copy-start.6 = (f32[8,64]{1,0:T(8,128)}, f32[8,64]{1,0:T(8,128)S(1)}, u32[]{:S(2)}) copy-start(f32[8,64]{1,0:T(8,128)S(1)} %get-tuple-element.23.den.refs_2_) | copy-start | bytes 6148
  512.0 0.6 copy-start.4

commit v2 on v0

v2 whole, which is shorter than its diff:
```python
import functools

import jax
import jax.numpy as jnp
from jax import lax
from jax.experimental import pallas as pl
from jax.experimental.pallas import tpu as pltpu
from jax.sharding import PartitionSpec as P

ITERS = 3
TILE_USERS = 8
SLOTS = 4
COLUMNS = 256
MOST = 7.0
ROUNDING = 2.8e-6
ALLOWED = 6.4e-9
F32, BF16 = jnp.float32, jnp.bfloat16


def split(x):
    high = x.astype(BF16)
    low = (x - high.astype(F32)).astype(BF16)
    return high, low


def sum_over(x, axes):
    for axis, size in axes:
        if size & (size - 1):
            x = lax.psum(x, axis)
            continue
        bit = 1
        while bit < size:
            x = x + lax.ppermute(x, axis, [(i, i ^ bit) for i in range(size)])
            bit *= 2
    return x


def spread(index, multiplier):
    return jnp.exp2(((index * multiplier) & 65535).astype(F32) * (1.0 / 65536.0))


def pack(x):
    half = x.shape[0] // 2
    return jnp.concatenate([x[:half], x[half:]], axis=1)


def unpack(x):
    rank = x.shape[1] // 2
    return jnp.concatenate([x[:, :rank], x[:, rank:]], axis=0)


def column_sums(item_t, week, n_item, n_week):
    rank, items = item_t.shape
    both = lax.dot_general(
        jnp.ones((8, items), BF16), jnp.concatenate(split(item_t), axis=0),
        (((1,), (1,)), ((), ())), preferred_element_type=F32,
    )
    sums = (both[:, :rank] + both[:, rank:]) * (1.0 / n_week)
    weeks = jnp.broadcast_to(jnp.sum(week, axis=0, keepdims=True), sums.shape) * (1.0 / n_item)
    return jnp.concatenate([sums, weeks], axis=1)


def update(factor, phi, den):
    new = factor * phi / den
    spread_sum = jnp.sum(jnp.sum(new / den, axis=0, keepdims=True), axis=1, keepdims=True)
    square_sum = jnp.sum(jnp.sum(new * new, axis=0, keepdims=True), axis=1, keepdims=True)
    sound = jnp.where((MOST * ROUNDING) * spread_sum <= ALLOWED * square_sum, 1.0, 0.0)
    return new, jnp.broadcast_to(sound, (8, 128))


def sweep_kernel(iteration, exact, axes, names, *refs):
    r = dict(zip(names, refs))
    counts, slots, arrived = r["counts"], r["slots"], r["arrived"]
    users, weeks, items = counts.shape
    rank = r["week"].shape[1]
    rows = TILE_USERS * weeks
    blocks = users // TILE_USERS
    model_w, phi_w, factor_s, week_s = r["model_w"], r["phi_w"], r["factor_s"], r["week_s"]

    def fetch(block, slot):
        at = pl.ds(pl.multiple_of(block * TILE_USERS, TILE_USERS), TILE_USERS)
        return pltpu.make_async_copy(counts.at[at], slots.at[slot], arrived.at[slot])

    for slot in range(min(SLOTS, blocks)):
        fetch(slot, slot).start()

    item_at = lax.broadcasted_iota(jnp.int32, (1, items), 1) + lax.axis_index("item") * items
    week_at = lax.broadcasted_iota(jnp.int32, (weeks, 1), 0) + lax.axis_index("week") * weeks
    item_t = r["item_t"][...] * spread(item_at, 40503)
    week_s[...] = r["week"][...] * spread(week_at, 27146)
    high, low = split(item_t)
    model_w[...] = jnp.concatenate([high, high, low, low], axis=0)
    phi_w[...] = jnp.concatenate([high.astype(F32), low.astype(F32)], axis=0).T.astype(BF16)

    if iteration == 0:
        factor_s[...] = r["factor_t"][...].T
    else:
        summed = r["summed"][...]
        if iteration == 1:
            sums = summed[users // 2:]
            den = sums[:, :rank] * sums[:, rank:]
            r["den_out"][...] = den
            old = r["factor_t"][...].T
        else:
            den = r["den"][...]
            old = r["factor"][...]
        new, sound = update(old, unpack(summed[: users // 2]), den[0:1, :])
        factor_s[...] = new
        r["factor_out"][...] = new
        r["sound_out"][...] = sound if iteration == 1 else sound * r["sound"][...]

    def operand(block):
        at = pl.ds(pl.multiple_of(block * TILE_USERS, TILE_USERS), TILE_USERS)
        scaled = factor_s[at, :][:, None, :] * week_s[...][None, :, :]
        high, low = split(scaled.reshape(rows, rank))
        return jnp.concatenate([high, low, high, low], axis=1)

    def model_of(lhs, start):
        return jnp.dot(lhs, model_w[:, start:start + COLUMNS], preferred_element_type=F32)

    r["lhs_s"][...] = operand(0)
    r["ahead_s"][...] = model_of(r["lhs_s"][...], 0)

    def body(block, carry):
        slot = lax.rem(block, SLOTS)
        fetch(block, slot).wait()
        lhs = r["lhs_s"][...]
        following = operand(jnp.minimum(block + 1, blocks - 1))
        ahead = r["ahead_s"][...]
        total = None
        for start in range(0, items, COLUMNS):
            model = ahead
            if start + COLUMNS < items:
                ahead = model_of(lhs, start + COLUMNS)
            else:
                r["ahead_s"][...] = model_of(following, 0)
                r["lhs_s"][...] = following
            count = slots[slot, :, :, start:start + COLUMNS].reshape(rows, COLUMNS)
            ratio = count.astype(F32) * pltpu.reciprocal(model, approx=True)
            rhs = phi_w[start:start + COLUMNS, :]
            if exact:
                ratio = jnp.concatenate(split(ratio), axis=1)
                rhs = jnp.concatenate([rhs, rhs], axis=0)
            else:
                ratio = ratio.astype(BF16)
            part = jnp.dot(ratio, rhs, preferred_element_type=F32)
            total = part if total is None else total + part
        total = (total[:, :rank] + total[:, rank:]).reshape(TILE_USERS, weeks, rank)
        at = pl.ds(pl.multiple_of(block * TILE_USERS, TILE_USERS), TILE_USERS)
        r["phi_s"][at, :] = jnp.sum(total * week_s[...][None, :, :], axis=1)

        @pl.when(block + SLOTS < blocks)
        def _():
            fetch(block + SLOTS, slot).start()

        return carry

    lax.fori_loop(0, blocks, body, 0)
    r["phi_out"][: users // 2, :] = pack(r["phi_s"][...])
    if iteration == 0:
        n_item, n_week = (dict(axes)[a] for a in ("item", "week"))
        r["phi_out"][users // 2:, :] = column_sums(r["item_t"][...], r["week"][...], n_item, n_week)


def last_kernel(factor, summed, den, sound, out, sound_out):
    new, fine = update(factor[...], unpack(summed[...]), den[0:1, :])
    out[...] = new.T
    sound_out[...] = (fine * sound[...]).astype(jnp.int32)


def updates(exact, axes, counts, user_factor, item_factor, week_factor):
    users, rank = user_factor.shape
    weeks, items = counts.shape[1:]
    rows = TILE_USERS * weeks
    factor_t, item_t = user_factor.T, item_factor.T
    travel = sorted(axes, reverse=True)

    def shape(dims, dtype=F32):
        return jax.ShapeDtypeStruct(dims, dtype)

    scratch = {
        "slots": pltpu.VMEM((SLOTS, TILE_USERS, weeks, items), jnp.int32),
        "arrived": pltpu.SemaphoreType.DMA((SLOTS,)),
        "model_w": pltpu.VMEM((4 * rank, items), BF16),
        "phi_w": pltpu.VMEM((items, 2 * rank), BF16),
        "factor_s": pltpu.VMEM((users, rank), F32),
        "week_s": pltpu.VMEM((weeks, rank), F32),
        "phi_s": pltpu.VMEM((users, rank), F32),
        "lhs_s": pltpu.VMEM((rows, 4 * rank), BF16),
        "ahead_s": pltpu.VMEM((rows, COLUMNS), F32),
    }

    def sweep(iteration, ins, outs):
        ins = {"counts": counts, "week": week_factor, "item_t": item_t, **ins}
        names = list(ins) + list(outs) + list(scratch)
        results = pl.pallas_call(
            functools.partial(sweep_kernel, iteration, exact, axes, names),
            in_specs=[
                pl.BlockSpec(memory_space=pl.ANY if n == "counts" else pltpu.VMEM) for n in ins
            ],
            out_specs=[pl.BlockSpec(memory_space=pltpu.VMEM)] * len(outs),
            out_shape=list(outs.values()),
            scratch_shapes=list(scratch.values()),
            compiler_params=pltpu.CompilerParams(vmem_limit_bytes=48 * 1024 * 1024),
            cost_estimate=pl.CostEstimate(
                flops=2 * (3 if exact else 2) * users * weeks * items * 256,
                bytes_accessed=4 * users * weeks * items,
                transcendentals=0,
            ),
        )(*ins.values())
        return dict(zip(outs, results))

    packed = shape((users // 2, 2 * rank))
    factor_out, sound_out = shape((users, rank)), shape((8, 128))
    got = sweep(0, {"factor_t": factor_t}, {"phi_out": shape((users // 2 + 8, 2 * rank))})
    summed = sum_over(got["phi_out"], travel)
    got = sweep(
        1, {"factor_t": factor_t, "summed": summed},
        {"phi_out": packed, "factor_out": factor_out, "sound_out": sound_out,
         "den_out": shape((8, rank))},
    )
    den = got["den_out"]
    for iteration in range(2, ITERS):
        got = sweep(
            iteration,
            {"factor": got["factor_out"], "summed": sum_over(got["phi_out"], travel),
             "den": den, "sound": got["sound_out"]},
            {"phi_out": packed, "factor_out": factor_out, "sound_out": sound_out},
        )
    out, sound = pl.pallas_call(
        last_kernel, out_shape=[shape((rank, users)), shape((8, 128), jnp.int32)]
    )(got["factor_out"], sum_over(got["phi_out"], travel), den, got["sound_out"])
    return out.T, sound[0, 0]


def per_device(axes, *arrays):
    out, sound = updates(False, axes, *arrays)
    return lax.cond(sound == 1, lambda *_: out, lambda *a: updates(True, axes, *a)[0], *arrays)


def solution(mesh):
    axes = tuple(zip(mesh.axis_names, mesh.devices.shape))
    placed = (P(None, "week", "item"), P(), P("item", None), P("week", None))
    run = functools.partial(per_device, axes)
    return jax.shard_map(run, mesh=mesh, in_specs=placed, out_specs=P(), check_vma=False)
```

time: 779 us -> 139 us (0.18); the launches traced: 767 us -> 139 us
  matrix products: 489 us -> 0 us
  blocking collectives: 145 us -> 0 us
  Pallas kernels: 0 us -> 80 us
  local copies, waits for them, and re-layouts: 81.4 us -> 1.79 us
  other arithmetic: 50.7 us -> 0.69 us
  waiting for transfers between devices: 0 us -> 28.8 us
  starting transfers between devices: 0 us -> 26.3 us
    dot_general x6 -> x0, matrix products: 489 us -> none  [the longest x3 342 us: per_device(): model = jnp.dot(factor, khatri_rao.T, precision=lax.Precision.HIGHEST)]
    psum x5 -> x0, blocking collectives: 145 us -> none  [the longest x3 118 us: combine(): return lax.psum(partials, ('item', 'week'))]
    pallas_call x0 -> x4, Pallas kernels: none -> 80 us  [the longest x3 78.3 us: sweep(): pl.pallas_call(functools.partial(sweep_kernel, iteration, exact, axes, na...]
    convert_element_type x1 -> x0, local copies, waits for them, and re-layouts: 70.4 us -> none  [per_device(): ratio = flat_counts.astype(jnp.float32) / model]
    convert_element_type x1 -> x0, other arithmetic: 43.4 us -> none  [per_device(): ratio = flat_counts.astype(jnp.float32) / model]
    ppermute x0 -> x15, waiting for transfers between devices: none -> 28.8 us  [sum_over(): x = x + lax.ppermute(x, axis, [(i, i ^ bit) for i in range(size)])]
    ppermute x0 -> x15, starting transfers between devices: none -> 26.3 us  [sum_over(): x = x + lax.ppermute(x, axis, [(i, i ^ bit) for i in range(size)])]
    mul x1 -> x0, local copies, waits for them, and re-layouts: 11 us -> none  [per_device(): week_factor[:, None, :] * item_factor[None, :, :]]
  transfers between devices with their start and end apart: 0 -> 15, of which waited for: 0 -> 15; matrix products, arithmetic and copies ran while one was open for 0% -> 0% of each run, Pallas kernels for 0% -> 0%
where the time goes in v2:
time: 139 us
  Pallas kernels  80 us (58%)
  waiting for transfers between devices  28.8 us (21%)
  starting transfers between devices  26.3 us (19%)
  local copies, waits for them, and re-layouts  1.79 us (1%)
    pallas_call x3, Pallas kernels, sweep(): pl.pallas_call(functools.partial(sweep_kernel, iteration, exact, axes, na...  78.3 us
    ppermute x15, waiting for transfers between devices, sum_over(): x = x + lax.ppermute(x, axis, [(i, i ^ bit) for i in range(size)])  28.8 us
    ppermute x15, starting transfers between devices, sum_over(): x = x + lax.ppermute(x, axis, [(i, i ^ bit) for i in range(size)])  26.3 us
  transfers between devices with their start and end apart: 15, of which 15 were waited for; matrix products, arithmetic and copies ran while one was open for 0% of the time, Pallas kernels for 0%

profile of v2, /device:TPU:0, one launch (start us, length us, event | category | flops | bytes accessed | tf_op | source)
XLA Modules:
  0.0 138.5 jit_solution(15934317278584723355)
XLA Ops:
  0.0 26.8 %shard_map.48 = f32[72,128]{1,0:T(8,128)S(1)} custom-call(s32[128,64,2048]{2,1,0:T(8,128)} %refs_0_.5, f32[64,64]{1,0:T(8,128)} %refs_1_.5, f32[64,2048]{1,0:T(8,128)} %bitcast.7, f32[64,128]{1,0:T(8,128)} %bitcast.13), custom_call_target="tpu_custom_call" | custom-call | flops 17179869184 | bytes 67108864 | tf_op jit(solution)/shard_map/pallas_call | solution.py:196
  26.8 3.1 %collective-permute-start.15 = (f32[72,128]{1,0:T(8,128)S(1)}, f32[72,128]{1,0:T(8,128)S(1)}, u32[]{:S(2)}, u32[]{:S(2)}) collective-permute-start(f32[72,128]{1,0:T(8,128)S(1)} %shard_map.48), channel_id=1, source_target_pairs={{0,1},{1,0},{2,3},{3,2},{4,5},{5,4},{6,7},{7,6},{8,9},{9,8},{10,11... | collective-permute-start | bytes 110600 | tf_op jit(solution)/shard_map/ppermute | solution.py:33
  29.9 1.9 %collective-permute-done.15 = f32[72,128]{1,0:T(8,128)S(1)} collective-permute-done((f32[72,128]{1,0:T(8,128)S(1)}, f32[72,128]{1,0:T(8,128)S(1)}, u32[]{:S(2)}, u32[]{:S(2)}) %collective-permute-start.15) | collective-permute-done | bytes 36896 | tf_op jit(solution)/shard_map/ppermute | solution.py:33
  31.8 3.0 %collective-permute-start.16 = (f32[72,128]{1,0:T(8,128)S(1)}, f32[72,128]{1,0:T(8,128)S(1)}, u32[]{:S(2)}, u32[]{:S(2)}) collective-permute-start(f32[72,128]{1,0:T(8,128)S(1)} %add.90), channel_id=1, source_target_pairs={{0,2},{1,3},{2,0},{3,1},{4,6},{5,7},{6,4},{7,5},{8,10},{9,11},{10,... | collective-permute-start | bytes 110600 | tf_op jit(solution)/shard_map/ppermute | solution.py:33
  34.8 1.9 %collective-permute-done.16 = f32[72,128]{1,0:T(8,128)S(1)} collective-permute-done((f32[72,128]{1,0:T(8,128)S(1)}, f32[72,128]{1,0:T(8,128)S(1)}, u32[]{:S(2)}, u32[]{:S(2)}) %collective-permute-start.16) | collective-permute-done | bytes 36896 | tf_op jit(solution)/shard_map/ppermute | solution.py:33
  36.8 1.2 collective-permute-done.17
  38.0 1.8 %collective-permute-start.18 = (f32[72,128]{1,0:T(8,128)S(1)}, f32[72,128]{1,0:T(8,128)S(1)}, u32[]{:S(2)}, u32[]{:S(2)}) collective-permute-start(f32[72,128]{1,0:T(8,128)S(1)} %add.92), channel_id=1, source_target_pairs={{0,8},{4,12},{8,0},{12,4},{16,24},{20,28},{24,16},{28,20},{1,9},{5... | collective-permute-start | bytes 110600 | tf_op jit(solution)/shard_map/ppermute | solution.py:33
  39.8 2.1 %collective-permute-done.18 = f32[72,128]{1,0:T(8,128)S(1)} collective-permute-done((f32[72,128]{1,0:T(8,128)S(1)}, f32[72,128]{1,0:T(8,128)S(1)}, u32[]{:S(2)}, u32[]{:S(2)}) %collective-permute-start.18) | collective-permute-done | bytes 36896 | tf_op jit(solution)/shard_map/ppermute | solution.py:33
  42.0 1.9 %collective-permute-start.19 = (f32[72,128]{1,0:T(8,128)S(1)}, f32[72,128]{1,0:T(8,128)S(1)}, u32[]{:S(2)}, u32[]{:S(2)}) collective-permute-start(f32[72,128]{1,0:T(8,128)S(1)} %add.93), channel_id=1, source_target_pairs={{0,16},{4,20},{8,24},{12,28},{16,0},{20,4},{24,8},{28,12},{1,17},{... | collective-permute-start | bytes 110600 | tf_op jit(solution)/shard_map/ppermute | solution.py:33
  43.8 2.1 %collective-permute-done.19 = f32[72,128]{1,0:T(8,128)S(1)} collective-permute-done((f32[72,128]{1,0:T(8,128)S(1)}, f32[72,128]{1,0:T(8,128)S(1)}, u32[]{:S(2)}, u32[]{:S(2)}) %collective-permute-start.19) | collective-permute-done | bytes 36896 | tf_op jit(solution)/shard_map/ppermute | solution.py:33
  46.0 25.8 %shard_map.49 = (f32[64,128]{1,0:T(8,128)S(1)}, f32[128,64]{1,0:T(8,128)S(1)}, f32[8,128]{1,0:T(8,128)S(1)}, f32[8,64]{1,0:T(8,128)S(1)}) custom-call(s32[128,64,2048]{2,1,0:T(8,128)} %refs_0_.5, f32[64,64]{1,0:T(8,128)S(1)} %copy-done.7, f32[64,2048]{1,0:T(8,128)S(1)} %bitcast.8, f32[64,128]{1,0:T(8,128)S(1)} %bitcast.14, f32[72,128]{1,0:T(8,128)S(1)} %add.94.refs_4_), custom_call_target="tpu_custom_call" | custom-call | flops 17179869184 | bytes 67108864 | tf_op jit(solution)/shard_map/pallas_call | solution.py:196
  71.8 2.0 %collective-permute-start.20 = (f32[64,128]{1,0:T(8,128)S(1)}, f32[64,128]{1,0:T(8,128)S(1)}, u32[]{:S(2)}, u32[]{:S(2)}) collective-permute-start(f32[64,128]{1,0:T(8,128)S(1)} %get-tuple-element.39), channel_id=1, source_target_pairs={{0,1},{1,0},{2,3},{3,2},{4,5},{5,4},{6,7},{7,6},{8,9},{9,8},{10,11... | collective-permute-start | bytes 98312 | tf_op jit(solution)/shard_map/ppermute | solution.py:33
  73.8 2.0 %collective-permute-done.20 = f32[64,128]{1,0:T(8,128)S(1)} collective-permute-done((f32[64,128]{1,0:T(8,128)S(1)}, f32[64,128]{1,0:T(8,128)S(1)}, u32[]{:S(2)}, u32[]{:S(2)}) %collective-permute-start.20) | collective-permute-done | bytes 32800 | tf_op jit(solution)/shard_map/ppermute | solution.py:33
  75.8 3.1 %collective-permute-start.21 = (f32[64,128]{1,0:T(8,128)S(1)}, f32[64,128]{1,0:T(8,128)S(1)}, u32[]{:S(2)}, u32[]{:S(2)}) collective-permute-start(f32[64,128]{1,0:T(8,128)S(1)} %add.95), channel_id=1, source_target_pairs={{0,2},{1,3},{2,0},{3,1},{4,6},{5,7},{6,4},{7,5},{8,10},{9,11},{10,... | collective-permute-start | bytes 98312 | tf_op jit(solution)/shard_map/ppermute | solution.py:33
  78.9 1.9 %collective-permute-done.21 = f32[64,128]{1,0:T(8,128)S(1)} collective-permute-done((f32[64,128]{1,0:T(8,128)S(1)}, f32[64,128]{1,0:T(8,128)S(1)}, u32[]{:S(2)}, u32[]{:S(2)}) %collective-permute-start.21) | collective-permute-done | bytes 32800 | tf_op jit(solution)/shard_map/ppermute | solution.py:33
  80.8 1.2 collective-permute-done.22
  82.0 1.7 %collective-permute-start.23 = (f32[64,128]{1,0:T(8,128)S(1)}, f32[64,128]{1,0:T(8,128)S(1)}, u32[]{:S(2)}, u32[]{:S(2)}) collective-permute-start(f32[64,128]{1,0:T(8,128)S(1)} %add.97), channel_id=1, source_target_pairs={{0,8},{4,12},{8,0},{12,4},{16,24},{20,28},{24,16},{28,20},{1,9},{5... | collective-permute-start | bytes 98312 | tf_op jit(solution)/shard_map/ppermute | solution.py:33
  83.7 2.2 %collective-permute-done.23 = f32[64,128]{1,0:T(8,128)S(1)} collective-permute-done((f32[64,128]{1,0:T(8,128)S(1)}, f32[64,128]{1,0:T(8,128)S(1)}, u32[]{:S(2)}, u32[]{:S(2)}) %collective-permute-start.23) | collective-permute-done | bytes 32800 | tf_op jit(solution)/shard_map/ppermute | solution.py:33
  85.9 1.7 %collective-permute-start.24 = (f32[64,128]{1,0:T(8,128)S(1)}, f32[64,128]{1,0:T(8,128)S(1)}, u32[]{:S(2)}, u32[]{:S(2)}) collective-permute-start(f32[64,128]{1,0:T(8,128)S(1)} %add.98), channel_id=1, source_target_pairs={{0,16},{4,20},{8,24},{12,28},{16,0},{20,4},{24,8},{28,12},{1,17},{... | collective-permute-start | bytes 98312 | tf_op jit(solution)/shard_map/ppermute | solution.py:33
  87.6 2.2 %collective-permute-done.24 = f32[64,128]{1,0:T(8,128)S(1)} collective-permute-done((f32[64,128]{1,0:T(8,128)S(1)}, f32[64,128]{1,0:T(8,128)S(1)}, u32[]{:S(2)}, u32[]{:S(2)}) %collective-permute-start.24) | collective-permute-done | bytes 32800 | tf_op jit(solution)/shard_map/ppermute | solution.py:33
  89.8 25.7 %shard_map.50 = (f32[64,128]{1,0:T(8,128)S(1)}, f32[128,64]{1,0:T(8,128)S(1)}, f32[8,128]{1,0:T(8,128)S(1)}) custom-call(s32[128,64,2048]{2,1,0:T(8,128)} %refs_0_.5, f32[64,64]{1,0:T(8,128)S(1)} %copy-done.7, f32[64,2048]{1,0:T(8,128)S(1)} %bitcast.9, f32[128,64]{1,0:T(8,128)S(1)} %get-tuple-element.38.refs_3_, f32[64,128]{1,0:T(8,128)S(1)} %add.99.refs_4_, ...), custom_call_target="tpu_custom_call" | custom-call | flops 17179869184 | bytes 67108864 | tf_op jit(solution)/shard_map/pallas_call | solution.py:196
  116.1 1.8 %collective-permute-start.25 = (f32[64,128]{1,0:T(8,128)S(1)}, f32[64,128]{1,0:T(8,128)S(1)}, u32[]{:S(2)}, u32[]{:S(2)}) collective-permute-start(f32[64,128]{1,0:T(8,128)S(1)} %get-tuple-element.43), channel_id=1, source_target_pairs={{0,1},{1,0},{2,3},{3,2},{4,5},{5,4},{6,7},{7,6},{8,9},{9,8},{10,11... | collective-permute-start | bytes 98312 | tf_op jit(solution)/shard_map/ppermute | solution.py:33
  117.9 2.1 %collective-permute-done.25 = f32[64,128]{1,0:T(8,128)S(1)} collective-permute-done((f32[64,128]{1,0:T(8,128)S(1)}, f32[64,128]{1,0:T(8,128)S(1)}, u32[]{:S(2)}, u32[]{:S(2)}) %collective-permute-start.25) | collective-permute-done | bytes 32800 | tf_op jit(solution)/shard_map/ppermute | solution.py:33
  120.1 3.1 %collective-permute-start.26 = (f32[64,128]{1,0:T(8,128)S(1)}, f32[64,128]{1,0:T(8,128)S(1)}, u32[]{:S(2)}, u32[]{:S(2)}) collective-permute-start(f32[64,128]{1,0:T(8,128)S(1)} %add.100), channel_id=1, source_target_pairs={{0,2},{1,3},{2,0},{3,1},{4,6},{5,7},{6,4},{7,5},{8,10},{9,11},{10,... | collective-permute-start | bytes 98312 | tf_op jit(solution)/shard_map/ppermute | solution.py:33
  123.2 1.9 %collective-permute-done.26 = f32[64,128]{1,0:T(8,128)S(1)} collective-permute-done((f32[64,128]{1,0:T(8,128)S(1)}, f32[64,128]{1,0:T(8,128)S(1)}, u32[]{:S(2)}, u32[]{:S(2)}) %collective-permute-start.26) | collective-permute-done | bytes 32800 | tf_op jit(solution)/shard_map/ppermute | solution.py:33
  125.1 1.2 collective-permute-done.27
  126.3 1.5 %collective-permute-start.28 = (f32[64,128]{1,0:T(8,128)S(1)}, f32[64,128]{1,0:T(8,128)S(1)}, u32[]{:S(2)}, u32[]{:S(2)}) collective-permute-start(f32[64,128]{1,0:T(8,128)S(1)} %add.102), channel_id=1, source_target_pairs={{0,8},{4,12},{8,0},{12,4},{16,24},{20,28},{24,16},{28,20},{1,9},{5... | collective-permute-start | bytes 98312 | tf_op jit(solution)/shard_map/ppermute | solution.py:33
  127.9 2.4 %collective-permute-done.28 = f32[64,128]{1,0:T(8,128)S(1)} collective-permute-done((f32[64,128]{1,0:T(8,128)S(1)}, f32[64,128]{1,0:T(8,128)S(1)}, u32[]{:S(2)}, u32[]{:S(2)}) %collective-permute-start.28) | collective-permute-done | bytes 32800 | tf_op jit(solution)/shard_map/ppermute | solution.py:33
  130.3 1.6 %collective-permute-start.29 = (f32[64,128]{1,0:T(8,128)S(1)}, f32[64,128]{1,0:T(8,128)S(1)}, u32[]{:S(2)}, u32[]{:S(2)}) collective-permute-start(f32[64,128]{1,0:T(8,128)S(1)} %add.103), channel_id=1, source_target_pairs={{0,16},{4,20},{8,24},{12,28},{16,0},{20,4},{24,8},{28,12},{1,17},{... | collective-permute-start | bytes 98312 | tf_op jit(solution)/shard_map/ppermute | solution.py:33
  131.8 2.4 %collective-permute-done.29 = f32[64,128]{1,0:T(8,128)S(1)} collective-permute-done((f32[64,128]{1,0:T(8,128)S(1)}, f32[64,128]{1,0:T(8,128)S(1)}, u32[]{:S(2)}, u32[]{:S(2)}) %collective-permute-start.29) | collective-permute-done | bytes 32800 | tf_op jit(solution)/shard_map/ppermute | solution.py:33
  134.8 1.7 %shard_map.51 = (f32[64,128]{1,0:T(8,128)}, s32[8,128]{1,0:T(8,128)}) custom-call(f32[128,64]{1,0:T(8,128)} %copy-done, f32[64,128]{1,0:T(8,128)} %add.104.summed, f32[8,64]{1,0:T(8,128)} %copy-done.2, f32[8,128]{1,0:T(8,128)} %copy-done.4), custom_call_target="tpu_custom_call" | custom-call | tf_op jit(solution)/shard_map/pallas_call | solution.py:230
  136.5 1.2 slice.3
  (31 shorter events, 1.5 us)
Async XLA Ops:
  0.0 45.9 %copy-start.7 = (f32[64,64]{1,0:T(8,128)S(1)}, f32[64,64]{1,0:T(8,128)}, u32[]{:S(2)}) copy-start(f32[64,64]{1,0:T(8,128)} %refs_1_.5) | copy-start | bytes 49156
  0.0 45.9 %copy-start.6 = (f32[2048,64]{0,1:T(8,128)S(1)}, f32[2048,64]{0,1:T(8,128)}, u32[]{:S(2)}) copy-start(f32[2048,64]{0,1:T(8,128)} %param.8) | copy-start | bytes 1572868
  0.0 46.0 %copy-start.8 = (f32[128,64]{0,1:T(8,128)S(1)}, f32[128,64]{0,1:T(8,128)}, u32[]{:S(2)}) copy-start(f32[128,64]{0,1:T(8,128)} %param.7) | copy-start | bytes 98308
  26.8 5.0 %collective-permute-start.15 = (f32[72,128]{1,0:T(8,128)S(1)}, f32[72,128]{1,0:T(8,128)S(1)}, u32[]{:S(2)}, u32[]{:S(2)}) collective-permute-start(f32[72,128]{1,0:T(8,128)S(1)} %shard_map.48), channel_id=1, source_target_pairs={{0,1},{1,0},{2,3},{3,2},{4,5},{5,4},{6,7},{7,6},{8,9},{9,8},{10,11... | collective-permute-start | bytes 110600 | tf_op jit(solution)/shard_map/ppermute | solution.py:33
  31.8 5.0 %collective-permute-start.16 = (f32[72,128]{1,0:T(8,128)S(1)}, f32[72,128]{1,0:T(8,128)S(1)}, u32[]{:S(2)}, u32[]{:S(2)}) collective-permute-start(f32[72,128]{1,0:T(8,128)S(1)} %add.90), channel_id=1, source_target_pairs={{0,2},{1,3},{2,0},{3,1},{4,6},{5,7},{6,4},{7,5},{8,10},{9,11},{10,... | collective-permute-start | bytes 110600 | tf_op jit(solution)/shard_map/ppermute | solution.py:33
  36.8 1.2 collective-permute-start.17
  38.0 4.0 %collective-permute-start.18 = (f32[72,128]{1,0:T(8,128)S(1)}, f32[72,128]{1,0:T(8,128)S(1)}, u32[]{:S(2)}, u32[]{:S(2)}) collective-permute-start(f32[72,128]{1,0:T(8,128)S(1)} %add.92), channel_id=1, source_target_pairs={{0,8},{4,12},{8,0},{12,4},{16,24},{20,28},{24,16},{28,20},{1,9},{5... | collective-permute-start | bytes 110600 | tf_op jit(solution)/shard_map/ppermute | solution.py:33
  42.0 4.0 %collective-permute-start.19 = (f32[72,128]{1,0:T(8,128)S(1)}, f32[72,128]{1,0:T(8,128)S(1)}, u32[]{:S(2)}, u32[]{:S(2)}) collective-permute-start(f32[72,128]{1,0:T(8,128)S(1)} %add.93), channel_id=1, source_target_pairs={{0,16},{4,20},{8,24},{12,28},{16,0},{20,4},{24,8},{28,12},{1,17},{... | collective-permute-start | bytes 110600 | tf_op jit(solution)/shard_map/ppermute | solution.py:33
  71.8 63.0 %copy-start.2 = (f32[8,64]{1,0:T(8,128)}, f32[8,64]{1,0:T(8,128)S(1)}, u32[]{:S(2)}) copy-start(f32[8,64]{1,0:T(8,128)S(1)} %get-tuple-element.40.refs_5_.den) | copy-start | bytes 6148
  71.8 4.0 %collective-permute-start.20 = (f32[64,128]{1,0:T(8,128)S(1)}, f32[64,128]{1,0:T(8,128)S(1)}, u32[]{:S(2)}, u32[]{:S(2)}) collective-permute-start(f32[64,128]{1,0:T(8,128)S(1)} %get-tuple-element.39), channel_id=1, source_target_pairs={{0,1},{1,0},{2,3},{3,2},{4,5},{5,4},{6,7},{7,6},{8,9},{9,8},{10,11... | collective-permute-start | bytes 98312 | tf_op jit(solution)/shard_map/ppermute | solution.py:33
  75.8 4.9 %collective-permute-start.21 = (f32[64,128]{1,0:T(8,128)S(1)}, f32[64,128]{1,0:T(8,128)S(1)}, u32[]{:S(2)}, u32[]{:S(2)}) collective-permute-start(f32[64,128]{1,0:T(8,128)S(1)} %add.95), channel_id=1, source_target_pairs={{0,2},{1,3},{2,0},{3,1},{4,6},{5,7},{6,4},{7,5},{8,10},{9,11},{10,... | collective-permute-start | bytes 98312 | tf_op jit(solution)/shard_map/ppermute | solution.py:33
  80.8 1.2 collective-permute-start.22
  82.0 3.9 %collective-permute-start.23 = (f32[64,128]{1,0:T(8,128)S(1)}, f32[64,128]{1,0:T(8,128)S(1)}, u32[]{:S(2)}, u32[]{:S(2)}) collective-permute-start(f32[64,128]{1,0:T(8,128)S(1)} %add.97), channel_id=1, source_target_pairs={{0,8},{4,12},{8,0},{12,4},{16,24},{20,28},{24,16},{28,20},{1,9},{5... | collective-permute-start | bytes 98312 | tf_op jit(solution)/shard_map/ppermute | solution.py:33
  85.9 3.9 %collective-permute-start.24 = (f32[64,128]{1,0:T(8,128)S(1)}, f32[64,128]{1,0:T(8,128)S(1)}, u32[]{:S(2)}, u32[]{:S(2)}) collective-permute-start(f32[64,128]{1,0:T(8,128)S(1)} %add.98), channel_id=1, source_target_pairs={{0,16},{4,20},{8,24},{12,28},{16,0},{20,4},{24,8},{28,12},{1,17},{... | collective-permute-start | bytes 98312 | tf_op jit(solution)/shard_map/ppermute | solution.py:33
  115.5 0.6 copy-start
  116.1 3.9 %copy-start.4 = (f32[8,128]{1,0:T(8,128)}, f32[8,128]{1,0:T(8,128)S(1)}, u32[]{:S(2)}) copy-start(f32[8,128]{1,0:T(8,128)S(1)} %get-tuple-element.44.sound) | copy-start | bytes 12292
  116.1 3.9 %collective-permute-start.25 = (f32[64,128]{1,0:T(8,128)S(1)}, f32[64,128]{1,0:T(8,128)S(1)}, u32[]{:S(2)}, u32[]{:S(2)}) collective-permute-start(f32[64,128]{1,0:T(8,128)S(1)} %get-tuple-element.43), channel_id=1, source_target_pairs={{0,1},{1,0},{2,3},{3,2},{4,5},{5,4},{6,7},{7,6},{8,9},{9,8},{10,11... | collective-permute-start | bytes 98312 | tf_op jit(solution)/shard_map/ppermute | solution.py:33
  120.1 5.0 %collective-permute-start.26 = (f32[64,128]{1,0:T(8,128)S(1)}, f32[64,128]{1,0:T(8,128)S(1)}, u32[]{:S(2)}, u32[]{:S(2)}) collective-permute-start(f32[64,128]{1,0:T(8,128)S(1)} %add.100), channel_id=1, source_target_pairs={{0,2},{1,3},{2,0},{3,1},{4,6},{5,7},{6,4},{7,5},{8,10},{9,11},{10,... | collective-permute-start | bytes 98312 | tf_op jit(solution)/shard_map/ppermute | solution.py:33
  125.1 1.2 collective-permute-start.27
  126.3 3.9 %collective-permute-start.28 = (f32[64,128]{1,0:T(8,128)S(1)}, f32[64,128]{1,0:T(8,128)S(1)}, u32[]{:S(2)}, u32[]{:S(2)}) collective-permute-start(f32[64,128]{1,0:T(8,128)S(1)} %add.102), channel_id=1, source_target_pairs={{0,8},{4,12},{8,0},{12,4},{16,24},{20,28},{24,16},{28,20},{1,9},{5... | collective-permute-start | bytes 98312 | tf_op jit(solution)/shard_map/ppermute | solution.py:33
  130.3 3.9 %collective-permute-start.29 = (f32[64,128]{1,0:T(8,128)S(1)}, f32[64,128]{1,0:T(8,128)S(1)}, u32[]{:S(2)}, u32[]{:S(2)}) collective-permute-start(f32[64,128]{1,0:T(8,128)S(1)} %add.103), channel_id=1, source_target_pairs={{0,16},{4,20},{8,24},{12,28},{16,0},{20,4},{24,8},{28,12},{1,17},{... | collective-permute-start | bytes 98312 | tf_op jit(solution)/shard_map/ppermute | solution.py:33

commit v3 on v2

--- a/solution.py
+++ b/solution.py
@@ -11,6 +11,7 @@
 TILE_USERS = 8
 SLOTS = 4
 COLUMNS = 256
+GROUP = 4
 MOST = 7.0
 ROUNDING = 2.8e-6
 ALLOWED = 6.4e-9
@@ -28,10 +29,17 @@
         if size & (size - 1):
             x = lax.psum(x, axis)
             continue
-        bit = 1
-        while bit < size:
-            x = x + lax.ppermute(x, axis, [(i, i ^ bit) for i in range(size)])
-            bit *= 2
+        left = size
+        while left > 1:
+            width = min(GROUP, left)
+            left //= width
+            parts = [x]
+            for k in range(1, width):
+                partners = [(i, i ^ (k * left)) for i in range(size)]
+                parts.append(lax.ppermute(x, axis, partners))
+            while len(parts) > 1:
+                parts = [p + q for p, q in zip(parts[0::2], parts[1::2])]
+            x = parts[0]
     return x
 
 
@@ -70,19 +78,25 @@
 
 def sweep_kernel(iteration, exact, axes, names, *refs):
     r = dict(zip(names, refs))
-    counts, slots, arrived = r["counts"], r["slots"], r["arrived"]
+    counts = r["counts"]
     users, weeks, items = counts.shape
+    first = iteration == 0
     rank = r["week"].shape[1]
     rows = TILE_USERS * weeks
     blocks = users // TILE_USERS
     model_w, phi_w, factor_s, week_s = r["model_w"], r["phi_w"], r["factor_s"], r["week_s"]
 
+    def users_of(block):
+        return pl.ds(pl.multiple_of(block * TILE_USERS, TILE_USERS), TILE_USERS)
+
     def fetch(block, slot):
-        at = pl.ds(pl.multiple_of(block * TILE_USERS, TILE_USERS), TILE_USERS)
-        return pltpu.make_async_copy(counts.at[at], slots.at[slot], arrived.at[slot])
-
-    for slot in range(min(SLOTS, blocks)):
-        fetch(slot, slot).start()
+        return pltpu.make_async_copy(
+            counts.at[users_of(block)], r["slots"].at[slot], r["arrived"].at[slot]
+        )
+
+    if first:
+        for slot in range(min(SLOTS, blocks)):
+            fetch(slot, slot).start()
 
     item_at = lax.broadcasted_iota(jnp.int32, (1, items), 1) + lax.axis_index("item") * items
     week_at = lax.broadcasted_iota(jnp.int32, (weeks, 1), 0) + lax.axis_index("week") * weeks
@@ -92,7 +106,7 @@
     model_w[...] = jnp.concatenate([high, high, low, low], axis=0)
     phi_w[...] = jnp.concatenate([high.astype(F32), low.astype(F32)], axis=0).T.astype(BF16)
 
-    if iteration == 0:
+    if first:
         factor_s[...] = r["factor_t"][...].T
     else:
         summed = r["summed"][...]
@@ -110,8 +124,7 @@
         r["sound_out"][...] = sound if iteration == 1 else sound * r["sound"][...]
 
     def operand(block):
-        at = pl.ds(pl.multiple_of(block * TILE_USERS, TILE_USERS), TILE_USERS)
-        scaled = factor_s[at, :][:, None, :] * week_s[...][None, :, :]
+        scaled = factor_s[users_of(block), :][:, None, :] * week_s[...][None, :, :]
         high, low = split(scaled.reshape(rows, rank))
         return jnp.concatenate([high, low, high, low], axis=1)
 
@@ -123,7 +136,8 @@
 
     def body(block, carry):
         slot = lax.rem(block, SLOTS)
-        fetch(block, slot).wait()
+        if first:
+            fetch(block, slot).wait()
         lhs = r["lhs_s"][...]
         following = operand(jnp.minimum(block + 1, blocks - 1))
         ahead = r["ahead_s"][...]
@@ -135,9 +149,15 @@
             else:
                 r["ahead_s"][...] = model_of(following, 0)
                 r["lhs_s"][...] = following
-            count = slots[slot, :, :, start:start + COLUMNS].reshape(rows, COLUMNS)
-            ratio = count.astype(F32) * pltpu.reciprocal(model, approx=True)
-            rhs = phi_w[start:start + COLUMNS, :]
+            at = slice(start, start + COLUMNS)
+            if first:
+                count = r["slots"][slot, :, :, at]
+                r["small_out"][users_of(block), :, at] = count.astype(jnp.int8)
+            else:
+                count = counts[users_of(block), :, at].astype(jnp.int32)
+            count = count.astype(F32).reshape(rows, COLUMNS)
+            ratio = count * pltpu.reciprocal(model, approx=True, full_range=False)
+            rhs = phi_w[at, :]
             if exact:
                 ratio = jnp.concatenate(split(ratio), axis=1)
                 rhs = jnp.concatenate([rhs, rhs], axis=0)
@@ -146,18 +166,19 @@
             part = jnp.dot(ratio, rhs, preferred_element_type=F32)
             total = part if total is None else total + part
         total = (total[:, :rank] + total[:, rank:]).reshape(TILE_USERS, weeks, rank)
-        at = pl.ds(pl.multiple_of(block * TILE_USERS, TILE_USERS), TILE_USERS)
-        r["phi_s"][at, :] = jnp.sum(total * week_s[...][None, :, :], axis=1)
-
-        @pl.when(block + SLOTS < blocks)
-        def _():
-            fetch(block + SLOTS, slot).start()
+        r["phi_s"][users_of(block), :] = jnp.sum(total * week_s[...][None, :, :], axis=1)
+
+        if first:
+
+            @pl.when(block + SLOTS < blocks)
+            def _():
+                fetch(block + SLOTS, slot).start()
 
         return carry
 
     lax.fori_loop(0, blocks, body, 0)
     r["phi_out"][: users // 2, :] = pack(r["phi_s"][...])
-    if iteration == 0:
+    if first:
         n_item, n_week = (dict(axes)[a] for a in ("item", "week"))
         r["phi_out"][users // 2:, :] = column_sums(r["item_t"][...], r["week"][...], n_item, n_week)
 
@@ -178,9 +199,11 @@
     def shape(dims, dtype=F32):
         return jax.ShapeDtypeStruct(dims, dtype)
 
-    scratch = {
+    stream = {
         "slots": pltpu.VMEM((SLOTS, TILE_USERS, weeks, items), jnp.int32),
         "arrived": pltpu.SemaphoreType.DMA((SLOTS,)),
+    }
+    scratch = {
         "model_w": pltpu.VMEM((4 * rank, items), BF16),
         "phi_w": pltpu.VMEM((items, 2 * rank), BF16),
         "factor_s": pltpu.VMEM((users, rank), F32),
@@ -190,18 +213,21 @@
         "ahead_s": pltpu.VMEM((rows, COLUMNS), F32),
     }
 
-    def sweep(iteration, ins, outs):
+    def sweep(iteration, counts, ins, outs):
         ins = {"counts": counts, "week": week_factor, "item_t": item_t, **ins}
-        names = list(ins) + list(outs) + list(scratch)
+        first = iteration == 0
+        scratches = {**stream, **scratch} if first else scratch
+        names = list(ins) + list(outs) + list(scratches)
         results = pl.pallas_call(
             functools.partial(sweep_kernel, iteration, exact, axes, names),
             in_specs=[
-                pl.BlockSpec(memory_space=pl.ANY if n == "counts" else pltpu.VMEM) for n in ins
+                pl.BlockSpec(memory_space=pl.ANY if first and n == "counts" else pltpu.VMEM)
+                for n in ins
             ],
             out_specs=[pl.BlockSpec(memory_space=pltpu.VMEM)] * len(outs),
             out_shape=list(outs.values()),
-            scratch_shapes=list(scratch.values()),
-            compiler_params=pltpu.CompilerParams(vmem_limit_bytes=48 * 1024 * 1024),
+            scratch_shapes=list(scratches.values()),
+            compiler_params=pltpu.CompilerParams(vmem_limit_bytes=(30 if first else 16) * 1024 * 1024),
             cost_estimate=pl.CostEstimate(
                 flops=2 * (3 if exact else 2) * users * weeks * items * 256,
                 bytes_accessed=4 * users * weeks * items,
@@ -212,17 +238,21 @@
 
     packed = shape((users // 2, 2 * rank))
     factor_out, sound_out = shape((users, rank)), shape((8, 128))
-    got = sweep(0, {"factor_t": factor_t}, {"phi_out": shape((users // 2 + 8, 2 * rank))})
+    got = sweep(
+        0, counts, {"factor_t": factor_t},
+        {"phi_out": shape((users // 2 + 8, 2 * rank)), "small_out": shape(counts.shape, jnp.int8)},
+    )
+    small = got["small_out"]
     summed = sum_over(got["phi_out"], travel)
     got = sweep(
-        1, {"factor_t": factor_t, "summed": summed},
+        1, small, {"factor_t": factor_t, "summed": summed},
         {"phi_out": packed, "factor_out": factor_out, "sound_out": sound_out,
          "den_out": shape((8, rank))},
     )
     den = got["den_out"]
     for iteration in range(2, ITERS):
         got = sweep(
-            iteration,
+            iteration, small,
             {"factor": got["factor_out"], "summed": sum_over(got["phi_out"], travel),
              "den": den, "sound": got["sound_out"]},
             {"phi_out": packed, "factor_out": factor_out, "sound_out": sound_out},

time: 139 us -> 128 us (0.921)
  waiting for transfers between devices: 28.8 us -> 22.3 us
  Pallas kernels: 80 us -> 76.6 us
    ppermute x15 -> x21, waiting for transfers between devices: 28.8 us -> 22.3 us  [sum_over(): parts.append(lax.ppermute(x, axis, partners))]
    pallas_call x3, Pallas kernels: 78.3 us -> 75 us  [sweep(): pl.pallas_call(functools.partial(sweep_kernel, iteration, exact, axes, na...]
    ppermute x15 -> x21, starting transfers between devices: 26.3 us -> 25.4 us  [sum_over(): parts.append(lax.ppermute(x, axis, partners))]
  transfers between devices with their start and end apart: 15 -> 21, of which waited for: 15 -> 20; matrix products, arithmetic and copies ran while one was open for 0% -> 0% of each run, Pallas kernels for 0% -> 0%
where the time goes in v3:
time: 128 us
  Pallas kernels  76.6 us (60%)
  starting transfers between devices  25.4 us (20%)
  waiting for transfers between devices  22.3 us (17%)
  local copies, waits for them, and re-layouts  1.81 us (1%)
    pallas_call x3, Pallas kernels, sweep(): pl.pallas_call(functools.partial(sweep_kernel, iteration, exact, axes, na...  75 us
    ppermute x21, starting transfers between devices, sum_over(): parts.append(lax.ppermute(x, axis, partners))  25.4 us
    ppermute x21, waiting for transfers between devices, sum_over(): parts.append(lax.ppermute(x, axis, partners))  22.3 us
  transfers between devices with their start and end apart: 21, of which 20 were waited for; matrix products, arithmetic and copies ran while one was open for 0% of the time, Pallas kernels for 0%

profile of v3, /device:TPU:0, one launch (start us, length us, event | category | flops | bytes accessed | tf_op | source)
XLA Modules:
  0.0 127.9 jit_solution(9011059306105228152)
XLA Ops:
  0.0 26.8 %shard_map.48 = (f32[72,128]{1,0:T(8,128)S(1)}, s8[128,64,2048]{2,1,0:T(32,128)(4,1)S(1)}) custom-call(s32[128,64,2048]{2,1,0:T(8,128)} %refs_0_.1, f32[64,64]{1,0:T(8,128)} %refs_1_.5, f32[64,2048]{1,0:T(8,128)} %bitcast.7, f32[64,128]{1,0:T(8,128)} %bitcast.13), custom_call_target="tpu_custom_call" | custom-call | flops 17179869184 | bytes 67108864 | tf_op jit(solution)/shard_map/pallas_call | solution.py:221
  26.8 5.1 %collective-permute-start.23 = (f32[72,128]{1,0:T(8,128)S(1)}, f32[72,128]{1,0:T(8,128)S(1)}, u32[]{:S(2)}, u32[]{:S(2)}) collective-permute-start(f32[72,128]{1,0:T(8,128)S(1)} %get-tuple-element.43), channel_id=1, source_target_pairs={{0,3},{1,2},{2,1},{3,0},{4,7},{5,6},{6,5},{7,4},{8,11},{9,10},{10,... | collective-permute-start | bytes 110600 | tf_op jit(solution)/shard_map/ppermute | solution.py:39
  31.9 0.6 collective-permute-start.21
  32.6 1.3 %collective-permute-done.23 = f32[72,128]{1,0:T(8,128)S(1)} collective-permute-done((f32[72,128]{1,0:T(8,128)S(1)}, f32[72,128]{1,0:T(8,128)S(1)}, u32[]{:S(2)}, u32[]{:S(2)}) %collective-permute-start.23) | collective-permute-done | bytes 36896 | tf_op jit(solution)/shard_map/ppermute | solution.py:39
  33.9 2.9 %collective-permute-done.22 = f32[72,128]{1,0:T(8,128)S(1)} collective-permute-done((f32[72,128]{1,0:T(8,128)S(1)}, f32[72,128]{1,0:T(8,128)S(1)}, u32[]{:S(2)}, u32[]{:S(2)}) %collective-permute-start.22) | collective-permute-done | bytes 36896 | tf_op jit(solution)/shard_map/ppermute | solution.py:39
  36.8 2.5 %collective-permute-start.26 = (f32[72,128]{1,0:T(8,128)S(1)}, f32[72,128]{1,0:T(8,128)S(1)}, u32[]{:S(2)}, u32[]{:S(2)}) collective-permute-start(f32[72,128]{1,0:T(8,128)S(1)} %add_add_fusion.7), channel_id=1, source_target_pairs={{0,24},{4,28},{8,16},{12,20},{16,8},{20,12},{24,0},{28,4},{1,25},{... | collective-permute-start | bytes 110600 | tf_op jit(solution)/shard_map/ppermute | solution.py:39
  40.4 1.6 %collective-permute-done.26 = f32[72,128]{1,0:T(8,128)S(1)} collective-permute-done((f32[72,128]{1,0:T(8,128)S(1)}, f32[72,128]{1,0:T(8,128)S(1)}, u32[]{:S(2)}, u32[]{:S(2)}) %collective-permute-start.26) | collective-permute-done | bytes 36896 | tf_op jit(solution)/shard_map/ppermute | solution.py:39
  42.0 1.3 collective-permute-done.25
  43.9 1.2 collective-permute-done.27
  45.1 24.1 %shard_map.49 = (f32[64,128]{1,0:T(8,128)S(1)}, f32[128,64]{1,0:T(8,128)S(1)}, f32[8,128]{1,0:T(8,128)S(1)}, f32[8,64]{1,0:T(8,128)S(1)}) custom-call(s8[128,64,2048]{2,1,0:T(32,128)(4,1)S(1)} %get-tuple-element.42.refs_0_, f32[64,64]{1,0:T(8,128)S(1)} %copy-done.7, f32[64,2048]{1,0:T(8,128)S(1)} %bitcast.8, f32[64,128]{1,0:T(8,128)S(1)} %bitcast.14, ...), custom_call_target="tpu_custom_call" | custom-call | flops 17179869184 | bytes 67108864 | tf_op jit(solution)/shard_map/pallas_call | solution.py:221
  69.3 1.5 %collective-permute-start.30 = (f32[64,128]{1,0:T(8,128)S(1)}, f32[64,128]{1,0:T(8,128)S(1)}, u32[]{:S(2)}, u32[]{:S(2)}) collective-permute-start(f32[64,128]{1,0:T(8,128)S(1)} %get-tuple-element.45), channel_id=1, source_target_pairs={{0,3},{1,2},{2,1},{3,0},{4,7},{5,6},{6,5},{7,4},{8,11},{9,10},{10,... | collective-permute-start | bytes 98312 | tf_op jit(solution)/shard_map/ppermute | solution.py:39
  70.8 0.6 collective-permute-start.29
  71.4 2.3 %collective-permute-start.28 = (f32[64,128]{1,0:T(8,128)S(1)}, f32[64,128]{1,0:T(8,128)S(1)}, u32[]{:S(2)}, u32[]{:S(2)}) collective-permute-start(f32[64,128]{1,0:T(8,128)S(1)} %get-tuple-element.45), channel_id=1, source_target_pairs={{0,1},{1,0},{2,3},{3,2},{4,5},{5,4},{6,7},{7,6},{8,9},{9,8},{10,11... | collective-permute-start | bytes 98312 | tf_op jit(solution)/shard_map/ppermute | solution.py:39
  73.7 1.6 %collective-permute-done.30 = f32[64,128]{1,0:T(8,128)S(1)} collective-permute-done((f32[64,128]{1,0:T(8,128)S(1)}, f32[64,128]{1,0:T(8,128)S(1)}, u32[]{:S(2)}, u32[]{:S(2)}) %collective-permute-start.30) | collective-permute-done | bytes 32800 | tf_op jit(solution)/shard_map/ppermute | solution.py:39
  76.0 1.6 %collective-permute-start.33 = (f32[64,128]{1,0:T(8,128)S(1)}, f32[64,128]{1,0:T(8,128)S(1)}, u32[]{:S(2)}, u32[]{:S(2)}) collective-permute-start(f32[64,128]{1,0:T(8,128)S(1)} %add_add_fusion.11), channel_id=1, source_target_pairs={{0,24},{4,28},{8,16},{12,20},{16,8},{20,12},{24,0},{28,4},{1,25},{... | collective-permute-start | bytes 98312 | tf_op jit(solution)/shard_map/ppermute | solution.py:39
  78.0 1.5 %collective-permute-start.31 = (f32[64,128]{1,0:T(8,128)S(1)}, f32[64,128]{1,0:T(8,128)S(1)}, u32[]{:S(2)}, u32[]{:S(2)}) collective-permute-start(f32[64,128]{1,0:T(8,128)S(1)} %add_add_fusion.11), channel_id=1, source_target_pairs={{0,8},{4,12},{8,0},{12,4},{16,24},{20,28},{24,16},{28,20},{1,9},{5... | collective-permute-start | bytes 98312 | tf_op jit(solution)/shard_map/ppermute | solution.py:39
  79.5 1.5 %collective-permute-done.33 = f32[64,128]{1,0:T(8,128)S(1)} collective-permute-done((f32[64,128]{1,0:T(8,128)S(1)}, f32[64,128]{1,0:T(8,128)S(1)}, u32[]{:S(2)}, u32[]{:S(2)}) %collective-permute-start.33) | collective-permute-done | bytes 32800 | tf_op jit(solution)/shard_map/ppermute | solution.py:39
  82.1 1.2 collective-permute-done.34
  83.3 24.0 %shard_map.50 = (f32[64,128]{1,0:T(8,128)S(1)}, f32[128,64]{1,0:T(8,128)S(1)}, f32[8,128]{1,0:T(8,128)S(1)}) custom-call(s8[128,64,2048]{2,1,0:T(32,128)(4,1)S(1)} %get-tuple-element.42.refs_0_, f32[64,64]{1,0:T(8,128)S(1)} %copy-done.7, f32[64,2048]{1,0:T(8,128)S(1)} %bitcast.9, f32[128,64]{1,0:T(8,128)S(1)} %get-tuple-element.44.refs_3_, ...), custom_call_target="tpu_custom_call" | custom-call | flops 17179869184 | bytes 67108864 | tf_op jit(solution)/shard_map/pallas_call | solution.py:221
  107.3 0.6 copy-done
  107.9 2.3 %collective-permute-start.37 = (f32[64,128]{1,0:T(8,128)S(1)}, f32[64,128]{1,0:T(8,128)S(1)}, u32[]{:S(2)}, u32[]{:S(2)}) collective-permute-start(f32[64,128]{1,0:T(8,128)S(1)} %get-tuple-element.49), channel_id=1, source_target_pairs={{0,3},{1,2},{2,1},{3,0},{4,7},{5,6},{6,5},{7,4},{8,11},{9,10},{10,... | collective-permute-start | bytes 98312 | tf_op jit(solution)/shard_map/ppermute | solution.py:39
  110.2 0.8 collective-permute-start.36
  111.0 1.3 %collective-permute-start.35 = (f32[64,128]{1,0:T(8,128)S(1)}, f32[64,128]{1,0:T(8,128)S(1)}, u32[]{:S(2)}, u32[]{:S(2)}) collective-permute-start(f32[64,128]{1,0:T(8,128)S(1)} %get-tuple-element.49), channel_id=1, source_target_pairs={{0,1},{1,0},{2,3},{3,2},{4,5},{5,4},{6,7},{7,6},{8,9},{9,8},{10,11... | collective-permute-start | bytes 98312 | tf_op jit(solution)/shard_map/ppermute | solution.py:39
  112.3 1.5 %collective-permute-done.37 = f32[64,128]{1,0:T(8,128)S(1)} collective-permute-done((f32[64,128]{1,0:T(8,128)S(1)}, f32[64,128]{1,0:T(8,128)S(1)}, u32[]{:S(2)}, u32[]{:S(2)}) %collective-permute-start.37) | collective-permute-done | bytes 32800 | tf_op jit(solution)/shard_map/ppermute | solution.py:39
  113.8 1.3 %collective-permute-done.36 = f32[64,128]{1,0:T(8,128)S(1)} collective-permute-done((f32[64,128]{1,0:T(8,128)S(1)}, f32[64,128]{1,0:T(8,128)S(1)}, u32[]{:S(2)}, u32[]{:S(2)}) %collective-permute-start.36) | collective-permute-done | bytes 32800 | tf_op jit(solution)/shard_map/ppermute | solution.py:39
  115.3 2.5 %collective-permute-start.40 = (f32[64,128]{1,0:T(8,128)S(1)}, f32[64,128]{1,0:T(8,128)S(1)}, u32[]{:S(2)}, u32[]{:S(2)}) collective-permute-start(f32[64,128]{1,0:T(8,128)S(1)} %add_add_fusion.9), channel_id=1, source_target_pairs={{0,24},{4,28},{8,16},{12,20},{16,8},{20,12},{24,0},{28,4},{1,25},{... | collective-permute-start | bytes 98312 | tf_op jit(solution)/shard_map/ppermute | solution.py:39
  118.9 1.3 %collective-permute-done.40 = f32[64,128]{1,0:T(8,128)S(1)} collective-permute-done((f32[64,128]{1,0:T(8,128)S(1)}, f32[64,128]{1,0:T(8,128)S(1)}, u32[]{:S(2)}, u32[]{:S(2)}) %collective-permute-start.40) | collective-permute-done | bytes 32800 | tf_op jit(solution)/shard_map/ppermute | solution.py:39
  120.2 1.5 %collective-permute-done.39 = f32[64,128]{1,0:T(8,128)S(1)} collective-permute-done((f32[64,128]{1,0:T(8,128)S(1)}, f32[64,128]{1,0:T(8,128)S(1)}, u32[]{:S(2)}, u32[]{:S(2)}) %collective-permute-start.39) | collective-permute-done | bytes 32800 | tf_op jit(solution)/shard_map/ppermute | solution.py:39
  122.3 1.2 collective-permute-done.41
  123.5 0.6 add.146.summed
  124.1 1.7 %shard_map.51 = (f32[64,128]{1,0:T(8,128)}, s32[8,128]{1,0:T(8,128)}) custom-call(f32[128,64]{1,0:T(8,128)} %copy-done, f32[64,128]{1,0:T(8,128)} %add.146.summed, f32[8,64]{1,0:T(8,128)} %copy-done.2, f32[8,128]{1,0:T(8,128)} %copy-done.4), custom_call_target="tpu_custom_call" | custom-call | tf_op jit(solution)/shard_map/pallas_call | solution.py:260
  125.8 1.2 slice.3
  (37 shorter events, 5.9 us)
Async XLA Ops:
  0.0 45.1 %copy-start.6 = (f32[2048,64]{0,1:T(8,128)S(1)}, f32[2048,64]{0,1:T(8,128)}, u32[]{:S(2)}) copy-start(f32[2048,64]{0,1:T(8,128)} %param.8) | copy-start | bytes 1572868
  0.0 45.1 %copy-start.7 = (f32[64,64]{1,0:T(8,128)S(1)}, f32[64,64]{1,0:T(8,128)}, u32[]{:S(2)}) copy-start(f32[64,64]{1,0:T(8,128)} %refs_1_.5) | copy-start | bytes 49156
  0.0 45.1 %copy-start.8 = (f32[128,64]{0,1:T(8,128)S(1)}, f32[128,64]{0,1:T(8,128)}, u32[]{:S(2)}) copy-start(f32[128,64]{0,1:T(8,128)} %param.7) | copy-start | bytes 98308
  26.8 7.1 %collective-permute-start.23 = (f32[72,128]{1,0:T(8,128)S(1)}, f32[72,128]{1,0:T(8,128)S(1)}, u32[]{:S(2)}, u32[]{:S(2)}) collective-permute-start(f32[72,128]{1,0:T(8,128)S(1)} %get-tuple-element.43), channel_id=1, source_target_pairs={{0,3},{1,2},{2,1},{3,0},{4,7},{5,6},{6,5},{7,4},{8,11},{9,10},{10,... | collective-permute-start | bytes 110600 | tf_op jit(solution)/shard_map/ppermute | solution.py:39
  31.9 4.9 %collective-permute-start.22 = (f32[72,128]{1,0:T(8,128)S(1)}, f32[72,128]{1,0:T(8,128)S(1)}, u32[]{:S(2)}, u32[]{:S(2)}) collective-permute-start(f32[72,128]{1,0:T(8,128)S(1)} %get-tuple-element.43), channel_id=1, source_target_pairs={{0,2},{1,3},{2,0},{3,1},{4,6},{5,7},{6,4},{7,5},{8,10},{9,11},{10,... | collective-permute-start | bytes 110600 | tf_op jit(solution)/shard_map/ppermute | solution.py:39
  31.9 4.9 %collective-permute-start.21 = (f32[72,128]{1,0:T(8,128)S(1)}, f32[72,128]{1,0:T(8,128)S(1)}, u32[]{:S(2)}, u32[]{:S(2)}) collective-permute-start(f32[72,128]{1,0:T(8,128)S(1)} %get-tuple-element.43), channel_id=1, source_target_pairs={{0,1},{1,0},{2,3},{3,2},{4,5},{5,4},{6,7},{7,6},{8,9},{9,8},{10,11... | collective-permute-start | bytes 110600 | tf_op jit(solution)/shard_map/ppermute | solution.py:39
  36.8 5.2 %collective-permute-start.26 = (f32[72,128]{1,0:T(8,128)S(1)}, f32[72,128]{1,0:T(8,128)S(1)}, u32[]{:S(2)}, u32[]{:S(2)}) collective-permute-start(f32[72,128]{1,0:T(8,128)S(1)} %add_add_fusion.7), channel_id=1, source_target_pairs={{0,24},{4,28},{8,16},{12,20},{16,8},{20,12},{24,0},{28,4},{1,25},{... | collective-permute-start | bytes 110600 | tf_op jit(solution)/shard_map/ppermute | solution.py:39
  39.3 4.0 %collective-permute-start.25 = (f32[72,128]{1,0:T(8,128)S(1)}, f32[72,128]{1,0:T(8,128)S(1)}, u32[]{:S(2)}, u32[]{:S(2)}) collective-permute-start(f32[72,128]{1,0:T(8,128)S(1)} %add_add_fusion.7), channel_id=1, source_target_pairs={{0,16},{4,20},{8,24},{12,28},{16,0},{20,4},{24,8},{28,12},{1,17},{... | collective-permute-start | bytes 110600 | tf_op jit(solution)/shard_map/ppermute | solution.py:39
  39.8 4.0 %collective-permute-start.24 = (f32[72,128]{1,0:T(8,128)S(1)}, f32[72,128]{1,0:T(8,128)S(1)}, u32[]{:S(2)}, u32[]{:S(2)}) collective-permute-start(f32[72,128]{1,0:T(8,128)S(1)} %add_add_fusion.7), channel_id=1, source_target_pairs={{0,8},{4,12},{8,0},{12,4},{16,24},{20,28},{24,16},{28,20},{1,9},{5... | collective-permute-start | bytes 110600 | tf_op jit(solution)/shard_map/ppermute | solution.py:39
  43.8 1.3 %collective-permute-start.27 = (f32[72,128]{1,0:T(8,128)S(1)}, f32[72,128]{1,0:T(8,128)S(1)}, u32[]{:S(2)}, u32[]{:S(2)}) collective-permute-start(f32[72,128]{1,0:T(8,128)S(1)} %add_add_fusion.6), channel_id=1, source_target_pairs={{0,4},{4,0},{8,12},{12,8},{16,20},{20,16},{24,28},{28,24},{1,5},{5... | collective-permute-start | bytes 110600 | tf_op jit(solution)/shard_map/ppermute | solution.py:39
  69.2 38.0 %copy-start.2 = (f32[8,64]{1,0:T(8,128)}, f32[8,64]{1,0:T(8,128)S(1)}, u32[]{:S(2)}) copy-start(f32[8,64]{1,0:T(8,128)S(1)} %get-tuple-element.46.refs_5_.den) | copy-start | bytes 6148
  69.3 6.1 %collective-permute-start.30 = (f32[64,128]{1,0:T(8,128)S(1)}, f32[64,128]{1,0:T(8,128)S(1)}, u32[]{:S(2)}, u32[]{:S(2)}) collective-permute-start(f32[64,128]{1,0:T(8,128)S(1)} %get-tuple-element.45), channel_id=1, source_target_pairs={{0,3},{1,2},{2,1},{3,0},{4,7},{5,6},{6,5},{7,4},{8,11},{9,10},{10,... | collective-permute-start | bytes 98312 | tf_op jit(solution)/shard_map/ppermute | solution.py:39
  70.8 5.0 %collective-permute-start.29 = (f32[64,128]{1,0:T(8,128)S(1)}, f32[64,128]{1,0:T(8,128)S(1)}, u32[]{:S(2)}, u32[]{:S(2)}) collective-permute-start(f32[64,128]{1,0:T(8,128)S(1)} %get-tuple-element.45), channel_id=1, source_target_pairs={{0,2},{1,3},{2,0},{3,1},{4,6},{5,7},{6,4},{7,5},{8,10},{9,11},{10,... | collective-permute-start | bytes 98312 | tf_op jit(solution)/shard_map/ppermute | solution.py:39
  71.4 4.6 %collective-permute-start.28 = (f32[64,128]{1,0:T(8,128)S(1)}, f32[64,128]{1,0:T(8,128)S(1)}, u32[]{:S(2)}, u32[]{:S(2)}) collective-permute-start(f32[64,128]{1,0:T(8,128)S(1)} %get-tuple-element.45), channel_id=1, source_target_pairs={{0,1},{1,0},{2,3},{3,2},{4,5},{5,4},{6,7},{7,6},{8,9},{9,8},{10,11... | collective-permute-start | bytes 98312 | tf_op jit(solution)/shard_map/ppermute | solution.py:39
  76.0 5.1 %collective-permute-start.33 = (f32[64,128]{1,0:T(8,128)S(1)}, f32[64,128]{1,0:T(8,128)S(1)}, u32[]{:S(2)}, u32[]{:S(2)}) collective-permute-start(f32[64,128]{1,0:T(8,128)S(1)} %add_add_fusion.11), channel_id=1, source_target_pairs={{0,24},{4,28},{8,16},{12,20},{16,8},{20,12},{24,0},{28,4},{1,25},{... | collective-permute-start | bytes 98312 | tf_op jit(solution)/shard_map/ppermute | solution.py:39
  77.5 3.9 %collective-permute-start.32 = (f32[64,128]{1,0:T(8,128)S(1)}, f32[64,128]{1,0:T(8,128)S(1)}, u32[]{:S(2)}, u32[]{:S(2)}) collective-permute-start(f32[64,128]{1,0:T(8,128)S(1)} %add_add_fusion.11), channel_id=1, source_target_pairs={{0,16},{4,20},{8,24},{12,28},{16,0},{20,4},{24,8},{28,12},{1,17},{... | collective-permute-start | bytes 98312 | tf_op jit(solution)/shard_map/ppermute | solution.py:39
  78.0 3.9 %collective-permute-start.31 = (f32[64,128]{1,0:T(8,128)S(1)}, f32[64,128]{1,0:T(8,128)S(1)}, u32[]{:S(2)}, u32[]{:S(2)}) collective-permute-start(f32[64,128]{1,0:T(8,128)S(1)} %add_add_fusion.11), channel_id=1, source_target_pairs={{0,8},{4,12},{8,0},{12,4},{16,24},{20,28},{24,16},{28,20},{1,9},{5... | collective-permute-start | bytes 98312 | tf_op jit(solution)/shard_map/ppermute | solution.py:39
  82.0 1.3 collective-permute-start.34
  107.3 0.6 copy-start
  107.9 7.4 %copy-start.4 = (f32[8,128]{1,0:T(8,128)}, f32[8,128]{1,0:T(8,128)S(1)}, u32[]{:S(2)}) copy-start(f32[8,128]{1,0:T(8,128)S(1)} %get-tuple-element.50.sound) | copy-start | bytes 12292
  107.9 5.8 %collective-permute-start.37 = (f32[64,128]{1,0:T(8,128)S(1)}, f32[64,128]{1,0:T(8,128)S(1)}, u32[]{:S(2)}, u32[]{:S(2)}) collective-permute-start(f32[64,128]{1,0:T(8,128)S(1)} %get-tuple-element.49), channel_id=1, source_target_pairs={{0,3},{1,2},{2,1},{3,0},{4,7},{5,6},{6,5},{7,4},{8,11},{9,10},{10,... | collective-permute-start | bytes 98312 | tf_op jit(solution)/shard_map/ppermute | solution.py:39
  110.2 4.9 %collective-permute-start.36 = (f32[64,128]{1,0:T(8,128)S(1)}, f32[64,128]{1,0:T(8,128)S(1)}, u32[]{:S(2)}, u32[]{:S(2)}) collective-permute-start(f32[64,128]{1,0:T(8,128)S(1)} %get-tuple-element.49), channel_id=1, source_target_pairs={{0,2},{1,3},{2,0},{3,1},{4,6},{5,7},{6,4},{7,5},{8,10},{9,11},{10,... | collective-permute-start | bytes 98312 | tf_op jit(solution)/shard_map/ppermute | solution.py:39
  111.0 4.3 %collective-permute-start.35 = (f32[64,128]{1,0:T(8,128)S(1)}, f32[64,128]{1,0:T(8,128)S(1)}, u32[]{:S(2)}, u32[]{:S(2)}) collective-permute-start(f32[64,128]{1,0:T(8,128)S(1)} %get-tuple-element.49), channel_id=1, source_target_pairs={{0,1},{1,0},{2,3},{3,2},{4,5},{5,4},{6,7},{7,6},{8,9},{9,8},{10,11... | collective-permute-start | bytes 98312 | tf_op jit(solution)/shard_map/ppermute | solution.py:39
  115.3 4.9 %collective-permute-start.40 = (f32[64,128]{1,0:T(8,128)S(1)}, f32[64,128]{1,0:T(8,128)S(1)}, u32[]{:S(2)}, u32[]{:S(2)}) collective-permute-start(f32[64,128]{1,0:T(8,128)S(1)} %add_add_fusion.9), channel_id=1, source_target_pairs={{0,24},{4,28},{8,16},{12,20},{16,8},{20,12},{24,0},{28,4},{1,25},{... | collective-permute-start | bytes 98312 | tf_op jit(solution)/shard_map/ppermute | solution.py:39
  117.8 3.9 %collective-permute-start.39 = (f32[64,128]{1,0:T(8,128)S(1)}, f32[64,128]{1,0:T(8,128)S(1)}, u32[]{:S(2)}, u32[]{:S(2)}) collective-permute-start(f32[64,128]{1,0:T(8,128)S(1)} %add_add_fusion.9), channel_id=1, source_target_pairs={{0,16},{4,20},{8,24},{12,28},{16,0},{20,4},{24,8},{28,12},{1,17},{... | collective-permute-start | bytes 98312 | tf_op jit(solution)/shard_map/ppermute | solution.py:39
  118.3 3.9 %collective-permute-start.38 = (f32[64,128]{1,0:T(8,128)S(1)}, f32[64,128]{1,0:T(8,128)S(1)}, u32[]{:S(2)}, u32[]{:S(2)}) collective-permute-start(f32[64,128]{1,0:T(8,128)S(1)} %add_add_fusion.9), channel_id=1, source_target_pairs={{0,8},{4,12},{8,0},{12,4},{16,24},{20,28},{24,16},{28,20},{1,9},{5... | collective-permute-start | bytes 98312 | tf_op jit(solution)/shard_map/ppermute | solution.py:39
  122.2 1.3 collective-permute-start.41

commit v4 on v3

--- a/solution.py
+++ b/solution.py
@@ -11,6 +11,7 @@
 TILE_USERS = 8
 SLOTS = 4
 COLUMNS = 256
+STRIP = 64
 GROUP = 4
 MOST = 7.0
 ROUNDING = 2.8e-6
@@ -58,12 +59,9 @@
 
 
 def column_sums(item_t, week, n_item, n_week):
-    rank, items = item_t.shape
-    both = lax.dot_general(
-        jnp.ones((8, items), BF16), jnp.concatenate(split(item_t), axis=0),
-        (((1,), (1,)), ((), ())), preferred_element_type=F32,
-    )
-    sums = (both[:, :rank] + both[:, rank:]) * (1.0 / n_week)
+    rank = item_t.shape[0]
+    sums = jnp.broadcast_to(jnp.sum(item_t, axis=1, keepdims=True), (rank, 128)).T[:8]
+    sums = sums * (1.0 / n_week)
     weeks = jnp.broadcast_to(jnp.sum(week, axis=0, keepdims=True), sums.shape) * (1.0 / n_item)
     return jnp.concatenate([sums, weeks], axis=1)
 
@@ -76,7 +74,7 @@
     return new, jnp.broadcast_to(sound, (8, 128))
 
 
-def sweep_kernel(iteration, exact, axes, names, *refs):
+def sweep_kernel(iteration, exact, axes, names, units, *refs):
     r = dict(zip(names, refs))
     counts = r["counts"]
     users, weeks, items = counts.shape
@@ -104,7 +102,10 @@
     week_s[...] = r["week"][...] * spread(week_at, 27146)
     high, low = split(item_t)
     model_w[...] = jnp.concatenate([high, high, low, low], axis=0)
-    phi_w[...] = jnp.concatenate([high.astype(F32), low.astype(F32)], axis=0).T.astype(BF16)
+    phi_w[:, : 2 * rank] = jnp.concatenate(
+        [high.astype(F32), low.astype(F32)], axis=0
+    ).T.astype(BF16)
+    phi_w[:, 2 * rank:] = jnp.zeros((items, COLUMNS - 2 * rank), BF16)
 
     if first:
         factor_s[...] = r["factor_t"][...].T
@@ -128,55 +129,80 @@
         high, low = split(scaled.reshape(rows, rank))
         return jnp.concatenate([high, low, high, low], axis=1)
 
-    def model_of(lhs, start):
-        return jnp.dot(lhs, model_w[:, start:start + COLUMNS], preferred_element_type=F32)
-
-    r["lhs_s"][...] = operand(0)
-    r["ahead_s"][...] = model_of(r["lhs_s"][...], 0)
-
-    def body(block, carry):
-        slot = lax.rem(block, SLOTS)
-        if first:
-            fetch(block, slot).wait()
-        lhs = r["lhs_s"][...]
-        following = operand(jnp.minimum(block + 1, blocks - 1))
-        ahead = r["ahead_s"][...]
-        total = None
-        for start in range(0, items, COLUMNS):
-            model = ahead
-            if start + COLUMNS < items:
-                ahead = model_of(lhs, start + COLUMNS)
-            else:
-                r["ahead_s"][...] = model_of(following, 0)
-                r["lhs_s"][...] = following
-            at = slice(start, start + COLUMNS)
+    strips = [slice(at, at + STRIP) for at in range(0, rows, STRIP)]
+    chunks = items // COLUMNS
+    lhs_s = r["lhs_s"]
+
+    def push_model(chunk):
+        at = pl.ds(chunk % chunks * COLUMNS, COLUMNS)
+        pltpu.matmul_push_rhs(model_w[:, at], 0, 0)
+
+    def push_phi(chunk):
+        at = pl.ds(chunk % chunks * COLUMNS, COLUMNS)
+        pltpu.matmul_push_rhs(phi_w[at, :], 0, 1)
+
+    def matmuls(even, odd, total):
+        ahead = (even, odd)
+        lhs_s[0] = operand(0)
+        push_model(0)
+        for n, strip in enumerate(strips):
+            pltpu.matmul_acc_lhs(ahead[0][n], lhs_s[0, strip, :], None if n else 0)
+        push_model(1)
+        push_phi(0)
+
+        def body(block, carry):
+            slot = lax.rem(block, SLOTS)
             if first:
-                count = r["slots"][slot, :, :, at]
-                r["small_out"][users_of(block), :, at] = count.astype(jnp.int8)
-            else:
-                count = counts[users_of(block), :, at].astype(jnp.int32)
-            count = count.astype(F32).reshape(rows, COLUMNS)
-            ratio = count * pltpu.reciprocal(model, approx=True, full_range=False)
-            rhs = phi_w[at, :]
-            if exact:
-                ratio = jnp.concatenate(split(ratio), axis=1)
-                rhs = jnp.concatenate([rhs, rhs], axis=0)
-            else:
-                ratio = ratio.astype(BF16)
-            part = jnp.dot(ratio, rhs, preferred_element_type=F32)
-            total = part if total is None else total + part
-        total = (total[:, :rank] + total[:, rank:]).reshape(TILE_USERS, weeks, rank)
-        r["phi_s"][users_of(block), :] = jnp.sum(total * week_s[...][None, :, :], axis=1)
-
-        if first:
-
-            @pl.when(block + SLOTS < blocks)
-            def _():
-                fetch(block + SLOTS, slot).start()
-
-        return carry
-
-    lax.fori_loop(0, blocks, body, 0)
+                fetch(block, slot).wait()
+            this, other = lax.rem(block, 2), lax.rem(block + 1, 2)
+            lhs_s[other] = operand(jnp.minimum(block + 1, blocks - 1))
+            for chunk in range(chunks):
+                source = this if chunk + 1 < chunks else other
+                at = slice(chunk * COLUMNS, (chunk + 1) * COLUMNS)
+                for n, strip in enumerate(strips):
+                    staged = None if n else 0
+                    pltpu.matmul_acc_lhs(ahead[(chunk + 1) % 2][n], lhs_s[source, strip, :], staged)
+                    model = pltpu.matmul_pop(ahead[chunk % 2][n])
+                    user, week = divmod(strip.start, weeks)
+                    some = slice(user, user + max(1, STRIP // weeks))
+                    part = slice(week, week + min(STRIP, weeks))
+                    if first:
+                        count = r["slots"][slot, some, part, at]
+                        mine = pl.ds(block * TILE_USERS + some.start, some.stop - some.start)
+                        r["small_out"][mine, part, at] = count.astype(jnp.int8)
+                    else:
+                        mine = pl.ds(block * TILE_USERS + some.start, some.stop - some.start)
+                        count = counts[mine, part, at].astype(jnp.int32)
+                    count = count.astype(F32).reshape(STRIP, COLUMNS)
+                    ratio = count * pltpu.reciprocal(model, approx=True, full_range=False)
+                    if exact:
+                        high, low = split(ratio)
+                        pltpu.matmul_acc_lhs(total[n], high, staged)
+                        pltpu.matmul_acc_lhs(total[n], low)
+                    else:
+                        pltpu.matmul_acc_lhs(total[n], ratio.astype(BF16), staged)
+                    if n == len(strips) // 2:
+                        push_model(chunk + 2)
+                        push_phi(chunk + 1)
+            sums = jnp.concatenate([pltpu.matmul_pop(t) for t in total], axis=0)
+            sums = (sums[:, :rank] + sums[:, rank: 2 * rank]).reshape(TILE_USERS, weeks, rank)
+            r["phi_s"][users_of(block), :] = jnp.sum(sums * week_s[...][None, :, :], axis=1)
+            if first:
+
+                @pl.when(block + SLOTS < blocks)
+                def _():
+                    fetch(block + SLOTS, slot).start()
+
+            return carry
+
+        lax.fori_loop(0, blocks, body, 0)
+        nothing = jnp.zeros((STRIP, COLUMNS), BF16)
+        pltpu.matmul_acc_lhs(ahead[1][0], nothing, 0)
+        pltpu.matmul_acc_lhs(total[0], nothing, 0)
+        for ref in ahead[0] + [ahead[1][0], total[0]]:
+            pltpu.matmul_pop(ref)
+
+    pl.run_scoped(matmuls, *[[unit] * len(strips) for unit in units])
     r["phi_out"][: users // 2, :] = pack(r["phi_s"][...])
     if first:
         n_item, n_week = (dict(axes)[a] for a in ("item", "week"))
@@ -189,7 +215,7 @@
     sound_out[...] = (fine * sound[...]).astype(jnp.int32)
 
 
-def updates(exact, axes, counts, user_factor, item_factor, week_factor):
+def updates(exact, mesh, axes, counts, user_factor, item_factor, week_factor):
     users, rank = user_factor.shape
     weeks, items = counts.shape[1:]
     rows = TILE_USERS * weeks
@@ -205,13 +231,14 @@
     }
     scratch = {
         "model_w": pltpu.VMEM((4 * rank, items), BF16),
-        "phi_w": pltpu.VMEM((items, 2 * rank), BF16),
+        "phi_w": pltpu.VMEM((items, COLUMNS), BF16),
         "factor_s": pltpu.VMEM((users, rank), F32),
         "week_s": pltpu.VMEM((weeks, rank), F32),
         "phi_s": pltpu.VMEM((users, rank), F32),
-        "lhs_s": pltpu.VMEM((rows, 4 * rank), BF16),
-        "ahead_s": pltpu.VMEM((rows, COLUMNS), F32),
+        "lhs_s": pltpu.VMEM((2, rows, 4 * rank), BF16),
     }
+    with jax.sharding.use_abstract_mesh(mesh.abstract_mesh):
+        units = [pltpu.ACC(unit)((STRIP, COLUMNS), F32) for unit in (0, 0, 1)]
 
     def sweep(iteration, counts, ins, outs):
         ins = {"counts": counts, "week": week_factor, "item_t": item_t, **ins}
@@ -219,7 +246,7 @@
         scratches = {**stream, **scratch} if first else scratch
         names = list(ins) + list(outs) + list(scratches)
         results = pl.pallas_call(
-            functools.partial(sweep_kernel, iteration, exact, axes, names),
+            functools.partial(sweep_kernel, iteration, exact, axes, names, units),
             in_specs=[
                 pl.BlockSpec(memory_space=pl.ANY if first and n == "counts" else pltpu.VMEM)
                 for n in ins
@@ -263,13 +290,13 @@
     return out.T, sound[0, 0]
 
 
-def per_device(axes, *arrays):
-    out, sound = updates(False, axes, *arrays)
-    return lax.cond(sound == 1, lambda *_: out, lambda *a: updates(True, axes, *a)[0], *arrays)
+def per_device(mesh, axes, *arrays):
+    out, sound = updates(False, mesh, axes, *arrays)
+    return lax.cond(sound == 1, lambda *_: out, lambda *a: updates(True, mesh, axes, *a)[0], *arrays)
 
 
 def solution(mesh):
     axes = tuple(zip(mesh.axis_names, mesh.devices.shape))
     placed = (P(None, "week", "item"), P(), P("item", None), P("week", None))
-    run = functools.partial(per_device, axes)
+    run = functools.partial(per_device, mesh, axes)
     return jax.shard_map(run, mesh=mesh, in_specs=placed, out_specs=P(), check_vma=False)

time: 128 us -> 124 us (0.969)
  Pallas kernels: 76.6 us -> 72.8 us
    pallas_call x3, Pallas kernels: 75 us -> 71.1 us  [sweep(): pl.pallas_call(functools.partial(sweep_kernel, iteration, exact, axes, na...]
where the time goes in v4:
time: 124 us
  Pallas kernels  72.8 us (59%)
  starting transfers between devices  25.5 us (21%)
  waiting for transfers between devices  22.3 us (18%)
  local copies, waits for them, and re-layouts  1.82 us (1%)
    pallas_call x3, Pallas kernels, sweep(): pl.pallas_call(functools.partial(sweep_kernel, iteration, exact, axes, na...  71.1 us
    ppermute x21, starting transfers between devices, sum_over(): parts.append(lax.ppermute(x, axis, partners))  25.5 us
    ppermute x21, waiting for transfers between devices, sum_over(): parts.append(lax.ppermute(x, axis, partners))  22.3 us
  transfers between devices with their start and end apart: 21, of which 20 were waited for; matrix products, arithmetic and copies ran while one was open for 0% of the time, Pallas kernels for 0%

profile of v4, /device:TPU:0, one launch (start us, length us, event | category | flops | bytes accessed | tf_op | source)
XLA Modules:
  0.0 124.1 jit_solution(7890576748795671051)
XLA Ops:
  0.0 25.5 %shard_map.48 = (f32[72,128]{1,0:T(8,128)S(1)}, s8[128,64,2048]{2,1,0:T(32,128)(4,1)S(1)}) custom-call(s32[128,64,2048]{2,1,0:T(8,128)} %refs_0_.1, f32[64,64]{1,0:T(8,128)} %refs_1_.5, f32[64,2048]{1,0:T(8,128)} %bitcast.7, f32[64,128]{1,0:T(8,128)} %bitcast.13), custom_call_target="tpu_custom_call" | custom-call | flops 17179869184 | bytes 67108864 | tf_op jit(solution)/shard_map/pallas_call | solution.py:248
  25.5 5.1 %collective-permute-start.23 = (f32[72,128]{1,0:T(8,128)S(1)}, f32[72,128]{1,0:T(8,128)S(1)}, u32[]{:S(2)}, u32[]{:S(2)}) collective-permute-start(f32[72,128]{1,0:T(8,128)S(1)} %get-tuple-element.43), channel_id=1, source_target_pairs={{0,3},{1,2},{2,1},{3,0},{4,7},{5,6},{6,5},{7,4},{8,11},{9,10},{10,... | collective-permute-start | bytes 110600 | tf_op jit(solution)/shard_map/ppermute | solution.py:40
  30.6 0.6 collective-permute-start.21
  31.3 1.3 %collective-permute-done.23 = f32[72,128]{1,0:T(8,128)S(1)} collective-permute-done((f32[72,128]{1,0:T(8,128)S(1)}, f32[72,128]{1,0:T(8,128)S(1)}, u32[]{:S(2)}, u32[]{:S(2)}) %collective-permute-start.23) | collective-permute-done | bytes 36896 | tf_op jit(solution)/shard_map/ppermute | solution.py:40
  32.6 2.9 %collective-permute-done.22 = f32[72,128]{1,0:T(8,128)S(1)} collective-permute-done((f32[72,128]{1,0:T(8,128)S(1)}, f32[72,128]{1,0:T(8,128)S(1)}, u32[]{:S(2)}, u32[]{:S(2)}) %collective-permute-start.22) | collective-permute-done | bytes 36896 | tf_op jit(solution)/shard_map/ppermute | solution.py:40
  35.5 2.5 %collective-permute-start.26 = (f32[72,128]{1,0:T(8,128)S(1)}, f32[72,128]{1,0:T(8,128)S(1)}, u32[]{:S(2)}, u32[]{:S(2)}) collective-permute-start(f32[72,128]{1,0:T(8,128)S(1)} %add_add_fusion.7), channel_id=1, source_target_pairs={{0,24},{4,28},{8,16},{12,20},{16,8},{20,12},{24,0},{28,4},{1,25},{... | collective-permute-start | bytes 110600 | tf_op jit(solution)/shard_map/ppermute | solution.py:40
  39.1 1.6 %collective-permute-done.26 = f32[72,128]{1,0:T(8,128)S(1)} collective-permute-done((f32[72,128]{1,0:T(8,128)S(1)}, f32[72,128]{1,0:T(8,128)S(1)}, u32[]{:S(2)}, u32[]{:S(2)}) %collective-permute-start.26) | collective-permute-done | bytes 36896 | tf_op jit(solution)/shard_map/ppermute | solution.py:40
  40.7 1.3 %collective-permute-done.25 = f32[72,128]{1,0:T(8,128)S(1)} collective-permute-done((f32[72,128]{1,0:T(8,128)S(1)}, f32[72,128]{1,0:T(8,128)S(1)}, u32[]{:S(2)}, u32[]{:S(2)}) %collective-permute-start.25) | collective-permute-done | bytes 36896 | tf_op jit(solution)/shard_map/ppermute | solution.py:40
  42.6 1.2 collective-permute-done.27
  43.8 22.8 %shard_map.49 = (f32[64,128]{1,0:T(8,128)S(1)}, f32[128,64]{1,0:T(8,128)S(1)}, f32[8,128]{1,0:T(8,128)S(1)}, f32[8,64]{1,0:T(8,128)S(1)}) custom-call(s8[128,64,2048]{2,1,0:T(32,128)(4,1)S(1)} %get-tuple-element.42.refs_0_, f32[64,64]{1,0:T(8,128)S(1)} %copy-done.7, f32[64,2048]{1,0:T(8,128)S(1)} %bitcast.8, f32[64,128]{1,0:T(8,128)S(1)} %bitcast.14, ...), custom_call_target="tpu_custom_call" | custom-call | flops 17179869184 | bytes 67108864 | tf_op jit(solution)/shard_map/pallas_call | solution.py:248
  66.7 1.5 %collective-permute-start.30 = (f32[64,128]{1,0:T(8,128)S(1)}, f32[64,128]{1,0:T(8,128)S(1)}, u32[]{:S(2)}, u32[]{:S(2)}) collective-permute-start(f32[64,128]{1,0:T(8,128)S(1)} %get-tuple-element.45), channel_id=1, source_target_pairs={{0,3},{1,2},{2,1},{3,0},{4,7},{5,6},{6,5},{7,4},{8,11},{9,10},{10,... | collective-permute-start | bytes 98312 | tf_op jit(solution)/shard_map/ppermute | solution.py:40
  68.2 0.6 collective-permute-start.29
  68.8 2.3 %collective-permute-start.28 = (f32[64,128]{1,0:T(8,128)S(1)}, f32[64,128]{1,0:T(8,128)S(1)}, u32[]{:S(2)}, u32[]{:S(2)}) collective-permute-start(f32[64,128]{1,0:T(8,128)S(1)} %get-tuple-element.45), channel_id=1, source_target_pairs={{0,1},{1,0},{2,3},{3,2},{4,5},{5,4},{6,7},{7,6},{8,9},{9,8},{10,11... | collective-permute-start | bytes 98312 | tf_op jit(solution)/shard_map/ppermute | solution.py:40
  71.1 1.6 %collective-permute-done.30 = f32[64,128]{1,0:T(8,128)S(1)} collective-permute-done((f32[64,128]{1,0:T(8,128)S(1)}, f32[64,128]{1,0:T(8,128)S(1)}, u32[]{:S(2)}, u32[]{:S(2)}) %collective-permute-start.30) | collective-permute-done | bytes 32800 | tf_op jit(solution)/shard_map/ppermute | solution.py:40
  73.4 1.6 %collective-permute-start.33 = (f32[64,128]{1,0:T(8,128)S(1)}, f32[64,128]{1,0:T(8,128)S(1)}, u32[]{:S(2)}, u32[]{:S(2)}) collective-permute-start(f32[64,128]{1,0:T(8,128)S(1)} %add_add_fusion.11), channel_id=1, source_target_pairs={{0,24},{4,28},{8,16},{12,20},{16,8},{20,12},{24,0},{28,4},{1,25},{... | collective-permute-start | bytes 98312 | tf_op jit(solution)/shard_map/ppermute | solution.py:40
  75.5 1.5 %collective-permute-start.31 = (f32[64,128]{1,0:T(8,128)S(1)}, f32[64,128]{1,0:T(8,128)S(1)}, u32[]{:S(2)}, u32[]{:S(2)}) collective-permute-start(f32[64,128]{1,0:T(8,128)S(1)} %add_add_fusion.11), channel_id=1, source_target_pairs={{0,8},{4,12},{8,0},{12,4},{16,24},{20,28},{24,16},{28,20},{1,9},{5... | collective-permute-start | bytes 98312 | tf_op jit(solution)/shard_map/ppermute | solution.py:40
  77.0 1.5 %collective-permute-done.33 = f32[64,128]{1,0:T(8,128)S(1)} collective-permute-done((f32[64,128]{1,0:T(8,128)S(1)}, f32[64,128]{1,0:T(8,128)S(1)}, u32[]{:S(2)}, u32[]{:S(2)}) %collective-permute-start.33) | collective-permute-done | bytes 32800 | tf_op jit(solution)/shard_map/ppermute | solution.py:40
  79.5 1.2 collective-permute-done.34
  80.7 22.8 %shard_map.50 = (f32[64,128]{1,0:T(8,128)S(1)}, f32[128,64]{1,0:T(8,128)S(1)}, f32[8,128]{1,0:T(8,128)S(1)}) custom-call(s8[128,64,2048]{2,1,0:T(32,128)(4,1)S(1)} %get-tuple-element.42.refs_0_, f32[64,64]{1,0:T(8,128)S(1)} %copy-done.7, f32[64,2048]{1,0:T(8,128)S(1)} %bitcast.9, f32[128,64]{1,0:T(8,128)S(1)} %get-tuple-element.44.refs_3_, ...), custom_call_target="tpu_custom_call" | custom-call | flops 17179869184 | bytes 67108864 | tf_op jit(solution)/shard_map/pallas_call | solution.py:248
  103.5 0.6 copy-done
  104.2 2.3 %collective-permute-start.37 = (f32[64,128]{1,0:T(8,128)S(1)}, f32[64,128]{1,0:T(8,128)S(1)}, u32[]{:S(2)}, u32[]{:S(2)}) collective-permute-start(f32[64,128]{1,0:T(8,128)S(1)} %get-tuple-element.49), channel_id=1, source_target_pairs={{0,3},{1,2},{2,1},{3,0},{4,7},{5,6},{6,5},{7,4},{8,11},{9,10},{10,... | collective-permute-start | bytes 98312 | tf_op jit(solution)/shard_map/ppermute | solution.py:40
  106.5 0.8 collective-permute-start.36
  107.2 1.3 %collective-permute-start.35 = (f32[64,128]{1,0:T(8,128)S(1)}, f32[64,128]{1,0:T(8,128)S(1)}, u32[]{:S(2)}, u32[]{:S(2)}) collective-permute-start(f32[64,128]{1,0:T(8,128)S(1)} %get-tuple-element.49), channel_id=1, source_target_pairs={{0,1},{1,0},{2,3},{3,2},{4,5},{5,4},{6,7},{7,6},{8,9},{9,8},{10,11... | collective-permute-start | bytes 98312 | tf_op jit(solution)/shard_map/ppermute | solution.py:40
  108.5 1.5 %collective-permute-done.37 = f32[64,128]{1,0:T(8,128)S(1)} collective-permute-done((f32[64,128]{1,0:T(8,128)S(1)}, f32[64,128]{1,0:T(8,128)S(1)}, u32[]{:S(2)}, u32[]{:S(2)}) %collective-permute-start.37) | collective-permute-done | bytes 32800 | tf_op jit(solution)/shard_map/ppermute | solution.py:40
  110.0 1.3 %collective-permute-done.36 = f32[64,128]{1,0:T(8,128)S(1)} collective-permute-done((f32[64,128]{1,0:T(8,128)S(1)}, f32[64,128]{1,0:T(8,128)S(1)}, u32[]{:S(2)}, u32[]{:S(2)}) %collective-permute-start.36) | collective-permute-done | bytes 32800 | tf_op jit(solution)/shard_map/ppermute | solution.py:40
  111.5 2.5 %collective-permute-start.40 = (f32[64,128]{1,0:T(8,128)S(1)}, f32[64,128]{1,0:T(8,128)S(1)}, u32[]{:S(2)}, u32[]{:S(2)}) collective-permute-start(f32[64,128]{1,0:T(8,128)S(1)} %add_add_fusion.9), channel_id=1, source_target_pairs={{0,24},{4,28},{8,16},{12,20},{16,8},{20,12},{24,0},{28,4},{1,25},{... | collective-permute-start | bytes 98312 | tf_op jit(solution)/shard_map/ppermute | solution.py:40
  115.1 1.3 %collective-permute-done.40 = f32[64,128]{1,0:T(8,128)S(1)} collective-permute-done((f32[64,128]{1,0:T(8,128)S(1)}, f32[64,128]{1,0:T(8,128)S(1)}, u32[]{:S(2)}, u32[]{:S(2)}) %collective-permute-start.40) | collective-permute-done | bytes 32800 | tf_op jit(solution)/shard_map/ppermute | solution.py:40
  116.4 1.5 %collective-permute-done.39 = f32[64,128]{1,0:T(8,128)S(1)} collective-permute-done((f32[64,128]{1,0:T(8,128)S(1)}, f32[64,128]{1,0:T(8,128)S(1)}, u32[]{:S(2)}, u32[]{:S(2)}) %collective-permute-start.39) | collective-permute-done | bytes 32800 | tf_op jit(solution)/shard_map/ppermute | solution.py:40
  118.6 1.2 collective-permute-done.41
  119.8 0.6 add.146.summed
  120.4 1.7 %shard_map.51 = (f32[64,128]{1,0:T(8,128)}, s32[8,128]{1,0:T(8,128)}) custom-call(f32[128,64]{1,0:T(8,128)} %copy-done, f32[64,128]{1,0:T(8,128)} %add.146.summed, f32[8,64]{1,0:T(8,128)} %copy-done.2, f32[8,128]{1,0:T(8,128)} %copy-done.4), custom_call_target="tpu_custom_call" | custom-call | tf_op jit(solution)/shard_map/pallas_call | solution.py:287
  122.1 1.2 slice.3
  (37 shorter events, 5.9 us)
Async XLA Ops:
  0.0 43.8 %copy-start.6 = (f32[2048,64]{0,1:T(8,128)S(1)}, f32[2048,64]{0,1:T(8,128)}, u32[]{:S(2)}) copy-start(f32[2048,64]{0,1:T(8,128)} %param.8) | copy-start | bytes 1572868
  0.0 43.8 %copy-start.7 = (f32[64,64]{1,0:T(8,128)S(1)}, f32[64,64]{1,0:T(8,128)}, u32[]{:S(2)}) copy-start(f32[64,64]{1,0:T(8,128)} %refs_1_.5) | copy-start | bytes 49156
  0.0 43.8 %copy-start.8 = (f32[128,64]{0,1:T(8,128)S(1)}, f32[128,64]{0,1:T(8,128)}, u32[]{:S(2)}) copy-start(f32[128,64]{0,1:T(8,128)} %param.7) | copy-start | bytes 98308
  25.5 7.1 %collective-permute-start.23 = (f32[72,128]{1,0:T(8,128)S(1)}, f32[72,128]{1,0:T(8,128)S(1)}, u32[]{:S(2)}, u32[]{:S(2)}) collective-permute-start(f32[72,128]{1,0:T(8,128)S(1)} %get-tuple-element.43), channel_id=1, source_target_pairs={{0,3},{1,2},{2,1},{3,0},{4,7},{5,6},{6,5},{7,4},{8,11},{9,10},{10,... | collective-permute-start | bytes 110600 | tf_op jit(solution)/shard_map/ppermute | solution.py:40
  30.6 4.9 %collective-permute-start.22 = (f32[72,128]{1,0:T(8,128)S(1)}, f32[72,128]{1,0:T(8,128)S(1)}, u32[]{:S(2)}, u32[]{:S(2)}) collective-permute-start(f32[72,128]{1,0:T(8,128)S(1)} %get-tuple-element.43), channel_id=1, source_target_pairs={{0,2},{1,3},{2,0},{3,1},{4,6},{5,7},{6,4},{7,5},{8,10},{9,11},{10,... | collective-permute-start | bytes 110600 | tf_op jit(solution)/shard_map/ppermute | solution.py:40
  30.6 4.9 %collective-permute-start.21 = (f32[72,128]{1,0:T(8,128)S(1)}, f32[72,128]{1,0:T(8,128)S(1)}, u32[]{:S(2)}, u32[]{:S(2)}) collective-permute-start(f32[72,128]{1,0:T(8,128)S(1)} %get-tuple-element.43), channel_id=1, source_target_pairs={{0,1},{1,0},{2,3},{3,2},{4,5},{5,4},{6,7},{7,6},{8,9},{9,8},{10,11... | collective-permute-start | bytes 110600 | tf_op jit(solution)/shard_map/ppermute | solution.py:40
  35.5 5.2 %collective-permute-start.26 = (f32[72,128]{1,0:T(8,128)S(1)}, f32[72,128]{1,0:T(8,128)S(1)}, u32[]{:S(2)}, u32[]{:S(2)}) collective-permute-start(f32[72,128]{1,0:T(8,128)S(1)} %add_add_fusion.7), channel_id=1, source_target_pairs={{0,24},{4,28},{8,16},{12,20},{16,8},{20,12},{24,0},{28,4},{1,25},{... | collective-permute-start | bytes 110600 | tf_op jit(solution)/shard_map/ppermute | solution.py:40
  38.0 4.0 %collective-permute-start.25 = (f32[72,128]{1,0:T(8,128)S(1)}, f32[72,128]{1,0:T(8,128)S(1)}, u32[]{:S(2)}, u32[]{:S(2)}) collective-permute-start(f32[72,128]{1,0:T(8,128)S(1)} %add_add_fusion.7), channel_id=1, source_target_pairs={{0,16},{4,20},{8,24},{12,28},{16,0},{20,4},{24,8},{28,12},{1,17},{... | collective-permute-start | bytes 110600 | tf_op jit(solution)/shard_map/ppermute | solution.py:40
  38.5 4.0 %collective-permute-start.24 = (f32[72,128]{1,0:T(8,128)S(1)}, f32[72,128]{1,0:T(8,128)S(1)}, u32[]{:S(2)}, u32[]{:S(2)}) collective-permute-start(f32[72,128]{1,0:T(8,128)S(1)} %add_add_fusion.7), channel_id=1, source_target_pairs={{0,8},{4,12},{8,0},{12,4},{16,24},{20,28},{24,16},{28,20},{1,9},{5... | collective-permute-start | bytes 110600 | tf_op jit(solution)/shard_map/ppermute | solution.py:40
  42.5 1.3 %collective-permute-start.27 = (f32[72,128]{1,0:T(8,128)S(1)}, f32[72,128]{1,0:T(8,128)S(1)}, u32[]{:S(2)}, u32[]{:S(2)}) collective-permute-start(f32[72,128]{1,0:T(8,128)S(1)} %add_add_fusion.6), channel_id=1, source_target_pairs={{0,4},{4,0},{8,12},{12,8},{16,20},{20,16},{24,28},{28,24},{1,5},{5... | collective-permute-start | bytes 110600 | tf_op jit(solution)/shard_map/ppermute | solution.py:40
  66.7 36.8 %copy-start.2 = (f32[8,64]{1,0:T(8,128)}, f32[8,64]{1,0:T(8,128)S(1)}, u32[]{:S(2)}) copy-start(f32[8,64]{1,0:T(8,128)S(1)} %get-tuple-element.46.refs_5_.den) | copy-start | bytes 6148
  66.7 6.1 %collective-permute-start.30 = (f32[64,128]{1,0:T(8,128)S(1)}, f32[64,128]{1,0:T(8,128)S(1)}, u32[]{:S(2)}, u32[]{:S(2)}) collective-permute-start(f32[64,128]{1,0:T(8,128)S(1)} %get-tuple-element.45), channel_id=1, source_target_pairs={{0,3},{1,2},{2,1},{3,0},{4,7},{5,6},{6,5},{7,4},{8,11},{9,10},{10,... | collective-permute-start | bytes 98312 | tf_op jit(solution)/shard_map/ppermute | solution.py:40
  68.2 5.0 %collective-permute-start.29 = (f32[64,128]{1,0:T(8,128)S(1)}, f32[64,128]{1,0:T(8,128)S(1)}, u32[]{:S(2)}, u32[]{:S(2)}) collective-permute-start(f32[64,128]{1,0:T(8,128)S(1)} %get-tuple-element.45), channel_id=1, source_target_pairs={{0,2},{1,3},{2,0},{3,1},{4,6},{5,7},{6,4},{7,5},{8,10},{9,11},{10,... | collective-permute-start | bytes 98312 | tf_op jit(solution)/shard_map/ppermute | solution.py:40
  68.8 4.6 %collective-permute-start.28 = (f32[64,128]{1,0:T(8,128)S(1)}, f32[64,128]{1,0:T(8,128)S(1)}, u32[]{:S(2)}, u32[]{:S(2)}) collective-permute-start(f32[64,128]{1,0:T(8,128)S(1)} %get-tuple-element.45), channel_id=1, source_target_pairs={{0,1},{1,0},{2,3},{3,2},{4,5},{5,4},{6,7},{7,6},{8,9},{9,8},{10,11... | collective-permute-start | bytes 98312 | tf_op jit(solution)/shard_map/ppermute | solution.py:40
  73.4 5.1 %collective-permute-start.33 = (f32[64,128]{1,0:T(8,128)S(1)}, f32[64,128]{1,0:T(8,128)S(1)}, u32[]{:S(2)}, u32[]{:S(2)}) collective-permute-start(f32[64,128]{1,0:T(8,128)S(1)} %add_add_fusion.11), channel_id=1, source_target_pairs={{0,24},{4,28},{8,16},{12,20},{16,8},{20,12},{24,0},{28,4},{1,25},{... | collective-permute-start | bytes 98312 | tf_op jit(solution)/shard_map/ppermute | solution.py:40
  75.0 3.9 %collective-permute-start.32 = (f32[64,128]{1,0:T(8,128)S(1)}, f32[64,128]{1,0:T(8,128)S(1)}, u32[]{:S(2)}, u32[]{:S(2)}) collective-permute-start(f32[64,128]{1,0:T(8,128)S(1)} %add_add_fusion.11), channel_id=1, source_target_pairs={{0,16},{4,20},{8,24},{12,28},{16,0},{20,4},{24,8},{28,12},{1,17},{... | collective-permute-start | bytes 98312 | tf_op jit(solution)/shard_map/ppermute | solution.py:40
  75.5 3.9 %collective-permute-start.31 = (f32[64,128]{1,0:T(8,128)S(1)}, f32[64,128]{1,0:T(8,128)S(1)}, u32[]{:S(2)}, u32[]{:S(2)}) collective-permute-start(f32[64,128]{1,0:T(8,128)S(1)} %add_add_fusion.11), channel_id=1, source_target_pairs={{0,8},{4,12},{8,0},{12,4},{16,24},{20,28},{24,16},{28,20},{1,9},{5... | collective-permute-start | bytes 98312 | tf_op jit(solution)/shard_map/ppermute | solution.py:40
  79.4 1.3 %collective-permute-start.34 = (f32[64,128]{1,0:T(8,128)S(1)}, f32[64,128]{1,0:T(8,128)S(1)}, u32[]{:S(2)}, u32[]{:S(2)}) collective-permute-start(f32[64,128]{1,0:T(8,128)S(1)} %add_add_fusion.10), channel_id=1, source_target_pairs={{0,4},{4,0},{8,12},{12,8},{16,20},{20,16},{24,28},{28,24},{1,5},{5... | collective-permute-start | bytes 98312 | tf_op jit(solution)/shard_map/ppermute | solution.py:40
  103.5 0.6 copy-start
  104.2 7.4 %copy-start.4 = (f32[8,128]{1,0:T(8,128)}, f32[8,128]{1,0:T(8,128)S(1)}, u32[]{:S(2)}) copy-start(f32[8,128]{1,0:T(8,128)S(1)} %get-tuple-element.50.sound) | copy-start | bytes 12292
  104.2 5.8 %collective-permute-start.37 = (f32[64,128]{1,0:T(8,128)S(1)}, f32[64,128]{1,0:T(8,128)S(1)}, u32[]{:S(2)}, u32[]{:S(2)}) collective-permute-start(f32[64,128]{1,0:T(8,128)S(1)} %get-tuple-element.49), channel_id=1, source_target_pairs={{0,3},{1,2},{2,1},{3,0},{4,7},{5,6},{6,5},{7,4},{8,11},{9,10},{10,... | collective-permute-start | bytes 98312 | tf_op jit(solution)/shard_map/ppermute | solution.py:40
  106.5 4.9 %collective-permute-start.36 = (f32[64,128]{1,0:T(8,128)S(1)}, f32[64,128]{1,0:T(8,128)S(1)}, u32[]{:S(2)}, u32[]{:S(2)}) collective-permute-start(f32[64,128]{1,0:T(8,128)S(1)} %get-tuple-element.49), channel_id=1, source_target_pairs={{0,2},{1,3},{2,0},{3,1},{4,6},{5,7},{6,4},{7,5},{8,10},{9,11},{10,... | collective-permute-start | bytes 98312 | tf_op jit(solution)/shard_map/ppermute | solution.py:40
  107.2 4.3 %collective-permute-start.35 = (f32[64,128]{1,0:T(8,128)S(1)}, f32[64,128]{1,0:T(8,128)S(1)}, u32[]{:S(2)}, u32[]{:S(2)}) collective-permute-start(f32[64,128]{1,0:T(8,128)S(1)} %get-tuple-element.49), channel_id=1, source_target_pairs={{0,1},{1,0},{2,3},{3,2},{4,5},{5,4},{6,7},{7,6},{8,9},{9,8},{10,11... | collective-permute-start | bytes 98312 | tf_op jit(solution)/shard_map/ppermute | solution.py:40
  111.5 4.9 %collective-permute-start.40 = (f32[64,128]{1,0:T(8,128)S(1)}, f32[64,128]{1,0:T(8,128)S(1)}, u32[]{:S(2)}, u32[]{:S(2)}) collective-permute-start(f32[64,128]{1,0:T(8,128)S(1)} %add_add_fusion.9), channel_id=1, source_target_pairs={{0,24},{4,28},{8,16},{12,20},{16,8},{20,12},{24,0},{28,4},{1,25},{... | collective-permute-start | bytes 98312 | tf_op jit(solution)/shard_map/ppermute | solution.py:40
  114.1 3.9 %collective-permute-start.39 = (f32[64,128]{1,0:T(8,128)S(1)}, f32[64,128]{1,0:T(8,128)S(1)}, u32[]{:S(2)}, u32[]{:S(2)}) collective-permute-start(f32[64,128]{1,0:T(8,128)S(1)} %add_add_fusion.9), channel_id=1, source_target_pairs={{0,16},{4,20},{8,24},{12,28},{16,0},{20,4},{24,8},{28,12},{1,17},{... | collective-permute-start | bytes 98312 | tf_op jit(solution)/shard_map/ppermute | solution.py:40
  114.6 3.9 %collective-permute-start.38 = (f32[64,128]{1,0:T(8,128)S(1)}, f32[64,128]{1,0:T(8,128)S(1)}, u32[]{:S(2)}, u32[]{:S(2)}) collective-permute-start(f32[64,128]{1,0:T(8,128)S(1)} %add_add_fusion.9), channel_id=1, source_target_pairs={{0,8},{4,12},{8,0},{12,4},{16,24},{20,28},{24,16},{28,20},{1,9},{5... | collective-permute-start | bytes 98312 | tf_op jit(solution)/shard_map/ppermute | solution.py:40
  118.5 1.3 %collective-permute-start.41 = (f32[64,128]{1,0:T(8,128)S(1)}, f32[64,128]{1,0:T(8,128)S(1)}, u32[]{:S(2)}, u32[]{:S(2)}) collective-permute-start(f32[64,128]{1,0:T(8,128)S(1)} %add_add_fusion.8), channel_id=1, source_target_pairs={{0,4},{4,0},{8,12},{12,8},{16,20},{20,16},{24,28},{28,24},{1,5},{5... | collective-permute-start | bytes 98312 | tf_op jit(solution)/shard_map/ppermute | solution.py:40

commit v5 on v4

v5 whole, which is shorter than its diff:
```python
import functools

import jax
import jax.numpy as jnp
from jax import lax
from jax.experimental import pallas as pl
from jax.experimental.pallas import tpu as pltpu
from jax.sharding import PartitionSpec as P

ITERS = 3
TILE_USERS = 16
FETCH_USERS = 8
SLOTS = 4
COLUMNS = 256
GROUP = 4
MOST = 7.0
ROUNDING = 2.8e-6
ALLOWED = 6.4e-9
F32, BF16 = jnp.float32, jnp.bfloat16


def split(x):
    high = x.astype(BF16)
    low = (x - high.astype(F32)).astype(BF16)
    return high, low


def sum_over(x, axes):
    for axis, size in axes:
        if size & (size - 1):
            x = lax.psum(x, axis)
            continue
        left = size
        while left > 1:
            width = min(GROUP, left)
            left //= width
            parts = [x]
            for k in range(1, width):
                partners = [(i, i ^ (k * left)) for i in range(size)]
                parts.append(lax.ppermute(x, axis, partners))
            while len(parts) > 1:
                parts = [p + q for p, q in zip(parts[0::2], parts[1::2])]
            x = parts[0]
    return x


def spread(index, multiplier):
    return jnp.exp2(((index * multiplier) & 65535).astype(F32) * (1.0 / 65536.0))


def pack(x):
    half = x.shape[0] // 2
    return jnp.concatenate([x[:half], x[half:]], axis=1)


def unpack(x):
    rank = x.shape[1] // 2
    return jnp.concatenate([x[:, :rank], x[:, rank:]], axis=0)


def column_sums(item_t, week, n_item, n_week):
    rank = item_t.shape[0]
    sums = jnp.broadcast_to(jnp.sum(item_t, axis=1, keepdims=True), (rank, 128)).T[:8]
    sums = sums * (1.0 / n_week)
    weeks = jnp.broadcast_to(jnp.sum(week, axis=0, keepdims=True), sums.shape) * (1.0 / n_item)
    return jnp.concatenate([sums, weeks], axis=1)


def update(factor, phi, den):
    new = factor * phi / den
    spread_sum = jnp.sum(jnp.sum(new / den, axis=0, keepdims=True), axis=1, keepdims=True)
    square_sum = jnp.sum(jnp.sum(new * new, axis=0, keepdims=True), axis=1, keepdims=True)
    sound = jnp.where((MOST * ROUNDING) * spread_sum <= ALLOWED * square_sum, 1.0, 0.0)
    return new, jnp.broadcast_to(sound, (8, 128))


def sweep_kernel(iteration, exact, axes, names, units, *refs):
    r = dict(zip(names, refs))
    counts = r["counts"]
    users, weeks, items = counts.shape
    first = iteration == 0
    rank = r["week"].shape[1]
    rows = TILE_USERS * weeks
    blocks = users // TILE_USERS
    halves = TILE_USERS // FETCH_USERS
    model_w, phi_w, factor_s, week_s = r["model_w"], r["phi_w"], r["factor_s"], r["week_s"]

    def fetch(part):
        at = pl.ds(pl.multiple_of(part * FETCH_USERS, FETCH_USERS), FETCH_USERS)
        slot = lax.rem(part, SLOTS)
        return pltpu.make_async_copy(
            counts.at[at], r["slots"].at[slot], r["arrived"].at[slot]
        )

    week_at = lax.broadcasted_iota(jnp.int32, (weeks, 1), 0) + lax.axis_index("week") * weeks
    week_s[...] = r["week"][...] * spread(week_at, 27146)

    if first:
        for part in range(min(SLOTS, users // FETCH_USERS)):
            fetch(jnp.int32(part)).start()
        item_at = lax.broadcasted_iota(jnp.int32, (1, items), 1)
        item_at = item_at + lax.axis_index("item") * items
        high, low = split(r["item_t"][...] * spread(item_at, 40503))
        model_w[...] = jnp.concatenate([high, high, low, low], axis=0)
        phi_w[:, : 2 * rank] = jnp.concatenate(
            [high.astype(F32), low.astype(F32)], axis=0
        ).T.astype(BF16)
        phi_w[:, 2 * rank:] = jnp.zeros((items, COLUMNS - 2 * rank), BF16)
        factor_s[...] = r["factor_t"][...].T
    else:
        summed = r["summed"][...]
        if iteration == 1:
            sums = summed[users // 2:]
            den = sums[:, :rank] * sums[:, rank:]
            r["den_out"][...] = den
            old = r["factor_t"][...].T
        else:
            den = r["den"][...]
            old = r["factor"][...]
        new, sound = update(old, unpack(summed[: users // 2]), den[0:1, :])
        factor_s[...] = new
        r["factor_out"][...] = new
        r["sound_out"][...] = sound if iteration == 1 else sound * r["sound"][...]

    strips = [slice(n * weeks, (n + 1) * weeks) for n in range(TILE_USERS)]
    chunks = items // COLUMNS
    lhs_s, phi_s = r["lhs_s"], r["phi_s"]

    def operand(user):
        high, low = split(factor_s[pl.ds(user, 1), :] * week_s[...])
        return jnp.concatenate([high, low, high, low], axis=1)

    def push_model(chunk):
        at = pl.ds(chunk % chunks * COLUMNS, COLUMNS)
        pltpu.matmul_push_rhs(model_w[:, at], 0, 0)

    def push_phi(chunk):
        at = pl.ds(chunk % chunks * COLUMNS, COLUMNS)
        pltpu.matmul_push_rhs(phi_w[at, :], 0, 1)

    def matmuls(ahead, total):
        def keep(n, user):
            sums = pltpu.matmul_pop(total[n])
            sums = (sums[:, :rank] + sums[:, rank: 2 * rank]) * week_s[...]
            phi_s[pl.ds(user, 1), :] = jnp.sum(sums, axis=0, keepdims=True)

        push_model(0)
        for n, strip in enumerate(strips):
            lhs_s[strip, :] = operand(n)
            pltpu.matmul_acc_lhs(ahead[n], lhs_s[strip, :], None if n else 0)
        push_model(1)
        push_phi(0)

        def body(block, carry):
            start = block * TILE_USERS
            before = lax.rem(start + users - TILE_USERS, users)
            after = jnp.minimum(start + TILE_USERS, users - TILE_USERS)
            for chunk in range(chunks):
                at = slice(chunk * COLUMNS, (chunk + 1) * COLUMNS)
                for n, strip in enumerate(strips):
                    part = block * halves + n // FETCH_USERS
                    if first and chunk == 0 and n % FETCH_USERS == 0:
                        fetch(part).wait()
                    staged = None if n else 0
                    model = pltpu.matmul_pop(ahead[n])
                    if chunk + 1 < chunks:
                        pltpu.matmul_acc_lhs(ahead[n], lhs_s[strip, :], staged)
                    else:
                        following = operand(after + n)
                        lhs_s[strip, :] = following
                        pltpu.matmul_acc_lhs(ahead[n], following, staged)
                    if first:
                        count = r["slots"][lax.rem(part, SLOTS), n % FETCH_USERS, :, at]
                        r["small_out"][start + n, :, at] = count.astype(jnp.int8)
                    else:
                        count = counts[start + n, :, at].astype(jnp.int32)
                    ratio = count.astype(F32) * pltpu.reciprocal(
                        model, approx=True, full_range=False
                    )
                    if chunk == 0:
                        keep(n, before + n)
                    if exact:
                        high, low = split(ratio)
                        pltpu.matmul_acc_lhs(total[n], high, staged)
                        pltpu.matmul_acc_lhs(total[n], low)
                    else:
                        pltpu.matmul_acc_lhs(total[n], ratio.astype(BF16), staged)
                    if n == len(strips) // 2:
                        push_model(chunk + 2)
                        push_phi(chunk + 1)
            if first:

                @pl.when((block + 1) * halves + SLOTS <= users // FETCH_USERS)
                def _():
                    for half in range(halves):
                        fetch(block * halves + SLOTS + half).start()

            return carry

        lax.fori_loop(0, blocks, body, 0)
        for n in range(TILE_USERS):
            keep(n, users - TILE_USERS + n)
        nothing = jnp.zeros((weeks, COLUMNS), BF16)
        for ref in ahead:
            pltpu.matmul_pop(ref)
        for ref in (ahead[0], total[0]):
            pltpu.matmul_acc_lhs(ref, nothing, 0)
            pltpu.matmul_pop(ref)

    pl.run_scoped(matmuls, *[[unit] * TILE_USERS for unit in units])
    r["phi_out"][: users // 2, :] = pack(phi_s[...])
    if first:
        n_item, n_week = (dict(axes)[a] for a in ("item", "week"))
        r["phi_out"][users // 2:, :] = column_sums(r["item_t"][...], r["week"][...], n_item, n_week)


def last_kernel(factor, summed, den, sound, out, sound_out):
    new, fine = update(factor[...], unpack(summed[...]), den[0:1, :])
    out[...] = new.T
    sound_out[0] = jnp.min(fine * sound[...]).astype(jnp.int32)


def updates(exact, mesh, axes, counts, user_factor, item_factor, week_factor):
    users, rank = user_factor.shape
    weeks, items = counts.shape[1:]
    rows = TILE_USERS * weeks
    factor_t, item_t = user_factor.T, item_factor.T
    travel = sorted(axes, reverse=True)

    def shape(dims, dtype=F32):
        return jax.ShapeDtypeStruct(dims, dtype)

    stream = {
        "slots": pltpu.VMEM((SLOTS, FETCH_USERS, weeks, items), jnp.int32),
        "arrived": pltpu.SemaphoreType.DMA((SLOTS,)),
    }
    scratch = {
        "factor_s": pltpu.VMEM((users, rank), F32),
        "week_s": pltpu.VMEM((weeks, rank), F32),
        "phi_s": pltpu.VMEM((users, rank), F32),
        "lhs_s": pltpu.VMEM((rows, 4 * rank), BF16),
    }
    with jax.sharding.use_abstract_mesh(mesh.abstract_mesh):
        units = [pltpu.ACC(unit)((weeks, COLUMNS), F32) for unit in (0, 1)]

    def sweep(iteration, counts, ins, outs):
        ins = {"counts": counts, "week": week_factor, **ins}
        first = iteration == 0
        scratches = {**stream, **scratch} if first else scratch
        names = list(ins) + list(outs) + list(scratches)
        results = pl.pallas_call(
            functools.partial(sweep_kernel, iteration, exact, axes, names, units),
            in_specs=[
                pl.BlockSpec(memory_space=pl.ANY if first and n == "counts" else pltpu.VMEM)
                for n in ins
            ],
            out_specs=[pl.BlockSpec(memory_space=pltpu.VMEM)] * len(outs),
            out_shape=list(outs.values()),
            scratch_shapes=list(scratches.values()),
            compiler_params=pltpu.CompilerParams(vmem_limit_bytes=(22 if first else 8) * 1024 * 1024),
            cost_estimate=pl.CostEstimate(
                flops=2 * (3 if exact else 2) * users * weeks * items * 256,
                bytes_accessed=4 * users * weeks * items,
                transcendentals=0,
            ),
        )(*ins.values())
        return dict(zip(outs, results))

    packed = shape((users // 2, 2 * rank))
    factor_out, sound_out = shape((users, rank)), shape((8, 128))
    got = sweep(
        0, counts, {"factor_t": factor_t, "item_t": item_t},
        {"phi_out": shape((users // 2 + 8, 2 * rank)), "small_out": shape(counts.shape, jnp.int8),
         "model_w": shape((4 * rank, items), BF16), "phi_w": shape((items, COLUMNS), BF16)},
    )
    small, weights = got["small_out"], {n: got[n] for n in ("model_w", "phi_w")}
    summed = sum_over(got["phi_out"], travel)
    got = sweep(
        1, small, {"factor_t": factor_t, "summed": summed, **weights},
        {"phi_out": packed, "factor_out": factor_out, "sound_out": sound_out,
         "den_out": shape((8, rank))},
    )
    den = got["den_out"]
    for iteration in range(2, ITERS):
        got = sweep(
            iteration, small,
            {"factor": got["factor_out"], "summed": sum_over(got["phi_out"], travel),
             "den": den, "sound": got["sound_out"], **weights},
            {"phi_out": packed, "factor_out": factor_out, "sound_out": sound_out},
        )
    out, sound = pl.pallas_call(
        last_kernel,
        in_specs=[pl.BlockSpec(memory_space=pltpu.VMEM)] * 4,
        out_specs=[pl.BlockSpec(memory_space=m) for m in (pltpu.VMEM, pltpu.SMEM)],
        out_shape=[shape((rank, users)), shape((1,), jnp.int32)],
        compiler_params=pltpu.CompilerParams(vmem_limit_bytes=4 * 1024 * 1024),
    )(got["factor_out"], sum_over(got["phi_out"], travel), den, got["sound_out"])
    return out.T, sound.reshape(())


def per_device(mesh, axes, *arrays):
    out, sound = updates(False, mesh, axes, *arrays)
    return lax.cond(sound, lambda *_: out, lambda *a: updates(True, mesh, axes, *a)[0], *arrays)


def solution(mesh):
    axes = tuple(zip(mesh.axis_names, mesh.devices.shape))
    placed = (P(None, "week", "item"), P(), P("item", None), P("week", None))
    run = functools.partial(per_device, mesh, axes)
    return jax.shard_map(run, mesh=mesh, in_specs=placed, out_specs=P(), check_vma=False)
```

time: 124 us -> 121 us (0.976)
  local copies, waits for them, and re-layouts: 1.82 us -> 0.01 us
where the time goes in v5:
time: 121 us
  Pallas kernels  72.2 us (60%)
  starting transfers between devices  25.4 us (21%)
  waiting for transfers between devices  22.3 us (18%)
    pallas_call x3, Pallas kernels, sweep(): pl.pallas_call(functools.partial(sweep_kernel, iteration, exact, axes, na...  71.3 us
    ppermute x21, starting transfers between devices, sum_over(): parts.append(lax.ppermute(x, axis, partners))  25.4 us
    ppermute x21, waiting for transfers between devices, sum_over(): parts.append(lax.ppermute(x, axis, partners))  22.3 us
  transfers between devices with their start and end apart: 21, of which 20 were waited for; matrix products, arithmetic and copies ran while one was open for 0% of the time, Pallas kernels for 0%

profile of v5, /device:TPU:0, one launch (start us, length us, event | category | flops | bytes accessed | tf_op | source)
XLA Modules:
  0.0 121.2 jit_solution(16189044425427875021)
XLA Ops:
  0.0 28.2 %shard_map.48 = (f32[72,128]{1,0:T(8,128)S(1)}, s8[128,64,2048]{2,1,0:T(32,128)(4,1)S(1)}, bf16[256,2048]{1,0:T(8,128)(2,1)S(1)}, bf16[2048,256]{1,0:T(8,128)(2,1)S(1)}) custom-call(s32[128,64,2048]{2,1,0:T(8,128)} %refs_0_.1, f32[64,64]{1,0:T(8,128)} %refs_1_.5, f32[64,128]{1,0:T(8,128)} %bitcast.9, f32[64,2048]{1,0:T(8,128)} %bitcast.7), custom_call_target="tpu_custom_call" | custom-call | flops 17179869184 | bytes 67108864 | tf_op jit(solution)/shard_map/pallas_call | solution.py:251
  28.2 5.1 %collective-permute-start.23 = (f32[72,128]{1,0:T(8,128)S(1)}, f32[72,128]{1,0:T(8,128)S(1)}, u32[]{:S(2)}, u32[]{:S(2)}) collective-permute-start(f32[72,128]{1,0:T(8,128)S(1)} %get-tuple-element.47), channel_id=1, source_target_pairs={{0,3},{1,2},{2,1},{3,0},{4,7},{5,6},{6,5},{7,4},{8,11},{9,10},{10,... | collective-permute-start | bytes 110600 | tf_op jit(solution)/shard_map/ppermute | solution.py:40
  33.3 0.6 collective-permute-start.21
  33.9 1.3 %collective-permute-done.23 = f32[72,128]{1,0:T(8,128)S(1)} collective-permute-done((f32[72,128]{1,0:T(8,128)S(1)}, f32[72,128]{1,0:T(8,128)S(1)}, u32[]{:S(2)}, u32[]{:S(2)}) %collective-permute-start.23) | collective-permute-done | bytes 36896 | tf_op jit(solution)/shard_map/ppermute | solution.py:40
  35.2 2.9 %collective-permute-done.22 = f32[72,128]{1,0:T(8,128)S(1)} collective-permute-done((f32[72,128]{1,0:T(8,128)S(1)}, f32[72,128]{1,0:T(8,128)S(1)}, u32[]{:S(2)}, u32[]{:S(2)}) %collective-permute-start.22) | collective-permute-done | bytes 36896 | tf_op jit(solution)/shard_map/ppermute | solution.py:40
  38.2 2.5 %collective-permute-start.26 = (f32[72,128]{1,0:T(8,128)S(1)}, f32[72,128]{1,0:T(8,128)S(1)}, u32[]{:S(2)}, u32[]{:S(2)}) collective-permute-start(f32[72,128]{1,0:T(8,128)S(1)} %add_add_fusion.7), channel_id=1, source_target_pairs={{0,24},{4,28},{8,16},{12,20},{16,8},{20,12},{24,0},{28,4},{1,25},{... | collective-permute-start | bytes 110600 | tf_op jit(solution)/shard_map/ppermute | solution.py:40
  41.2 0.5 collective-permute-start.24
  41.7 1.6 %collective-permute-done.26 = f32[72,128]{1,0:T(8,128)S(1)} collective-permute-done((f32[72,128]{1,0:T(8,128)S(1)}, f32[72,128]{1,0:T(8,128)S(1)}, u32[]{:S(2)}, u32[]{:S(2)}) %collective-permute-start.26) | collective-permute-done | bytes 36896 | tf_op jit(solution)/shard_map/ppermute | solution.py:40
  43.4 1.3 %collective-permute-done.25 = f32[72,128]{1,0:T(8,128)S(1)} collective-permute-done((f32[72,128]{1,0:T(8,128)S(1)}, f32[72,128]{1,0:T(8,128)S(1)}, u32[]{:S(2)}, u32[]{:S(2)}) %collective-permute-start.25) | collective-permute-done | bytes 36896 | tf_op jit(solution)/shard_map/ppermute | solution.py:40
  45.2 1.2 collective-permute-done.27
  46.5 21.6 %shard_map.49 = (f32[64,128]{1,0:T(8,128)S(1)}, f32[128,64]{1,0:T(8,128)S(1)}, f32[8,128]{1,0:T(8,128)S(1)}, f32[8,64]{1,0:T(8,128)S(1)}) custom-call(s8[128,64,2048]{2,1,0:T(32,128)(4,1)S(1)} %get-tuple-element.46.refs_0_, f32[64,64]{1,0:T(8,128)S(1)} %copy-done.1, f32[64,128]{1,0:T(8,128)S(1)} %bitcast.10, f32[72,128]{1,0:T(8,128)S(1)} %add.132.refs_3_, ...), custom_call_target="tpu_custom_call" | custom-call | flops 17179869184 | bytes 67108864 | tf_op jit(solution)/shard_map/pallas_call | solution.py:251
  68.1 1.5 %collective-permute-start.30 = (f32[64,128]{1,0:T(8,128)S(1)}, f32[64,128]{1,0:T(8,128)S(1)}, u32[]{:S(2)}, u32[]{:S(2)}) collective-permute-start(f32[64,128]{1,0:T(8,128)S(1)} %get-tuple-element.51), channel_id=1, source_target_pairs={{0,3},{1,2},{2,1},{3,0},{4,7},{5,6},{6,5},{7,4},{8,11},{9,10},{10,... | collective-permute-start | bytes 98312 | tf_op jit(solution)/shard_map/ppermute | solution.py:40
  69.5 0.6 collective-permute-start.29
  70.2 2.3 %collective-permute-start.28 = (f32[64,128]{1,0:T(8,128)S(1)}, f32[64,128]{1,0:T(8,128)S(1)}, u32[]{:S(2)}, u32[]{:S(2)}) collective-permute-start(f32[64,128]{1,0:T(8,128)S(1)} %get-tuple-element.51), channel_id=1, source_target_pairs={{0,1},{1,0},{2,3},{3,2},{4,5},{5,4},{6,7},{7,6},{8,9},{9,8},{10,11... | collective-permute-start | bytes 98312 | tf_op jit(solution)/shard_map/ppermute | solution.py:40
  72.5 1.6 %collective-permute-done.30 = f32[64,128]{1,0:T(8,128)S(1)} collective-permute-done((f32[64,128]{1,0:T(8,128)S(1)}, f32[64,128]{1,0:T(8,128)S(1)}, u32[]{:S(2)}, u32[]{:S(2)}) %collective-permute-start.30) | collective-permute-done | bytes 32800 | tf_op jit(solution)/shard_map/ppermute | solution.py:40
  74.8 1.6 %collective-permute-start.33 = (f32[64,128]{1,0:T(8,128)S(1)}, f32[64,128]{1,0:T(8,128)S(1)}, u32[]{:S(2)}, u32[]{:S(2)}) collective-permute-start(f32[64,128]{1,0:T(8,128)S(1)} %add_add_fusion.11), channel_id=1, source_target_pairs={{0,24},{4,28},{8,16},{12,20},{16,8},{20,12},{24,0},{28,4},{1,25},{... | collective-permute-start | bytes 98312 | tf_op jit(solution)/shard_map/ppermute | solution.py:40
  76.8 1.5 %collective-permute-start.31 = (f32[64,128]{1,0:T(8,128)S(1)}, f32[64,128]{1,0:T(8,128)S(1)}, u32[]{:S(2)}, u32[]{:S(2)}) collective-permute-start(f32[64,128]{1,0:T(8,128)S(1)} %add_add_fusion.11), channel_id=1, source_target_pairs={{0,8},{4,12},{8,0},{12,4},{16,24},{20,28},{24,16},{28,20},{1,9},{5... | collective-permute-start | bytes 98312 | tf_op jit(solution)/shard_map/ppermute | solution.py:40
  78.3 1.5 %collective-permute-done.33 = f32[64,128]{1,0:T(8,128)S(1)} collective-permute-done((f32[64,128]{1,0:T(8,128)S(1)}, f32[64,128]{1,0:T(8,128)S(1)}, u32[]{:S(2)}, u32[]{:S(2)}) %collective-permute-start.33) | collective-permute-done | bytes 32800 | tf_op jit(solution)/shard_map/ppermute | solution.py:40
  80.9 1.2 collective-permute-done.34
  82.1 21.5 %shard_map.50 = (f32[64,128]{1,0:T(8,128)S(1)}, f32[128,64]{1,0:T(8,128)S(1)}, f32[8,128]{1,0:T(8,128)S(1)}) custom-call(s8[128,64,2048]{2,1,0:T(32,128)(4,1)S(1)} %get-tuple-element.46.refs_0_, f32[64,64]{1,0:T(8,128)S(1)} %copy-done.1, f32[128,64]{1,0:T(8,128)S(1)} %get-tuple-element.50.refs_2_, f32[64,128]{1,0:T(8,128)S(1)} %add.139.refs_3_, ...), custom_call_target="tpu_custom_call" | custom-call | flops 17179869184 | bytes 67108864 | tf_op jit(solution)/shard_map/pallas_call | solution.py:251
  103.6 2.3 %collective-permute-start.37 = (f32[64,128]{1,0:T(8,128)S(1)}, f32[64,128]{1,0:T(8,128)S(1)}, u32[]{:S(2)}, u32[]{:S(2)}) collective-permute-start(f32[64,128]{1,0:T(8,128)S(1)} %get-tuple-element.55), channel_id=1, source_target_pairs={{0,3},{1,2},{2,1},{3,0},{4,7},{5,6},{6,5},{7,4},{8,11},{9,10},{10,... | collective-permute-start | bytes 98312 | tf_op jit(solution)/shard_map/ppermute | solution.py:40
  105.9 0.8 collective-permute-start.36
  106.7 1.3 %collective-permute-start.35 = (f32[64,128]{1,0:T(8,128)S(1)}, f32[64,128]{1,0:T(8,128)S(1)}, u32[]{:S(2)}, u32[]{:S(2)}) collective-permute-start(f32[64,128]{1,0:T(8,128)S(1)} %get-tuple-element.55), channel_id=1, source_target_pairs={{0,1},{1,0},{2,3},{3,2},{4,5},{5,4},{6,7},{7,6},{8,9},{9,8},{10,11... | collective-permute-start | bytes 98312 | tf_op jit(solution)/shard_map/ppermute | solution.py:40
  108.0 1.4 %collective-permute-done.37 = f32[64,128]{1,0:T(8,128)S(1)} collective-permute-done((f32[64,128]{1,0:T(8,128)S(1)}, f32[64,128]{1,0:T(8,128)S(1)}, u32[]{:S(2)}, u32[]{:S(2)}) %collective-permute-start.37) | collective-permute-done | bytes 32800 | tf_op jit(solution)/shard_map/ppermute | solution.py:40
  109.4 1.3 %collective-permute-done.36 = f32[64,128]{1,0:T(8,128)S(1)} collective-permute-done((f32[64,128]{1,0:T(8,128)S(1)}, f32[64,128]{1,0:T(8,128)S(1)}, u32[]{:S(2)}, u32[]{:S(2)}) %collective-permute-start.36) | collective-permute-done | bytes 32800 | tf_op jit(solution)/shard_map/ppermute | solution.py:40
  111.0 2.5 %collective-permute-start.40 = (f32[64,128]{1,0:T(8,128)S(1)}, f32[64,128]{1,0:T(8,128)S(1)}, u32[]{:S(2)}, u32[]{:S(2)}) collective-permute-start(f32[64,128]{1,0:T(8,128)S(1)} %add_add_fusion.9), channel_id=1, source_target_pairs={{0,24},{4,28},{8,16},{12,20},{16,8},{20,12},{24,0},{28,4},{1,25},{... | collective-permute-start | bytes 98312 | tf_op jit(solution)/shard_map/ppermute | solution.py:40
  113.5 0.5 collective-permute-start.39
  114.0 0.5 collective-permute-start.38
  114.5 1.3 %collective-permute-done.40 = f32[64,128]{1,0:T(8,128)S(1)} collective-permute-done((f32[64,128]{1,0:T(8,128)S(1)}, f32[64,128]{1,0:T(8,128)S(1)}, u32[]{:S(2)}, u32[]{:S(2)}) %collective-permute-start.40) | collective-permute-done | bytes 32800 | tf_op jit(solution)/shard_map/ppermute | solution.py:40
  115.8 1.5 %collective-permute-done.39 = f32[64,128]{1,0:T(8,128)S(1)} collective-permute-done((f32[64,128]{1,0:T(8,128)S(1)}, f32[64,128]{1,0:T(8,128)S(1)}, u32[]{:S(2)}, u32[]{:S(2)}) %collective-permute-start.39) | collective-permute-done | bytes 32800 | tf_op jit(solution)/shard_map/ppermute | solution.py:40
  118.0 1.2 collective-permute-done.41
  119.2 0.9 shard_map.51
  (30 shorter events, 4.3 us)
Async XLA Ops:
  0.0 46.5 %copy-start.1 = (f32[64,64]{1,0:T(8,128)S(1)}, f32[64,64]{1,0:T(8,128)}, u32[]{:S(2)}) copy-start(f32[64,64]{1,0:T(8,128)} %refs_1_.5) | copy-start | bytes 49156
  0.0 46.5 %copy-start.2 = (f32[128,64]{0,1:T(8,128)S(1)}, f32[128,64]{0,1:T(8,128)}, u32[]{:S(2)}) copy-start(f32[128,64]{0,1:T(8,128)} %param.7) | copy-start | bytes 98308
  28.2 7.1 %collective-permute-start.23 = (f32[72,128]{1,0:T(8,128)S(1)}, f32[72,128]{1,0:T(8,128)S(1)}, u32[]{:S(2)}, u32[]{:S(2)}) collective-permute-start(f32[72,128]{1,0:T(8,128)S(1)} %get-tuple-element.47), channel_id=1, source_target_pairs={{0,3},{1,2},{2,1},{3,0},{4,7},{5,6},{6,5},{7,4},{8,11},{9,10},{10,... | collective-permute-start | bytes 110600 | tf_op jit(solution)/shard_map/ppermute | solution.py:40
  33.3 4.9 %collective-permute-start.22 = (f32[72,128]{1,0:T(8,128)S(1)}, f32[72,128]{1,0:T(8,128)S(1)}, u32[]{:S(2)}, u32[]{:S(2)}) collective-permute-start(f32[72,128]{1,0:T(8,128)S(1)} %get-tuple-element.47), channel_id=1, source_target_pairs={{0,2},{1,3},{2,0},{3,1},{4,6},{5,7},{6,4},{7,5},{8,10},{9,11},{10,... | collective-permute-start | bytes 110600 | tf_op jit(solution)/shard_map/ppermute | solution.py:40
  33.3 4.9 %collective-permute-start.21 = (f32[72,128]{1,0:T(8,128)S(1)}, f32[72,128]{1,0:T(8,128)S(1)}, u32[]{:S(2)}, u32[]{:S(2)}) collective-permute-start(f32[72,128]{1,0:T(8,128)S(1)} %get-tuple-element.47), channel_id=1, source_target_pairs={{0,1},{1,0},{2,3},{3,2},{4,5},{5,4},{6,7},{7,6},{8,9},{9,8},{10,11... | collective-permute-start | bytes 110600 | tf_op jit(solution)/shard_map/ppermute | solution.py:40
  38.2 5.2 %collective-permute-start.26 = (f32[72,128]{1,0:T(8,128)S(1)}, f32[72,128]{1,0:T(8,128)S(1)}, u32[]{:S(2)}, u32[]{:S(2)}) collective-permute-start(f32[72,128]{1,0:T(8,128)S(1)} %add_add_fusion.7), channel_id=1, source_target_pairs={{0,24},{4,28},{8,16},{12,20},{16,8},{20,12},{24,0},{28,4},{1,25},{... | collective-permute-start | bytes 110600 | tf_op jit(solution)/shard_map/ppermute | solution.py:40
  40.7 4.0 %collective-permute-start.25 = (f32[72,128]{1,0:T(8,128)S(1)}, f32[72,128]{1,0:T(8,128)S(1)}, u32[]{:S(2)}, u32[]{:S(2)}) collective-permute-start(f32[72,128]{1,0:T(8,128)S(1)} %add_add_fusion.7), channel_id=1, source_target_pairs={{0,16},{4,20},{8,24},{12,28},{16,0},{20,4},{24,8},{28,12},{1,17},{... | collective-permute-start | bytes 110600 | tf_op jit(solution)/shard_map/ppermute | solution.py:40
  41.2 4.0 %collective-permute-start.24 = (f32[72,128]{1,0:T(8,128)S(1)}, f32[72,128]{1,0:T(8,128)S(1)}, u32[]{:S(2)}, u32[]{:S(2)}) collective-permute-start(f32[72,128]{1,0:T(8,128)S(1)} %add_add_fusion.7), channel_id=1, source_target_pairs={{0,8},{4,12},{8,0},{12,4},{16,24},{20,28},{24,16},{28,20},{1,9},{5... | collective-permute-start | bytes 110600 | tf_op jit(solution)/shard_map/ppermute | solution.py:40
  45.2 1.3 %collective-permute-start.27 = (f32[72,128]{1,0:T(8,128)S(1)}, f32[72,128]{1,0:T(8,128)S(1)}, u32[]{:S(2)}, u32[]{:S(2)}) collective-permute-start(f32[72,128]{1,0:T(8,128)S(1)} %add_add_fusion.6), channel_id=1, source_target_pairs={{0,4},{4,0},{8,12},{12,8},{16,20},{20,16},{24,28},{28,24},{1,5},{5... | collective-permute-start | bytes 110600 | tf_op jit(solution)/shard_map/ppermute | solution.py:40
  68.1 6.0 %collective-permute-start.30 = (f32[64,128]{1,0:T(8,128)S(1)}, f32[64,128]{1,0:T(8,128)S(1)}, u32[]{:S(2)}, u32[]{:S(2)}) collective-permute-start(f32[64,128]{1,0:T(8,128)S(1)} %get-tuple-element.51), channel_id=1, source_target_pairs={{0,3},{1,2},{2,1},{3,0},{4,7},{5,6},{6,5},{7,4},{8,11},{9,10},{10,... | collective-permute-start | bytes 98312 | tf_op jit(solution)/shard_map/ppermute | solution.py:40
  69.5 5.0 %collective-permute-start.29 = (f32[64,128]{1,0:T(8,128)S(1)}, f32[64,128]{1,0:T(8,128)S(1)}, u32[]{:S(2)}, u32[]{:S(2)}) collective-permute-start(f32[64,128]{1,0:T(8,128)S(1)} %get-tuple-element.51), channel_id=1, source_target_pairs={{0,2},{1,3},{2,0},{3,1},{4,6},{5,7},{6,4},{7,5},{8,10},{9,11},{10,... | collective-permute-start | bytes 98312 | tf_op jit(solution)/shard_map/ppermute | solution.py:40
  70.2 4.6 %collective-permute-start.28 = (f32[64,128]{1,0:T(8,128)S(1)}, f32[64,128]{1,0:T(8,128)S(1)}, u32[]{:S(2)}, u32[]{:S(2)}) collective-permute-start(f32[64,128]{1,0:T(8,128)S(1)} %get-tuple-element.51), channel_id=1, source_target_pairs={{0,1},{1,0},{2,3},{3,2},{4,5},{5,4},{6,7},{7,6},{8,9},{9,8},{10,11... | collective-permute-start | bytes 98312 | tf_op jit(solution)/shard_map/ppermute | solution.py:40
  74.8 5.1 %collective-permute-start.33 = (f32[64,128]{1,0:T(8,128)S(1)}, f32[64,128]{1,0:T(8,128)S(1)}, u32[]{:S(2)}, u32[]{:S(2)}) collective-permute-start(f32[64,128]{1,0:T(8,128)S(1)} %add_add_fusion.11), channel_id=1, source_target_pairs={{0,24},{4,28},{8,16},{12,20},{16,8},{20,12},{24,0},{28,4},{1,25},{... | collective-permute-start | bytes 98312 | tf_op jit(solution)/shard_map/ppermute | solution.py:40
  76.3 3.9 %collective-permute-start.32 = (f32[64,128]{1,0:T(8,128)S(1)}, f32[64,128]{1,0:T(8,128)S(1)}, u32[]{:S(2)}, u32[]{:S(2)}) collective-permute-start(f32[64,128]{1,0:T(8,128)S(1)} %add_add_fusion.11), channel_id=1, source_target_pairs={{0,16},{4,20},{8,24},{12,28},{16,0},{20,4},{24,8},{28,12},{1,17},{... | collective-permute-start | bytes 98312 | tf_op jit(solution)/shard_map/ppermute | solution.py:40
  76.8 3.9 %collective-permute-start.31 = (f32[64,128]{1,0:T(8,128)S(1)}, f32[64,128]{1,0:T(8,128)S(1)}, u32[]{:S(2)}, u32[]{:S(2)}) collective-permute-start(f32[64,128]{1,0:T(8,128)S(1)} %add_add_fusion.11), channel_id=1, source_target_pairs={{0,8},{4,12},{8,0},{12,4},{16,24},{20,28},{24,16},{28,20},{1,9},{5... | collective-permute-start | bytes 98312 | tf_op jit(solution)/shard_map/ppermute | solution.py:40
  80.8 1.3 %collective-permute-start.34 = (f32[64,128]{1,0:T(8,128)S(1)}, f32[64,128]{1,0:T(8,128)S(1)}, u32[]{:S(2)}, u32[]{:S(2)}) collective-permute-start(f32[64,128]{1,0:T(8,128)S(1)} %add_add_fusion.10), channel_id=1, source_target_pairs={{0,4},{4,0},{8,12},{12,8},{16,20},{20,16},{24,28},{28,24},{1,5},{5... | collective-permute-start | bytes 98312 | tf_op jit(solution)/shard_map/ppermute | solution.py:40
  82.1 38.7 %copy-start = (f32[2048,64]{0,1:T(8,128)S(1)}, f32[2048,64]{0,1:T(8,128)}, u32[]{:S(2)}) copy-start(f32[2048,64]{0,1:T(8,128)} %param.8) | copy-start | bytes 1572868
  103.6 5.8 %collective-permute-start.37 = (f32[64,128]{1,0:T(8,128)S(1)}, f32[64,128]{1,0:T(8,128)S(1)}, u32[]{:S(2)}, u32[]{:S(2)}) collective-permute-start(f32[64,128]{1,0:T(8,128)S(1)} %get-tuple-element.55), channel_id=1, source_target_pairs={{0,3},{1,2},{2,1},{3,0},{4,7},{5,6},{6,5},{7,4},{8,11},{9,10},{10,... | collective-permute-start | bytes 98312 | tf_op jit(solution)/shard_map/ppermute | solution.py:40
  105.9 4.9 %collective-permute-start.36 = (f32[64,128]{1,0:T(8,128)S(1)}, f32[64,128]{1,0:T(8,128)S(1)}, u32[]{:S(2)}, u32[]{:S(2)}) collective-permute-start(f32[64,128]{1,0:T(8,128)S(1)} %get-tuple-element.55), channel_id=1, source_target_pairs={{0,2},{1,3},{2,0},{3,1},{4,6},{5,7},{6,4},{7,5},{8,10},{9,11},{10,... | collective-permute-start | bytes 98312 | tf_op jit(solution)/shard_map/ppermute | solution.py:40
  106.7 4.3 %collective-permute-start.35 = (f32[64,128]{1,0:T(8,128)S(1)}, f32[64,128]{1,0:T(8,128)S(1)}, u32[]{:S(2)}, u32[]{:S(2)}) collective-permute-start(f32[64,128]{1,0:T(8,128)S(1)} %get-tuple-element.55), channel_id=1, source_target_pairs={{0,1},{1,0},{2,3},{3,2},{4,5},{5,4},{6,7},{7,6},{8,9},{9,8},{10,11... | collective-permute-start | bytes 98312 | tf_op jit(solution)/shard_map/ppermute | solution.py:40
  111.0 4.9 %collective-permute-start.40 = (f32[64,128]{1,0:T(8,128)S(1)}, f32[64,128]{1,0:T(8,128)S(1)}, u32[]{:S(2)}, u32[]{:S(2)}) collective-permute-start(f32[64,128]{1,0:T(8,128)S(1)} %add_add_fusion.9), channel_id=1, source_target_pairs={{0,24},{4,28},{8,16},{12,20},{16,8},{20,12},{24,0},{28,4},{1,25},{... | collective-permute-start | bytes 98312 | tf_op jit(solution)/shard_map/ppermute | solution.py:40
  113.5 3.9 %collective-permute-start.39 = (f32[64,128]{1,0:T(8,128)S(1)}, f32[64,128]{1,0:T(8,128)S(1)}, u32[]{:S(2)}, u32[]{:S(2)}) collective-permute-start(f32[64,128]{1,0:T(8,128)S(1)} %add_add_fusion.9), channel_id=1, source_target_pairs={{0,16},{4,20},{8,24},{12,28},{16,0},{20,4},{24,8},{28,12},{1,17},{... | collective-permute-start | bytes 98312 | tf_op jit(solution)/shard_map/ppermute | solution.py:40
  114.0 3.9 %collective-permute-start.38 = (f32[64,128]{1,0:T(8,128)S(1)}, f32[64,128]{1,0:T(8,128)S(1)}, u32[]{:S(2)}, u32[]{:S(2)}) collective-permute-start(f32[64,128]{1,0:T(8,128)S(1)} %add_add_fusion.9), channel_id=1, source_target_pairs={{0,8},{4,12},{8,0},{12,4},{16,24},{20,28},{24,16},{28,20},{1,9},{5... | collective-permute-start | bytes 98312 | tf_op jit(solution)/shard_map/ppermute | solution.py:40
  117.9 1.3 %collective-permute-start.41 = (f32[64,128]{1,0:T(8,128)S(1)}, f32[64,128]{1,0:T(8,128)S(1)}, u32[]{:S(2)}, u32[]{:S(2)}) collective-permute-start(f32[64,128]{1,0:T(8,128)S(1)} %add_add_fusion.8), channel_id=1, source_target_pairs={{0,4},{4,0},{8,12},{12,8},{16,20},{20,16},{24,28},{28,24},{1,5},{5... | collective-permute-start | bytes 98312 | tf_op jit(solution)/shard_map/ppermute | solution.py:40

commit v6 on v5

--- a/solution.py
+++ b/solution.py
@@ -10,7 +10,8 @@
 ITERS = 3
 TILE_USERS = 16
 FETCH_USERS = 8
-SLOTS = 4
+SLOTS = 6
+LAG = 2
 COLUMNS = 256
 GROUP = 4
 MOST = 7.0
@@ -25,10 +26,21 @@
     return high, low
 
 
+def add(parts):
+    while len(parts) > 1:
+        parts = [p + q for p, q in zip(parts[0::2], parts[1::2])]
+    return parts[0]
+
+
 def sum_over(x, axes):
     for axis, size in axes:
         if size & (size - 1):
             x = lax.psum(x, axis)
+            continue
+        if size <= GROUP:
+            sent = jnp.broadcast_to(x[None], (size, *x.shape))
+            parts = lax.all_to_all(sent, axis, 0, 0)
+            x = add([parts[k] for k in range(size)])
             continue
         left = size
         while left > 1:
@@ -38,9 +50,7 @@
             for k in range(1, width):
                 partners = [(i, i ^ (k * left)) for i in range(size)]
                 parts.append(lax.ppermute(x, axis, partners))
-            while len(parts) > 1:
-                parts = [p + q for p, q in zip(parts[0::2], parts[1::2])]
-            x = parts[0]
+            x = add(parts)
     return x
 
 
@@ -155,20 +165,33 @@
             start = block * TILE_USERS
             before = lax.rem(start + users - TILE_USERS, users)
             after = jnp.minimum(start + TILE_USERS, users - TILE_USERS)
+            lagging = []
+
+            def add_phi():
+                chunk, n, parts = lagging.pop(0)
+                if chunk == 0:
+                    keep(n, before + n)
+                pltpu.matmul_acc_lhs(total[n], parts[0], None if n else 0)
+                for part in parts[1:]:
+                    pltpu.matmul_acc_lhs(total[n], part)
+                if n == len(strips) // 2:
+                    push_phi(chunk + 1)
+
             for chunk in range(chunks):
                 at = slice(chunk * COLUMNS, (chunk + 1) * COLUMNS)
                 for n, strip in enumerate(strips):
                     part = block * halves + n // FETCH_USERS
                     if first and chunk == 0 and n % FETCH_USERS == 0:
                         fetch(part).wait()
-                    staged = None if n else 0
                     model = pltpu.matmul_pop(ahead[n])
                     if chunk + 1 < chunks:
-                        pltpu.matmul_acc_lhs(ahead[n], lhs_s[strip, :], staged)
+                        lhs = lhs_s[strip, :]
                     else:
-                        following = operand(after + n)
-                        lhs_s[strip, :] = following
-                        pltpu.matmul_acc_lhs(ahead[n], following, staged)
+                        lhs = operand(after + n)
+                        lhs_s[strip, :] = lhs
+                    pltpu.matmul_acc_lhs(ahead[n], lhs, None if n else 0)
+                    if n == len(strips) // 2:
+                        push_model(chunk + 2)
                     if first:
                         count = r["slots"][lax.rem(part, SLOTS), n % FETCH_USERS, :, at]
                         r["small_out"][start + n, :, at] = count.astype(jnp.int8)
@@ -177,17 +200,11 @@
                     ratio = count.astype(F32) * pltpu.reciprocal(
                         model, approx=True, full_range=False
                     )
-                    if chunk == 0:
-                        keep(n, before + n)
-                    if exact:
-                        high, low = split(ratio)
-                        pltpu.matmul_acc_lhs(total[n], high, staged)
-                        pltpu.matmul_acc_lhs(total[n], low)
-                    else:
-                        pltpu.matmul_acc_lhs(total[n], ratio.astype(BF16), staged)
-                    if n == len(strips) // 2:
-                        push_model(chunk + 2)
-                        push_phi(chunk + 1)
+                    lagging.append((chunk, n, split(ratio) if exact else (ratio.astype(BF16),)))
+                    if len(lagging) > LAG:
+                        add_phi()
+            while lagging:
+                add_phi()
             if first:
 
                 @pl.when((block + 1) * halves + SLOTS <= users // FETCH_USERS)
@@ -257,7 +274,7 @@
             out_specs=[pl.BlockSpec(memory_space=pltpu.VMEM)] * len(outs),
             out_shape=list(outs.values()),
             scratch_shapes=list(scratches.values()),
-            compiler_params=pltpu.CompilerParams(vmem_limit_bytes=(22 if first else 8) * 1024 * 1024),
+            compiler_params=pltpu.CompilerParams(vmem_limit_bytes=(28 if first else 8) * 1024 * 1024),
             cost_estimate=pl.CostEstimate(
                 flops=2 * (3 if exact else 2) * users * weeks * items * 256,
                 bytes_accessed=4 * users * weeks * items,

time: 121 us -> 126 us (1.041)
  blocking collectives: 0 us -> 30.6 us
  starting transfers between devices: 25.4 us -> 10.9 us
  waiting for transfers between devices: 22.3 us -> 12.8 us
  Pallas kernels: 72.2 us -> 70.2 us
    all_to_all x0 -> x3, blocking collectives: none -> 30.6 us  [sum_over(): parts = lax.all_to_all(sent, axis, 0, 0)]
    ppermute x21 -> x12, starting transfers between devices: 25.4 us -> 10.9 us  [sum_over(): parts.append(lax.ppermute(x, axis, partners))]
    ppermute x21 -> x12, waiting for transfers between devices: 22.3 us -> 12.8 us  [sum_over(): parts.append(lax.ppermute(x, axis, partners))]
    pallas_call x3, Pallas kernels: 71.3 us -> 69.3 us  [sweep(): pl.pallas_call(functools.partial(sweep_kernel, iteration, exact, axes, na...]
  transfers between devices with their start and end apart: 21 -> 12, of which waited for: 20 -> 11; matrix products, arithmetic and copies ran while one was open for 0% -> 0% of each run, Pallas kernels for 0% -> 0%
where the time goes in v6:
time: 126 us
  Pallas kernels  70.2 us (56%)
  blocking collectives  30.6 us (24%)
  waiting for transfers between devices  12.8 us (10%)
  starting transfers between devices  10.9 us (9%)
    pallas_call x3, Pallas kernels, sweep(): pl.pallas_call(functools.partial(sweep_kernel, iteration, exact, axes, na...  69.3 us
    all_to_all x3, blocking collectives, sum_over(): parts = lax.all_to_all(sent, axis, 0, 0)  30.6 us
    ppermute x12, waiting for transfers between devices, sum_over(): parts.append(lax.ppermute(x, axis, partners))  12.8 us
    ppermute x12, starting transfers between devices, sum_over(): parts.append(lax.ppermute(x, axis, partners))  10.9 us
  transfers between devices with their start and end apart: 12, of which 11 were waited for; matrix products, arithmetic and copies ran while one was open for 0% of the time, Pallas kernels for 0%

profile of v6, /device:TPU:0, one launch (start us, length us, event | category | flops | bytes accessed | tf_op | source)
XLA Modules:
  0.0 125.8 jit_solution(14857015699938612235)
XLA Ops:
  0.0 26.0 %shard_map.48 = (f32[72,128]{1,0:T(8,128)S(1)}, s8[128,64,2048]{2,1,0:T(32,128)(4,1)S(1)}, bf16[256,2048]{1,0:T(8,128)(2,1)S(1)}, bf16[2048,256]{1,0:T(8,128)(2,1)S(1)}) custom-call(s32[128,64,2048]{2,1,0:T(8,128)} %refs_0_.1, f32[64,64]{1,0:T(8,128)} %refs_1_.5, f32[64,128]{1,0:T(8,128)} %bitcast.33, f32[64,2048]{1,0:T(8,128)} %bitcast.31), custom_call_target="tpu_custom_call" | custom-call | flops 17179869184 | bytes 67108864 | tf_op jit(solution)/shard_map/pallas_call | solution.py:268
  26.0 12.8 %all_to_all.30 = f32[4,72,128]{2,1,0:T(8,128)S(1)} all-to-all(f32[4,72,128]{2,1,0:T(8,128)S(1)} %broadcast_in_dim.12), channel_id=1, replica_groups=mesh['item'=8,'week'=4] {'week'}, dimensions={0} | all-to-all | bytes 294912 | tf_op jit(solution)/shard_map/all_to_all | solution.py:42
  38.8 1.6 %collective-permute-start.13 = (f32[72,128]{1,0:T(8,128)S(1)}, f32[72,128]{1,0:T(8,128)S(1)}, u32[]{:S(2)}, u32[]{:S(2)}) collective-permute-start(f32[72,128]{1,0:T(8,128)S(1)} %fusion.7), channel_id=1, source_target_pairs={{0,16},{4,20},{8,24},{12,28},{16,0},{20,4},{24,8},{28,12},{1,17},{... | collective-permute-start | bytes 110600 | tf_op jit(solution)/shard_map/ppermute | solution.py:52
  40.4 1.4 %collective-permute-start.14 = (f32[72,128]{1,0:T(8,128)S(1)}, f32[72,128]{1,0:T(8,128)S(1)}, u32[]{:S(2)}, u32[]{:S(2)}) collective-permute-start(f32[72,128]{1,0:T(8,128)S(1)} %fusion.7), channel_id=1, source_target_pairs={{0,24},{4,28},{8,16},{12,20},{16,8},{20,12},{24,0},{28,4},{1,25},{... | collective-permute-start | bytes 110600 | tf_op jit(solution)/shard_map/ppermute | solution.py:52
  41.9 0.5 collective-permute-start.12
  42.4 0.5 collective-permute-done.13
  42.9 2.4 %collective-permute-done.14 = f32[72,128]{1,0:T(8,128)S(1)} collective-permute-done((f32[72,128]{1,0:T(8,128)S(1)}, f32[72,128]{1,0:T(8,128)S(1)}, u32[]{:S(2)}, u32[]{:S(2)}) %collective-permute-start.14) | collective-permute-done | bytes 36896 | tf_op jit(solution)/shard_map/ppermute | solution.py:52
  45.3 0.5 collective-permute-done.12
  45.8 0.1 collective-permute-start.15
  45.9 1.2 collective-permute-done.15
  47.1 21.6 %shard_map.49 = (f32[64,128]{1,0:T(8,128)S(1)}, f32[128,64]{1,0:T(8,128)S(1)}, f32[8,128]{1,0:T(8,128)S(1)}, f32[8,64]{1,0:T(8,128)S(1)}) custom-call(s8[128,64,2048]{2,1,0:T(32,128)(4,1)S(1)} %get-tuple-element.46.refs_0_, f32[64,64]{1,0:T(8,128)S(1)} %copy-done.1, f32[64,128]{1,0:T(8,128)S(1)} %bitcast.34, f32[72,128]{1,0:T(8,128)S(1)} %add.163.refs_3_, ...), custom_call_target="tpu_custom_call" | custom-call | flops 17179869184 | bytes 67108864 | tf_op jit(solution)/shard_map/pallas_call | solution.py:268
  68.8 8.8 %all_to_all.31 = f32[4,64,128]{2,1,0:T(8,128)S(1)} all-to-all(f32[4,64,128]{2,1,0:T(8,128)S(1)} %broadcast_in_dim.13), channel_id=1, replica_groups=mesh['item'=8,'week'=4] {'week'}, dimensions={0} | all-to-all | bytes 262144 | tf_op jit(solution)/shard_map/all_to_all | solution.py:42
  77.6 1.6 %collective-permute-start.17 = (f32[64,128]{1,0:T(8,128)S(1)}, f32[64,128]{1,0:T(8,128)S(1)}, u32[]{:S(2)}, u32[]{:S(2)}) collective-permute-start(f32[64,128]{1,0:T(8,128)S(1)} %fusion.11), channel_id=1, source_target_pairs={{0,16},{4,20},{8,24},{12,28},{16,0},{20,4},{24,8},{28,12},{1,17},{... | collective-permute-start | bytes 98312 | tf_op jit(solution)/shard_map/ppermute | solution.py:52
  79.2 0.9 collective-permute-start.18
  80.1 1.1 collective-permute-start.16
  81.2 0.6 collective-permute-done.17
  81.7 2.3 %collective-permute-done.18 = f32[64,128]{1,0:T(8,128)S(1)} collective-permute-done((f32[64,128]{1,0:T(8,128)S(1)}, f32[64,128]{1,0:T(8,128)S(1)}, u32[]{:S(2)}, u32[]{:S(2)}) %collective-permute-start.18) | collective-permute-done | bytes 32800 | tf_op jit(solution)/shard_map/ppermute | solution.py:52
  84.0 0.0 collective-permute-done.16
  84.1 0.1 collective-permute-start.19
  84.1 1.2 collective-permute-done.19
  85.3 21.6 %shard_map.50 = (f32[64,128]{1,0:T(8,128)S(1)}, f32[128,64]{1,0:T(8,128)S(1)}, f32[8,128]{1,0:T(8,128)S(1)}) custom-call(s8[128,64,2048]{2,1,0:T(32,128)(4,1)S(1)} %get-tuple-element.46.refs_0_, f32[64,64]{1,0:T(8,128)S(1)} %copy-done.1, f32[128,64]{1,0:T(8,128)S(1)} %get-tuple-element.50.refs_2_, f32[64,128]{1,0:T(8,128)S(1)} %add.171.refs_3_, ...), custom_call_target="tpu_custom_call" | custom-call | flops 17179869184 | bytes 67108864 | tf_op jit(solution)/shard_map/pallas_call | solution.py:268
  107.0 9.0 %all_to_all.32 = f32[4,64,128]{2,1,0:T(8,128)S(1)} all-to-all(f32[4,64,128]{2,1,0:T(8,128)S(1)} %broadcast_in_dim.14), channel_id=1, replica_groups=mesh['item'=8,'week'=4] {'week'}, dimensions={0} | all-to-all | bytes 262144 | tf_op jit(solution)/shard_map/all_to_all | solution.py:42
  116.0 1.2 collective-permute-start.21
  117.2 1.4 %collective-permute-start.22 = (f32[64,128]{1,0:T(8,128)S(1)}, f32[64,128]{1,0:T(8,128)S(1)}, u32[]{:S(2)}, u32[]{:S(2)}) collective-permute-start(f32[64,128]{1,0:T(8,128)S(1)} %fusion.9), channel_id=1, source_target_pairs={{0,24},{4,28},{8,16},{12,20},{16,8},{20,12},{24,0},{28,4},{1,25},{... | collective-permute-start | bytes 98312 | tf_op jit(solution)/shard_map/ppermute | solution.py:52
  118.6 1.0 collective-permute-start.20
  119.6 0.4 collective-permute-done.21
  120.0 2.0 %collective-permute-done.22 = f32[64,128]{1,0:T(8,128)S(1)} collective-permute-done((f32[64,128]{1,0:T(8,128)S(1)}, f32[64,128]{1,0:T(8,128)S(1)}, u32[]{:S(2)}, u32[]{:S(2)}) %collective-permute-start.22) | collective-permute-done | bytes 32800 | tf_op jit(solution)/shard_map/ppermute | solution.py:52
  122.0 0.5 collective-permute-done.20
  122.5 0.1 collective-permute-start.23
  122.6 1.2 collective-permute-done.23
  123.8 0.9 shard_map.51
  125.4 0.2 conditional.1
  (18 shorter events, 0.1 us)
Async XLA Ops:
  0.0 47.1 %copy-start.1 = (f32[64,64]{1,0:T(8,128)S(1)}, f32[64,64]{1,0:T(8,128)}, u32[]{:S(2)}) copy-start(f32[64,64]{1,0:T(8,128)} %refs_1_.5) | copy-start | bytes 49156
  0.0 47.1 %copy-start.2 = (f32[128,64]{0,1:T(8,128)S(1)}, f32[128,64]{0,1:T(8,128)}, u32[]{:S(2)}) copy-start(f32[128,64]{0,1:T(8,128)} %param.7) | copy-start | bytes 98308
  38.8 4.1 %collective-permute-start.13 = (f32[72,128]{1,0:T(8,128)S(1)}, f32[72,128]{1,0:T(8,128)S(1)}, u32[]{:S(2)}, u32[]{:S(2)}) collective-permute-start(f32[72,128]{1,0:T(8,128)S(1)} %fusion.7), channel_id=1, source_target_pairs={{0,16},{4,20},{8,24},{12,28},{16,0},{20,4},{24,8},{28,12},{1,17},{... | collective-permute-start | bytes 110600 | tf_op jit(solution)/shard_map/ppermute | solution.py:52
  40.4 4.9 %collective-permute-start.14 = (f32[72,128]{1,0:T(8,128)S(1)}, f32[72,128]{1,0:T(8,128)S(1)}, u32[]{:S(2)}, u32[]{:S(2)}) collective-permute-start(f32[72,128]{1,0:T(8,128)S(1)} %fusion.7), channel_id=1, source_target_pairs={{0,24},{4,28},{8,16},{12,20},{16,8},{20,12},{24,0},{28,4},{1,25},{... | collective-permute-start | bytes 110600 | tf_op jit(solution)/shard_map/ppermute | solution.py:52
  41.9 4.0 %collective-permute-start.12 = (f32[72,128]{1,0:T(8,128)S(1)}, f32[72,128]{1,0:T(8,128)S(1)}, u32[]{:S(2)}, u32[]{:S(2)}) collective-permute-start(f32[72,128]{1,0:T(8,128)S(1)} %fusion.7), channel_id=1, source_target_pairs={{0,8},{4,12},{8,0},{12,4},{16,24},{20,28},{24,16},{28,20},{1,9},{5... | collective-permute-start | bytes 110600 | tf_op jit(solution)/shard_map/ppermute | solution.py:52
  45.8 1.3 %collective-permute-start.15 = (f32[72,128]{1,0:T(8,128)S(1)}, f32[72,128]{1,0:T(8,128)S(1)}, u32[]{:S(2)}, u32[]{:S(2)}) collective-permute-start(f32[72,128]{1,0:T(8,128)S(1)} %add_add_fusion.3), channel_id=1, source_target_pairs={{0,4},{4,0},{8,12},{12,8},{16,20},{20,16},{24,28},{28,24},{1,5},{5... | collective-permute-start | bytes 110600 | tf_op jit(solution)/shard_map/ppermute | solution.py:52
  77.6 4.1 %collective-permute-start.17 = (f32[64,128]{1,0:T(8,128)S(1)}, f32[64,128]{1,0:T(8,128)S(1)}, u32[]{:S(2)}, u32[]{:S(2)}) collective-permute-start(f32[64,128]{1,0:T(8,128)S(1)} %fusion.11), channel_id=1, source_target_pairs={{0,16},{4,20},{8,24},{12,28},{16,0},{20,4},{24,8},{28,12},{1,17},{... | collective-permute-start | bytes 98312 | tf_op jit(solution)/shard_map/ppermute | solution.py:52
  79.2 4.8 %collective-permute-start.18 = (f32[64,128]{1,0:T(8,128)S(1)}, f32[64,128]{1,0:T(8,128)S(1)}, u32[]{:S(2)}, u32[]{:S(2)}) collective-permute-start(f32[64,128]{1,0:T(8,128)S(1)} %fusion.11), channel_id=1, source_target_pairs={{0,24},{4,28},{8,16},{12,20},{16,8},{20,12},{24,0},{28,4},{1,25},{... | collective-permute-start | bytes 98312 | tf_op jit(solution)/shard_map/ppermute | solution.py:52
  80.1 3.9 %collective-permute-start.16 = (f32[64,128]{1,0:T(8,128)S(1)}, f32[64,128]{1,0:T(8,128)S(1)}, u32[]{:S(2)}, u32[]{:S(2)}) collective-permute-start(f32[64,128]{1,0:T(8,128)S(1)} %fusion.11), channel_id=1, source_target_pairs={{0,8},{4,12},{8,0},{12,4},{16,24},{20,28},{24,16},{28,20},{1,9},{5... | collective-permute-start | bytes 98312 | tf_op jit(solution)/shard_map/ppermute | solution.py:52
  84.1 1.3 %collective-permute-start.19 = (f32[64,128]{1,0:T(8,128)S(1)}, f32[64,128]{1,0:T(8,128)S(1)}, u32[]{:S(2)}, u32[]{:S(2)}) collective-permute-start(f32[64,128]{1,0:T(8,128)S(1)} %add_add_fusion.5), channel_id=1, source_target_pairs={{0,4},{4,0},{8,12},{12,8},{16,20},{20,16},{24,28},{28,24},{1,5},{5... | collective-permute-start | bytes 98312 | tf_op jit(solution)/shard_map/ppermute | solution.py:52
  85.3 40.1 %copy-start = (f32[2048,64]{0,1:T(8,128)S(1)}, f32[2048,64]{0,1:T(8,128)}, u32[]{:S(2)}) copy-start(f32[2048,64]{0,1:T(8,128)} %param.8) | copy-start | bytes 1572868
  116.0 4.0 %collective-permute-start.21 = (f32[64,128]{1,0:T(8,128)S(1)}, f32[64,128]{1,0:T(8,128)S(1)}, u32[]{:S(2)}, u32[]{:S(2)}) collective-permute-start(f32[64,128]{1,0:T(8,128)S(1)} %fusion.9), channel_id=1, source_target_pairs={{0,16},{4,20},{8,24},{12,28},{16,0},{20,4},{24,8},{28,12},{1,17},{... | collective-permute-start | bytes 98312 | tf_op jit(solution)/shard_map/ppermute | solution.py:52
  117.2 4.8 %collective-permute-start.22 = (f32[64,128]{1,0:T(8,128)S(1)}, f32[64,128]{1,0:T(8,128)S(1)}, u32[]{:S(2)}, u32[]{:S(2)}) collective-permute-start(f32[64,128]{1,0:T(8,128)S(1)} %fusion.9), channel_id=1, source_target_pairs={{0,24},{4,28},{8,16},{12,20},{16,8},{20,12},{24,0},{28,4},{1,25},{... | collective-permute-start | bytes 98312 | tf_op jit(solution)/shard_map/ppermute | solution.py:52
  118.6 3.9 %collective-permute-start.20 = (f32[64,128]{1,0:T(8,128)S(1)}, f32[64,128]{1,0:T(8,128)S(1)}, u32[]{:S(2)}, u32[]{:S(2)}) collective-permute-start(f32[64,128]{1,0:T(8,128)S(1)} %fusion.9), channel_id=1, source_target_pairs={{0,8},{4,12},{8,0},{12,4},{16,24},{20,28},{24,16},{28,20},{1,9},{5... | collective-permute-start | bytes 98312 | tf_op jit(solution)/shard_map/ppermute | solution.py:52
  122.5 1.3 %collective-permute-start.23 = (f32[64,128]{1,0:T(8,128)S(1)}, f32[64,128]{1,0:T(8,128)S(1)}, u32[]{:S(2)}, u32[]{:S(2)}) collective-permute-start(f32[64,128]{1,0:T(8,128)S(1)} %add_add_fusion.4), channel_id=1, source_target_pairs={{0,4},{4,0},{8,12},{12,8},{16,20},{20,16},{24,28},{28,24},{1,5},{5... | collective-permute-start | bytes 98312 | tf_op jit(solution)/shard_map/ppermute | solution.py:52

commit v7 on v6

--- a/solution.py
+++ b/solution.py
@@ -8,16 +8,16 @@
 from jax.sharding import PartitionSpec as P
 
 ITERS = 3
-TILE_USERS = 16
-FETCH_USERS = 8
-SLOTS = 6
+FIRST_TILE, NEXT_TILE = 8, 16
+SLOTS = 4
 LAG = 2
 COLUMNS = 256
 GROUP = 4
 MOST = 7.0
-ROUNDING = 2.8e-6
+ROUNDING = 5.6e-6
 ALLOWED = 6.4e-9
 F32, BF16 = jnp.float32, jnp.bfloat16
+SMALL = jnp.float8_e4m3fn
 
 
 def split(x):
@@ -36,11 +36,6 @@
     for axis, size in axes:
         if size & (size - 1):
             x = lax.psum(x, axis)
-            continue
-        if size <= GROUP:
-            sent = jnp.broadcast_to(x[None], (size, *x.shape))
-            parts = lax.all_to_all(sent, axis, 0, 0)
-            x = add([parts[k] for k in range(size)])
             continue
         left = size
         while left > 1:
@@ -89,15 +84,15 @@
     counts = r["counts"]
     users, weeks, items = counts.shape
     first = iteration == 0
+    stream = "slots" in r
     rank = r["week"].shape[1]
-    rows = TILE_USERS * weeks
-    blocks = users // TILE_USERS
-    halves = TILE_USERS // FETCH_USERS
+    tile = FIRST_TILE if stream else NEXT_TILE
+    blocks = users // tile
     model_w, phi_w, factor_s, week_s = r["model_w"], r["phi_w"], r["factor_s"], r["week_s"]
 
-    def fetch(part):
-        at = pl.ds(pl.multiple_of(part * FETCH_USERS, FETCH_USERS), FETCH_USERS)
-        slot = lax.rem(part, SLOTS)
+    def fetch(block):
+        at = pl.ds(pl.multiple_of(block * tile, tile), tile)
+        slot = lax.rem(block, SLOTS)
         return pltpu.make_async_copy(
             counts.at[at], r["slots"].at[slot], r["arrived"].at[slot]
         )
@@ -105,9 +100,10 @@
     week_at = lax.broadcasted_iota(jnp.int32, (weeks, 1), 0) + lax.axis_index("week") * weeks
     week_s[...] = r["week"][...] * spread(week_at, 27146)
 
+    if stream:
+        for block in range(min(SLOTS, blocks)):
+            fetch(jnp.int32(block)).start()
     if first:
-        for part in range(min(SLOTS, users // FETCH_USERS)):
-            fetch(jnp.int32(part)).start()
         item_at = lax.broadcasted_iota(jnp.int32, (1, items), 1)
         item_at = item_at + lax.axis_index("item") * items
         high, low = split(r["item_t"][...] * spread(item_at, 40503))
@@ -132,7 +128,7 @@
         r["factor_out"][...] = new
         r["sound_out"][...] = sound if iteration == 1 else sound * r["sound"][...]
 
-    strips = [slice(n * weeks, (n + 1) * weeks) for n in range(TILE_USERS)]
+    strips = [slice(n * weeks, (n + 1) * weeks) for n in range(tile)]
     chunks = items // COLUMNS
     lhs_s, phi_s = r["lhs_s"], r["phi_s"]
 
@@ -162,10 +158,12 @@
         push_phi(0)
 
         def body(block, carry):
-            start = block * TILE_USERS
-            before = lax.rem(start + users - TILE_USERS, users)
-            after = jnp.minimum(start + TILE_USERS, users - TILE_USERS)
+            start = block * tile
+            before = lax.rem(start + users - tile, users)
+            after = jnp.minimum(start + tile, users - tile)
             lagging = []
+            if stream:
+                fetch(block).wait()
 
             def add_phi():
                 chunk, n, parts = lagging.pop(0)
@@ -180,9 +178,6 @@
             for chunk in range(chunks):
                 at = slice(chunk * COLUMNS, (chunk + 1) * COLUMNS)
                 for n, strip in enumerate(strips):
-                    part = block * halves + n // FETCH_USERS
-                    if first and chunk == 0 and n % FETCH_USERS == 0:
-                        fetch(part).wait()
                     model = pltpu.matmul_pop(ahead[n])
                     if chunk + 1 < chunks:
                         lhs = lhs_s[strip, :]
@@ -192,31 +187,35 @@
                     pltpu.matmul_acc_lhs(ahead[n], lhs, None if n else 0)
                     if n == len(strips) // 2:
                         push_model(chunk + 2)
-                    if first:
-                        count = r["slots"][lax.rem(part, SLOTS), n % FETCH_USERS, :, at]
-                        r["small_out"][start + n, :, at] = count.astype(jnp.int8)
+                    if stream:
+                        count = r["slots"][lax.rem(block, SLOTS), n, :, at]
+                        count = count.astype(F32)
+                        if "small_out" in r:
+                            r["small_out"][start + n, :, at] = count.astype(SMALL)
+                        count = count.astype(BF16)
                     else:
-                        count = counts[start + n, :, at].astype(jnp.int32)
-                    ratio = count.astype(F32) * pltpu.reciprocal(
-                        model, approx=True, full_range=False
-                    )
-                    lagging.append((chunk, n, split(ratio) if exact else (ratio.astype(BF16),)))
+                        count = counts[start + n, :, at].astype(BF16)
+                    inverse = pltpu.reciprocal(model, approx=True, full_range=False)
+                    if exact:
+                        parts = split(count.astype(F32) * inverse)
+                    else:
+                        parts = (count * inverse.astype(BF16),)
+                    lagging.append((chunk, n, parts))
                     if len(lagging) > LAG:
                         add_phi()
             while lagging:
                 add_phi()
-            if first:
-
-                @pl.when((block + 1) * halves + SLOTS <= users // FETCH_USERS)
+            if stream:
+
+                @pl.when(block + SLOTS < blocks)
                 def _():
-                    for half in range(halves):
-                        fetch(block * halves + SLOTS + half).start()
+                    fetch(block + SLOTS).start()
 
             return carry
 
         lax.fori_loop(0, blocks, body, 0)
-        for n in range(TILE_USERS):
-            keep(n, users - TILE_USERS + n)
+        for n in range(tile):
+            keep(n, users - tile + n)
         nothing = jnp.zeros((weeks, COLUMNS), BF16)
         for ref in ahead:
             pltpu.matmul_pop(ref)
@@ -224,7 +223,7 @@
             pltpu.matmul_acc_lhs(ref, nothing, 0)
             pltpu.matmul_pop(ref)
 
-    pl.run_scoped(matmuls, *[[unit] * TILE_USERS for unit in units])
+    pl.run_scoped(matmuls, *[[unit] * tile for unit in units])
     r["phi_out"][: users // 2, :] = pack(phi_s[...])
     if first:
         n_item, n_week = (dict(axes)[a] for a in ("item", "week"))
@@ -240,7 +239,6 @@
 def updates(exact, mesh, axes, counts, user_factor, item_factor, week_factor):
     users, rank = user_factor.shape
     weeks, items = counts.shape[1:]
-    rows = TILE_USERS * weeks
     factor_t, item_t = user_factor.T, item_factor.T
     travel = sorted(axes, reverse=True)
 
@@ -248,33 +246,33 @@
         return jax.ShapeDtypeStruct(dims, dtype)
 
     stream = {
-        "slots": pltpu.VMEM((SLOTS, FETCH_USERS, weeks, items), jnp.int32),
+        "slots": pltpu.VMEM((SLOTS, FIRST_TILE, weeks, items), jnp.int32),
         "arrived": pltpu.SemaphoreType.DMA((SLOTS,)),
     }
     scratch = {
         "factor_s": pltpu.VMEM((users, rank), F32),
         "week_s": pltpu.VMEM((weeks, rank), F32),
         "phi_s": pltpu.VMEM((users, rank), F32),
-        "lhs_s": pltpu.VMEM((rows, 4 * rank), BF16),
+        "lhs_s": pltpu.VMEM((NEXT_TILE * weeks, 4 * rank), BF16),
     }
     with jax.sharding.use_abstract_mesh(mesh.abstract_mesh):
         units = [pltpu.ACC(unit)((weeks, COLUMNS), F32) for unit in (0, 1)]
 
     def sweep(iteration, counts, ins, outs):
         ins = {"counts": counts, "week": week_factor, **ins}
-        first = iteration == 0
-        scratches = {**stream, **scratch} if first else scratch
+        streamed = counts.dtype == jnp.int32
+        scratches = {**stream, **scratch} if streamed else scratch
         names = list(ins) + list(outs) + list(scratches)
         results = pl.pallas_call(
             functools.partial(sweep_kernel, iteration, exact, axes, names, units),
             in_specs=[
-                pl.BlockSpec(memory_space=pl.ANY if first and n == "counts" else pltpu.VMEM)
+                pl.BlockSpec(memory_space=pl.ANY if streamed and n == "counts" else pltpu.VMEM)
                 for n in ins
             ],
             out_specs=[pl.BlockSpec(memory_space=pltpu.VMEM)] * len(outs),
             out_shape=list(outs.values()),
             scratch_shapes=list(scratches.values()),
-            compiler_params=pltpu.CompilerParams(vmem_limit_bytes=(28 if first else 8) * 1024 * 1024),
+            compiler_params=pltpu.CompilerParams(vmem_limit_bytes=(22 if streamed else 8) * 1024 * 1024),
             cost_estimate=pl.CostEstimate(
                 flops=2 * (3 if exact else 2) * users * weeks * items * 256,
                 bytes_accessed=4 * users * weeks * items,
@@ -285,12 +283,15 @@
 
     packed = shape((users // 2, 2 * rank))
     factor_out, sound_out = shape((users, rank)), shape((8, 128))
-    got = sweep(
-        0, counts, {"factor_t": factor_t, "item_t": item_t},
-        {"phi_out": shape((users // 2 + 8, 2 * rank)), "small_out": shape(counts.shape, jnp.int8),
-         "model_w": shape((4 * rank, items), BF16), "phi_w": shape((items, COLUMNS), BF16)},
-    )
-    small, weights = got["small_out"], {n: got[n] for n in ("model_w", "phi_w")}
+    outs = {
+        "phi_out": shape((users // 2 + 8, 2 * rank)),
+        "model_w": shape((4 * rank, items), BF16),
+        "phi_w": shape((items, COLUMNS), BF16),
+    }
+    if not exact:
+        outs["small_out"] = shape(counts.shape, SMALL)
+    got = sweep(0, counts, {"factor_t": factor_t, "item_t": item_t}, outs)
+    small, weights = got.get("small_out", counts), {n: got[n] for n in ("model_w", "phi_w")}
     summed = sum_over(got["phi_out"], travel)
     got = sweep(
         1, small, {"factor_t": factor_t, "summed": summed, **weights},

time: 126 us -> 112 us (0.89)
  blocking collectives: 30.6 us -> 0 us
  starting transfers between devices: 10.9 us -> 25.4 us
  waiting for transfers between devices: 12.8 us -> 22.3 us
  Pallas kernels: 70.2 us -> 63.4 us
    all_to_all x3 -> x0, blocking collectives: 30.6 us -> none  [sum_over(): parts = lax.all_to_all(sent, axis, 0, 0)]
    ppermute x12 -> x21, starting transfers between devices: 10.9 us -> 25.4 us  [sum_over(): parts.append(lax.ppermute(x, axis, partners))]
    ppermute x12 -> x21, waiting for transfers between devices: 12.8 us -> 22.3 us  [sum_over(): parts.append(lax.ppermute(x, axis, partners))]
    pallas_call x3, Pallas kernels: 69.3 us -> 62.5 us  [sweep(): pl.pallas_call(functools.partial(sweep_kernel, iteration, exact, axes, na...]
  transfers between devices with their start and end apart: 12 -> 21, of which waited for: 11 -> 20; matrix products, arithmetic and copies ran while one was open for 0% -> 0% of each run, Pallas kernels for 0% -> 0%
where the time goes in v7:
time: 112 us
  Pallas kernels  63.4 us (57%)
  starting transfers between devices  25.4 us (23%)
  waiting for transfers between devices  22.3 us (20%)
    pallas_call x3, Pallas kernels, sweep(): pl.pallas_call(functools.partial(sweep_kernel, iteration, exact, axes, na...  62.5 us
    ppermute x21, starting transfers between devices, sum_over(): parts.append(lax.ppermute(x, axis, partners))  25.4 us
    ppermute x21, waiting for transfers between devices, sum_over(): parts.append(lax.ppermute(x, axis, partners))  22.3 us
  transfers between devices with their start and end apart: 21, of which 20 were waited for; matrix products, arithmetic and copies ran while one was open for 0% of the time, Pallas kernels for 0%

profile of v7, /device:TPU:0, one launch (start us, length us, event | category | flops | bytes accessed | tf_op | source)
XLA Modules:
  0.0 112.3 jit_solution(8250970211012112419)
XLA Ops:
  0.0 23.2 %shard_map.48 = (f32[72,128]{1,0:T(8,128)S(1)}, bf16[256,2048]{1,0:T(8,128)(2,1)S(1)}, bf16[2048,256]{1,0:T(8,128)(2,1)S(1)}, f8e4m3fn[128,64,2048]{2,1,0:T(32,128)(4,1)S(1)}) custom-call(s32[128,64,2048]{2,1,0:T(8,128)} %refs_0_.1, f32[64,64]{1,0:T(8,128)} %refs_1_.5, f32[64,128]{1,0:T(8,128)} %bitcast.9, f32[64,2048]{1,0:T(8,128)} %bitcast.7), custom_call_target="tpu_custom_call" | custom-call | flops 17179869184 | bytes 67108864 | tf_op jit(solution)/shard_map/pallas_call | solution.py:266
  23.2 5.1 %collective-permute-start.23 = (f32[72,128]{1,0:T(8,128)S(1)}, f32[72,128]{1,0:T(8,128)S(1)}, u32[]{:S(2)}, u32[]{:S(2)}) collective-permute-start(f32[72,128]{1,0:T(8,128)S(1)} %get-tuple-element.46), channel_id=1, source_target_pairs={{0,3},{1,2},{2,1},{3,0},{4,7},{5,6},{6,5},{7,4},{8,11},{9,10},{10,... | collective-permute-start | bytes 110600 | tf_op jit(solution)/shard_map/ppermute | solution.py:47
  28.4 0.6 collective-permute-start.21
  29.0 1.3 %collective-permute-done.23 = f32[72,128]{1,0:T(8,128)S(1)} collective-permute-done((f32[72,128]{1,0:T(8,128)S(1)}, f32[72,128]{1,0:T(8,128)S(1)}, u32[]{:S(2)}, u32[]{:S(2)}) %collective-permute-start.23) | collective-permute-done | bytes 36896 | tf_op jit(solution)/shard_map/ppermute | solution.py:47
  30.3 2.9 %collective-permute-done.22 = f32[72,128]{1,0:T(8,128)S(1)} collective-permute-done((f32[72,128]{1,0:T(8,128)S(1)}, f32[72,128]{1,0:T(8,128)S(1)}, u32[]{:S(2)}, u32[]{:S(2)}) %collective-permute-start.22) | collective-permute-done | bytes 36896 | tf_op jit(solution)/shard_map/ppermute | solution.py:47
  33.2 2.5 %collective-permute-start.26 = (f32[72,128]{1,0:T(8,128)S(1)}, f32[72,128]{1,0:T(8,128)S(1)}, u32[]{:S(2)}, u32[]{:S(2)}) collective-permute-start(f32[72,128]{1,0:T(8,128)S(1)} %add_add_fusion.7), channel_id=1, source_target_pairs={{0,24},{4,28},{8,16},{12,20},{16,8},{20,12},{24,0},{28,4},{1,25},{... | collective-permute-start | bytes 110600 | tf_op jit(solution)/shard_map/ppermute | solution.py:47
  36.3 0.5 collective-permute-start.24
  36.8 1.6 %collective-permute-done.26 = f32[72,128]{1,0:T(8,128)S(1)} collective-permute-done((f32[72,128]{1,0:T(8,128)S(1)}, f32[72,128]{1,0:T(8,128)S(1)}, u32[]{:S(2)}, u32[]{:S(2)}) %collective-permute-start.26) | collective-permute-done | bytes 36896 | tf_op jit(solution)/shard_map/ppermute | solution.py:47
  38.4 1.3 %collective-permute-done.25 = f32[72,128]{1,0:T(8,128)S(1)} collective-permute-done((f32[72,128]{1,0:T(8,128)S(1)}, f32[72,128]{1,0:T(8,128)S(1)}, u32[]{:S(2)}, u32[]{:S(2)}) %collective-permute-start.25) | collective-permute-done | bytes 36896 | tf_op jit(solution)/shard_map/ppermute | solution.py:47
  40.3 1.2 %collective-permute-done.27 = f32[72,128]{1,0:T(8,128)S(1)} collective-permute-done((f32[72,128]{1,0:T(8,128)S(1)}, f32[72,128]{1,0:T(8,128)S(1)}, u32[]{:S(2)}, u32[]{:S(2)}) %collective-permute-start.27) | collective-permute-done | bytes 36896 | tf_op jit(solution)/shard_map/ppermute | solution.py:47
  41.5 19.7 %shard_map.49 = (f32[64,128]{1,0:T(8,128)S(1)}, f32[128,64]{1,0:T(8,128)S(1)}, f32[8,128]{1,0:T(8,128)S(1)}, f32[8,64]{1,0:T(8,128)S(1)}) custom-call(f8e4m3fn[128,64,2048]{2,1,0:T(32,128)(4,1)S(1)} %get-tuple-element.45.refs_0_, f32[64,64]{1,0:T(8,128)S(1)} %copy-done.1, f32[64,128]{1,0:T(8,128)S(1)} %bitcast.10, f32[72,128]{1,0:T(8,128)S(1)} %add.132.refs_3_, ...), custom_call_target="tpu_custom_call" | custom-call | flops 17179869184 | bytes 67108864 | tf_op jit(solution)/shard_map/pallas_call | solution.py:266
  61.2 1.5 %collective-permute-start.30 = (f32[64,128]{1,0:T(8,128)S(1)}, f32[64,128]{1,0:T(8,128)S(1)}, u32[]{:S(2)}, u32[]{:S(2)}) collective-permute-start(f32[64,128]{1,0:T(8,128)S(1)} %get-tuple-element.50), channel_id=1, source_target_pairs={{0,3},{1,2},{2,1},{3,0},{4,7},{5,6},{6,5},{7,4},{8,11},{9,10},{10,... | collective-permute-start | bytes 98312 | tf_op jit(solution)/shard_map/ppermute | solution.py:47
  62.7 0.6 collective-permute-start.29
  63.3 2.3 %collective-permute-start.28 = (f32[64,128]{1,0:T(8,128)S(1)}, f32[64,128]{1,0:T(8,128)S(1)}, u32[]{:S(2)}, u32[]{:S(2)}) collective-permute-start(f32[64,128]{1,0:T(8,128)S(1)} %get-tuple-element.50), channel_id=1, source_target_pairs={{0,1},{1,0},{2,3},{3,2},{4,5},{5,4},{6,7},{7,6},{8,9},{9,8},{10,11... | collective-permute-start | bytes 98312 | tf_op jit(solution)/shard_map/ppermute | solution.py:47
  65.6 1.6 %collective-permute-done.30 = f32[64,128]{1,0:T(8,128)S(1)} collective-permute-done((f32[64,128]{1,0:T(8,128)S(1)}, f32[64,128]{1,0:T(8,128)S(1)}, u32[]{:S(2)}, u32[]{:S(2)}) %collective-permute-start.30) | collective-permute-done | bytes 32800 | tf_op jit(solution)/shard_map/ppermute | solution.py:47
  67.9 1.6 %collective-permute-start.33 = (f32[64,128]{1,0:T(8,128)S(1)}, f32[64,128]{1,0:T(8,128)S(1)}, u32[]{:S(2)}, u32[]{:S(2)}) collective-permute-start(f32[64,128]{1,0:T(8,128)S(1)} %add_add_fusion.11), channel_id=1, source_target_pairs={{0,24},{4,28},{8,16},{12,20},{16,8},{20,12},{24,0},{28,4},{1,25},{... | collective-permute-start | bytes 98312 | tf_op jit(solution)/shard_map/ppermute | solution.py:47
  70.0 1.5 %collective-permute-start.31 = (f32[64,128]{1,0:T(8,128)S(1)}, f32[64,128]{1,0:T(8,128)S(1)}, u32[]{:S(2)}, u32[]{:S(2)}) collective-permute-start(f32[64,128]{1,0:T(8,128)S(1)} %add_add_fusion.11), channel_id=1, source_target_pairs={{0,8},{4,12},{8,0},{12,4},{16,24},{20,28},{24,16},{28,20},{1,9},{5... | collective-permute-start | bytes 98312 | tf_op jit(solution)/shard_map/ppermute | solution.py:47
  71.5 1.5 %collective-permute-done.33 = f32[64,128]{1,0:T(8,128)S(1)} collective-permute-done((f32[64,128]{1,0:T(8,128)S(1)}, f32[64,128]{1,0:T(8,128)S(1)}, u32[]{:S(2)}, u32[]{:S(2)}) %collective-permute-start.33) | collective-permute-done | bytes 32800 | tf_op jit(solution)/shard_map/ppermute | solution.py:47
  73.4 0.5 collective-permute-done.31
  74.0 1.2 %collective-permute-done.34 = f32[64,128]{1,0:T(8,128)S(1)} collective-permute-done((f32[64,128]{1,0:T(8,128)S(1)}, f32[64,128]{1,0:T(8,128)S(1)}, u32[]{:S(2)}, u32[]{:S(2)}) %collective-permute-start.34) | collective-permute-done | bytes 32800 | tf_op jit(solution)/shard_map/ppermute | solution.py:47
  75.2 19.6 %shard_map.50 = (f32[64,128]{1,0:T(8,128)S(1)}, f32[128,64]{1,0:T(8,128)S(1)}, f32[8,128]{1,0:T(8,128)S(1)}) custom-call(f8e4m3fn[128,64,2048]{2,1,0:T(32,128)(4,1)S(1)} %get-tuple-element.45.refs_0_, f32[64,64]{1,0:T(8,128)S(1)} %copy-done.1, f32[128,64]{1,0:T(8,128)S(1)} %get-tuple-element.49.refs_2_, f32[64,128]{1,0:T(8,128)S(1)} %add.139.refs_3_, ...), custom_call_target="tpu_custom_call" | custom-call | flops 17179869184 | bytes 67108864 | tf_op jit(solution)/shard_map/pallas_call | solution.py:266
  94.8 2.3 %collective-permute-start.37 = (f32[64,128]{1,0:T(8,128)S(1)}, f32[64,128]{1,0:T(8,128)S(1)}, u32[]{:S(2)}, u32[]{:S(2)}) collective-permute-start(f32[64,128]{1,0:T(8,128)S(1)} %get-tuple-element.54), channel_id=1, source_target_pairs={{0,3},{1,2},{2,1},{3,0},{4,7},{5,6},{6,5},{7,4},{8,11},{9,10},{10,... | collective-permute-start | bytes 98312 | tf_op jit(solution)/shard_map/ppermute | solution.py:47
  97.1 0.8 collective-permute-start.36
  97.9 1.3 %collective-permute-start.35 = (f32[64,128]{1,0:T(8,128)S(1)}, f32[64,128]{1,0:T(8,128)S(1)}, u32[]{:S(2)}, u32[]{:S(2)}) collective-permute-start(f32[64,128]{1,0:T(8,128)S(1)} %get-tuple-element.54), channel_id=1, source_target_pairs={{0,1},{1,0},{2,3},{3,2},{4,5},{5,4},{6,7},{7,6},{8,9},{9,8},{10,11... | collective-permute-start | bytes 98312 | tf_op jit(solution)/shard_map/ppermute | solution.py:47
  99.2 1.5 %collective-permute-done.37 = f32[64,128]{1,0:T(8,128)S(1)} collective-permute-done((f32[64,128]{1,0:T(8,128)S(1)}, f32[64,128]{1,0:T(8,128)S(1)}, u32[]{:S(2)}, u32[]{:S(2)}) %collective-permute-start.37) | collective-permute-done | bytes 32800 | tf_op jit(solution)/shard_map/ppermute | solution.py:47
  100.6 1.3 %collective-permute-done.36 = f32[64,128]{1,0:T(8,128)S(1)} collective-permute-done((f32[64,128]{1,0:T(8,128)S(1)}, f32[64,128]{1,0:T(8,128)S(1)}, u32[]{:S(2)}, u32[]{:S(2)}) %collective-permute-start.36) | collective-permute-done | bytes 32800 | tf_op jit(solution)/shard_map/ppermute | solution.py:47
  102.2 2.5 %collective-permute-start.40 = (f32[64,128]{1,0:T(8,128)S(1)}, f32[64,128]{1,0:T(8,128)S(1)}, u32[]{:S(2)}, u32[]{:S(2)}) collective-permute-start(f32[64,128]{1,0:T(8,128)S(1)} %add_add_fusion.9), channel_id=1, source_target_pairs={{0,24},{4,28},{8,16},{12,20},{16,8},{20,12},{24,0},{28,4},{1,25},{... | collective-permute-start | bytes 98312 | tf_op jit(solution)/shard_map/ppermute | solution.py:47
  105.2 0.5 collective-permute-start.38
  105.7 1.3 %collective-permute-done.40 = f32[64,128]{1,0:T(8,128)S(1)} collective-permute-done((f32[64,128]{1,0:T(8,128)S(1)}, f32[64,128]{1,0:T(8,128)S(1)}, u32[]{:S(2)}, u32[]{:S(2)}) %collective-permute-start.40) | collective-permute-done | bytes 32800 | tf_op jit(solution)/shard_map/ppermute | solution.py:47
  107.0 1.5 %collective-permute-done.39 = f32[64,128]{1,0:T(8,128)S(1)} collective-permute-done((f32[64,128]{1,0:T(8,128)S(1)}, f32[64,128]{1,0:T(8,128)S(1)}, u32[]{:S(2)}, u32[]{:S(2)}) %collective-permute-start.39) | collective-permute-done | bytes 32800 | tf_op jit(solution)/shard_map/ppermute | solution.py:47
  109.2 1.2 %collective-permute-done.41 = f32[64,128]{1,0:T(8,128)S(1)} collective-permute-done((f32[64,128]{1,0:T(8,128)S(1)}, f32[64,128]{1,0:T(8,128)S(1)}, u32[]{:S(2)}, u32[]{:S(2)}) %collective-permute-start.41) | collective-permute-done | bytes 32800 | tf_op jit(solution)/shard_map/ppermute | solution.py:47
  110.4 0.9 shard_map.51
  (30 shorter events, 4.3 us)
Async XLA Ops:
  0.0 41.5 %copy-start.1 = (f32[64,64]{1,0:T(8,128)S(1)}, f32[64,64]{1,0:T(8,128)}, u32[]{:S(2)}) copy-start(f32[64,64]{1,0:T(8,128)} %refs_1_.5) | copy-start | bytes 49156
  0.0 41.5 %copy-start.2 = (f32[128,64]{0,1:T(8,128)S(1)}, f32[128,64]{0,1:T(8,128)}, u32[]{:S(2)}) copy-start(f32[128,64]{0,1:T(8,128)} %param.7) | copy-start | bytes 98308
  23.2 88.7 %copy-start = (f32[2048,64]{0,1:T(8,128)S(1)}, f32[2048,64]{0,1:T(8,128)}, u32[]{:S(2)}) copy-start(f32[2048,64]{0,1:T(8,128)} %param.8) | copy-start | bytes 1572868
  23.2 7.1 %collective-permute-start.23 = (f32[72,128]{1,0:T(8,128)S(1)}, f32[72,128]{1,0:T(8,128)S(1)}, u32[]{:S(2)}, u32[]{:S(2)}) collective-permute-start(f32[72,128]{1,0:T(8,128)S(1)} %get-tuple-element.46), channel_id=1, source_target_pairs={{0,3},{1,2},{2,1},{3,0},{4,7},{5,6},{6,5},{7,4},{8,11},{9,10},{10,... | collective-permute-start | bytes 110600 | tf_op jit(solution)/shard_map/ppermute | solution.py:47
  28.4 4.9 %collective-permute-start.22 = (f32[72,128]{1,0:T(8,128)S(1)}, f32[72,128]{1,0:T(8,128)S(1)}, u32[]{:S(2)}, u32[]{:S(2)}) collective-permute-start(f32[72,128]{1,0:T(8,128)S(1)} %get-tuple-element.46), channel_id=1, source_target_pairs={{0,2},{1,3},{2,0},{3,1},{4,6},{5,7},{6,4},{7,5},{8,10},{9,11},{10,... | collective-permute-start | bytes 110600 | tf_op jit(solution)/shard_map/ppermute | solution.py:47
  28.4 4.9 %collective-permute-start.21 = (f32[72,128]{1,0:T(8,128)S(1)}, f32[72,128]{1,0:T(8,128)S(1)}, u32[]{:S(2)}, u32[]{:S(2)}) collective-permute-start(f32[72,128]{1,0:T(8,128)S(1)} %get-tuple-element.46), channel_id=1, source_target_pairs={{0,1},{1,0},{2,3},{3,2},{4,5},{5,4},{6,7},{7,6},{8,9},{9,8},{10,11... | collective-permute-start | bytes 110600 | tf_op jit(solution)/shard_map/ppermute | solution.py:47
  33.2 5.2 %collective-permute-start.26 = (f32[72,128]{1,0:T(8,128)S(1)}, f32[72,128]{1,0:T(8,128)S(1)}, u32[]{:S(2)}, u32[]{:S(2)}) collective-permute-start(f32[72,128]{1,0:T(8,128)S(1)} %add_add_fusion.7), channel_id=1, source_target_pairs={{0,24},{4,28},{8,16},{12,20},{16,8},{20,12},{24,0},{28,4},{1,25},{... | collective-permute-start | bytes 110600 | tf_op jit(solution)/shard_map/ppermute | solution.py:47
  35.7 4.0 %collective-permute-start.25 = (f32[72,128]{1,0:T(8,128)S(1)}, f32[72,128]{1,0:T(8,128)S(1)}, u32[]{:S(2)}, u32[]{:S(2)}) collective-permute-start(f32[72,128]{1,0:T(8,128)S(1)} %add_add_fusion.7), channel_id=1, source_target_pairs={{0,16},{4,20},{8,24},{12,28},{16,0},{20,4},{24,8},{28,12},{1,17},{... | collective-permute-start | bytes 110600 | tf_op jit(solution)/shard_map/ppermute | solution.py:47
  36.3 4.0 %collective-permute-start.24 = (f32[72,128]{1,0:T(8,128)S(1)}, f32[72,128]{1,0:T(8,128)S(1)}, u32[]{:S(2)}, u32[]{:S(2)}) collective-permute-start(f32[72,128]{1,0:T(8,128)S(1)} %add_add_fusion.7), channel_id=1, source_target_pairs={{0,8},{4,12},{8,0},{12,4},{16,24},{20,28},{24,16},{28,20},{1,9},{5... | collective-permute-start | bytes 110600 | tf_op jit(solution)/shard_map/ppermute | solution.py:47
  40.2 1.3 %collective-permute-start.27 = (f32[72,128]{1,0:T(8,128)S(1)}, f32[72,128]{1,0:T(8,128)S(1)}, u32[]{:S(2)}, u32[]{:S(2)}) collective-permute-start(f32[72,128]{1,0:T(8,128)S(1)} %add_add_fusion.6), channel_id=1, source_target_pairs={{0,4},{4,0},{8,12},{12,8},{16,20},{20,16},{24,28},{28,24},{1,5},{5... | collective-permute-start | bytes 110600 | tf_op jit(solution)/shard_map/ppermute | solution.py:47
  61.2 6.0 %collective-permute-start.30 = (f32[64,128]{1,0:T(8,128)S(1)}, f32[64,128]{1,0:T(8,128)S(1)}, u32[]{:S(2)}, u32[]{:S(2)}) collective-permute-start(f32[64,128]{1,0:T(8,128)S(1)} %get-tuple-element.50), channel_id=1, source_target_pairs={{0,3},{1,2},{2,1},{3,0},{4,7},{5,6},{6,5},{7,4},{8,11},{9,10},{10,... | collective-permute-start | bytes 98312 | tf_op jit(solution)/shard_map/ppermute | solution.py:47
  62.7 5.0 %collective-permute-start.29 = (f32[64,128]{1,0:T(8,128)S(1)}, f32[64,128]{1,0:T(8,128)S(1)}, u32[]{:S(2)}, u32[]{:S(2)}) collective-permute-start(f32[64,128]{1,0:T(8,128)S(1)} %get-tuple-element.50), channel_id=1, source_target_pairs={{0,2},{1,3},{2,0},{3,1},{4,6},{5,7},{6,4},{7,5},{8,10},{9,11},{10,... | collective-permute-start | bytes 98312 | tf_op jit(solution)/shard_map/ppermute | solution.py:47
  63.3 4.6 %collective-permute-start.28 = (f32[64,128]{1,0:T(8,128)S(1)}, f32[64,128]{1,0:T(8,128)S(1)}, u32[]{:S(2)}, u32[]{:S(2)}) collective-permute-start(f32[64,128]{1,0:T(8,128)S(1)} %get-tuple-element.50), channel_id=1, source_target_pairs={{0,1},{1,0},{2,3},{3,2},{4,5},{5,4},{6,7},{7,6},{8,9},{9,8},{10,11... | collective-permute-start | bytes 98312 | tf_op jit(solution)/shard_map/ppermute | solution.py:47
  67.9 5.1 %collective-permute-start.33 = (f32[64,128]{1,0:T(8,128)S(1)}, f32[64,128]{1,0:T(8,128)S(1)}, u32[]{:S(2)}, u32[]{:S(2)}) collective-permute-start(f32[64,128]{1,0:T(8,128)S(1)} %add_add_fusion.11), channel_id=1, source_target_pairs={{0,24},{4,28},{8,16},{12,20},{16,8},{20,12},{24,0},{28,4},{1,25},{... | collective-permute-start | bytes 98312 | tf_op jit(solution)/shard_map/ppermute | solution.py:47
  69.5 3.9 %collective-permute-start.32 = (f32[64,128]{1,0:T(8,128)S(1)}, f32[64,128]{1,0:T(8,128)S(1)}, u32[]{:S(2)}, u32[]{:S(2)}) collective-permute-start(f32[64,128]{1,0:T(8,128)S(1)} %add_add_fusion.11), channel_id=1, source_target_pairs={{0,16},{4,20},{8,24},{12,28},{16,0},{20,4},{24,8},{28,12},{1,17},{... | collective-permute-start | bytes 98312 | tf_op jit(solution)/shard_map/ppermute | solution.py:47
  70.0 3.9 %collective-permute-start.31 = (f32[64,128]{1,0:T(8,128)S(1)}, f32[64,128]{1,0:T(8,128)S(1)}, u32[]{:S(2)}, u32[]{:S(2)}) collective-permute-start(f32[64,128]{1,0:T(8,128)S(1)} %add_add_fusion.11), channel_id=1, source_target_pairs={{0,8},{4,12},{8,0},{12,4},{16,24},{20,28},{24,16},{28,20},{1,9},{5... | collective-permute-start | bytes 98312 | tf_op jit(solution)/shard_map/ppermute | solution.py:47
  73.9 1.3 %collective-permute-start.34 = (f32[64,128]{1,0:T(8,128)S(1)}, f32[64,128]{1,0:T(8,128)S(1)}, u32[]{:S(2)}, u32[]{:S(2)}) collective-permute-start(f32[64,128]{1,0:T(8,128)S(1)} %add_add_fusion.10), channel_id=1, source_target_pairs={{0,4},{4,0},{8,12},{12,8},{16,20},{20,16},{24,28},{28,24},{1,5},{5... | collective-permute-start | bytes 98312 | tf_op jit(solution)/shard_map/ppermute | solution.py:47
  94.8 5.8 %collective-permute-start.37 = (f32[64,128]{1,0:T(8,128)S(1)}, f32[64,128]{1,0:T(8,128)S(1)}, u32[]{:S(2)}, u32[]{:S(2)}) collective-permute-start(f32[64,128]{1,0:T(8,128)S(1)} %get-tuple-element.54), channel_id=1, source_target_pairs={{0,3},{1,2},{2,1},{3,0},{4,7},{5,6},{6,5},{7,4},{8,11},{9,10},{10,... | collective-permute-start | bytes 98312 | tf_op jit(solution)/shard_map/ppermute | solution.py:47
  97.1 4.9 %collective-permute-start.36 = (f32[64,128]{1,0:T(8,128)S(1)}, f32[64,128]{1,0:T(8,128)S(1)}, u32[]{:S(2)}, u32[]{:S(2)}) collective-permute-start(f32[64,128]{1,0:T(8,128)S(1)} %get-tuple-element.54), channel_id=1, source_target_pairs={{0,2},{1,3},{2,0},{3,1},{4,6},{5,7},{6,4},{7,5},{8,10},{9,11},{10,... | collective-permute-start | bytes 98312 | tf_op jit(solution)/shard_map/ppermute | solution.py:47
  97.9 4.3 %collective-permute-start.35 = (f32[64,128]{1,0:T(8,128)S(1)}, f32[64,128]{1,0:T(8,128)S(1)}, u32[]{:S(2)}, u32[]{:S(2)}) collective-permute-start(f32[64,128]{1,0:T(8,128)S(1)} %get-tuple-element.54), channel_id=1, source_target_pairs={{0,1},{1,0},{2,3},{3,2},{4,5},{5,4},{6,7},{7,6},{8,9},{9,8},{10,11... | collective-permute-start | bytes 98312 | tf_op jit(solution)/shard_map/ppermute | solution.py:47
  102.2 4.9 %collective-permute-start.40 = (f32[64,128]{1,0:T(8,128)S(1)}, f32[64,128]{1,0:T(8,128)S(1)}, u32[]{:S(2)}, u32[]{:S(2)}) collective-permute-start(f32[64,128]{1,0:T(8,128)S(1)} %add_add_fusion.9), channel_id=1, source_target_pairs={{0,24},{4,28},{8,16},{12,20},{16,8},{20,12},{24,0},{28,4},{1,25},{... | collective-permute-start | bytes 98312 | tf_op jit(solution)/shard_map/ppermute | solution.py:47
  104.7 3.9 %collective-permute-start.39 = (f32[64,128]{1,0:T(8,128)S(1)}, f32[64,128]{1,0:T(8,128)S(1)}, u32[]{:S(2)}, u32[]{:S(2)}) collective-permute-start(f32[64,128]{1,0:T(8,128)S(1)} %add_add_fusion.9), channel_id=1, source_target_pairs={{0,16},{4,20},{8,24},{12,28},{16,0},{20,4},{24,8},{28,12},{1,17},{... | collective-permute-start | bytes 98312 | tf_op jit(solution)/shard_map/ppermute | solution.py:47
  105.2 3.9 %collective-permute-start.38 = (f32[64,128]{1,0:T(8,128)S(1)}, f32[64,128]{1,0:T(8,128)S(1)}, u32[]{:S(2)}, u32[]{:S(2)}) collective-permute-start(f32[64,128]{1,0:T(8,128)S(1)} %add_add_fusion.9), channel_id=1, source_target_pairs={{0,8},{4,12},{8,0},{12,4},{16,24},{20,28},{24,16},{28,20},{1,9},{5... | collective-permute-start | bytes 98312 | tf_op jit(solution)/shard_map/ppermute | solution.py:47
  109.1 1.3 %collective-permute-start.41 = (f32[64,128]{1,0:T(8,128)S(1)}, f32[64,128]{1,0:T(8,128)S(1)}, u32[]{:S(2)}, u32[]{:S(2)}) collective-permute-start(f32[64,128]{1,0:T(8,128)S(1)} %add_add_fusion.8), channel_id=1, source_target_pairs={{0,4},{4,0},{8,12},{12,8},{16,20},{20,16},{24,28},{28,24},{1,5},{5... | collective-permute-start | bytes 98312 | tf_op jit(solution)/shard_map/ppermute | solution.py:47

commit v8 on v7

--- a/solution.py
+++ b/solution.py
@@ -14,7 +14,7 @@
 COLUMNS = 256
 GROUP = 4
 MOST = 7.0
-ROUNDING = 5.6e-6
+ROUNDING = 9.2e-6
 ALLOWED = 6.4e-9
 F32, BF16 = jnp.float32, jnp.bfloat16
 SMALL = jnp.float8_e4m3fn
@@ -195,11 +195,13 @@
                         count = count.astype(BF16)
                     else:
                         count = counts[start + n, :, at].astype(BF16)
+                    if not exact:
+                        model = model.astype(BF16)
                     inverse = pltpu.reciprocal(model, approx=True, full_range=False)
                     if exact:
                         parts = split(count.astype(F32) * inverse)
                     else:
-                        parts = (count * inverse.astype(BF16),)
+                        parts = (count * inverse,)
                     lagging.append((chunk, n, parts))
                     if len(lagging) > LAG:
                         add_phi()

time: 112 us -> 112 us (level)
  no operation moved by 1% of the time
where the time goes in v8:
time: 112 us
  Pallas kernels  62.9 us (56%)
  starting transfers between devices  25.4 us (23%)
  waiting for transfers between devices  22.3 us (20%)
    pallas_call x3, Pallas kernels, sweep(): pl.pallas_call(functools.partial(sweep_kernel, iteration, exact, axes, na...  62 us
    ppermute x21, starting transfers between devices, sum_over(): parts.append(lax.ppermute(x, axis, partners))  25.4 us
    ppermute x21, waiting for transfers between devices, sum_over(): parts.append(lax.ppermute(x, axis, partners))  22.3 us
  transfers between devices with their start and end apart: 21, of which 20 were waited for; matrix products, arithmetic and copies ran while one was open for 0% of the time, Pallas kernels for 0%

profile of v8, /device:TPU:0, one launch (start us, length us, event | category | flops | bytes accessed | tf_op | source)
XLA Modules:
  0.0 111.9 jit_solution(9123909826079304380)
XLA Ops:
  0.0 23.3 %shard_map.48 = (f32[72,128]{1,0:T(8,128)S(1)}, bf16[256,2048]{1,0:T(8,128)(2,1)S(1)}, bf16[2048,256]{1,0:T(8,128)(2,1)S(1)}, f8e4m3fn[128,64,2048]{2,1,0:T(32,128)(4,1)S(1)}) custom-call(s32[128,64,2048]{2,1,0:T(8,128)} %refs_0_.1, f32[64,64]{1,0:T(8,128)} %refs_1_.5, f32[64,128]{1,0:T(8,128)} %bitcast.9, f32[64,2048]{1,0:T(8,128)} %bitcast.7), custom_call_target="tpu_custom_call" | custom-call | flops 17179869184 | bytes 67108864 | tf_op jit(solution)/shard_map/pallas_call | solution.py:268
  23.3 5.1 %collective-permute-start.23 = (f32[72,128]{1,0:T(8,128)S(1)}, f32[72,128]{1,0:T(8,128)S(1)}, u32[]{:S(2)}, u32[]{:S(2)}) collective-permute-start(f32[72,128]{1,0:T(8,128)S(1)} %get-tuple-element.46), channel_id=1, source_target_pairs={{0,3},{1,2},{2,1},{3,0},{4,7},{5,6},{6,5},{7,4},{8,11},{9,10},{10,... | collective-permute-start | bytes 110600 | tf_op jit(solution)/shard_map/ppermute | solution.py:47
  28.4 0.6 collective-permute-start.21
  29.1 1.3 %collective-permute-done.23 = f32[72,128]{1,0:T(8,128)S(1)} collective-permute-done((f32[72,128]{1,0:T(8,128)S(1)}, f32[72,128]{1,0:T(8,128)S(1)}, u32[]{:S(2)}, u32[]{:S(2)}) %collective-permute-start.23) | collective-permute-done | bytes 36896 | tf_op jit(solution)/shard_map/ppermute | solution.py:47
  30.4 2.9 %collective-permute-done.22 = f32[72,128]{1,0:T(8,128)S(1)} collective-permute-done((f32[72,128]{1,0:T(8,128)S(1)}, f32[72,128]{1,0:T(8,128)S(1)}, u32[]{:S(2)}, u32[]{:S(2)}) %collective-permute-start.22) | collective-permute-done | bytes 36896 | tf_op jit(solution)/shard_map/ppermute | solution.py:47
  33.3 2.5 %collective-permute-start.26 = (f32[72,128]{1,0:T(8,128)S(1)}, f32[72,128]{1,0:T(8,128)S(1)}, u32[]{:S(2)}, u32[]{:S(2)}) collective-permute-start(f32[72,128]{1,0:T(8,128)S(1)} %add_add_fusion.7), channel_id=1, source_target_pairs={{0,24},{4,28},{8,16},{12,20},{16,8},{20,12},{24,0},{28,4},{1,25},{... | collective-permute-start | bytes 110600 | tf_op jit(solution)/shard_map/ppermute | solution.py:47
  36.3 0.5 collective-permute-start.24
  36.9 1.6 %collective-permute-done.26 = f32[72,128]{1,0:T(8,128)S(1)} collective-permute-done((f32[72,128]{1,0:T(8,128)S(1)}, f32[72,128]{1,0:T(8,128)S(1)}, u32[]{:S(2)}, u32[]{:S(2)}) %collective-permute-start.26) | collective-permute-done | bytes 36896 | tf_op jit(solution)/shard_map/ppermute | solution.py:47
  38.5 1.3 %collective-permute-done.25 = f32[72,128]{1,0:T(8,128)S(1)} collective-permute-done((f32[72,128]{1,0:T(8,128)S(1)}, f32[72,128]{1,0:T(8,128)S(1)}, u32[]{:S(2)}, u32[]{:S(2)}) %collective-permute-start.25) | collective-permute-done | bytes 36896 | tf_op jit(solution)/shard_map/ppermute | solution.py:47
  40.4 1.2 %collective-permute-done.27 = f32[72,128]{1,0:T(8,128)S(1)} collective-permute-done((f32[72,128]{1,0:T(8,128)S(1)}, f32[72,128]{1,0:T(8,128)S(1)}, u32[]{:S(2)}, u32[]{:S(2)}) %collective-permute-start.27) | collective-permute-done | bytes 36896 | tf_op jit(solution)/shard_map/ppermute | solution.py:47
  41.6 19.4 %shard_map.49 = (f32[64,128]{1,0:T(8,128)S(1)}, f32[128,64]{1,0:T(8,128)S(1)}, f32[8,128]{1,0:T(8,128)S(1)}, f32[8,64]{1,0:T(8,128)S(1)}) custom-call(f8e4m3fn[128,64,2048]{2,1,0:T(32,128)(4,1)S(1)} %get-tuple-element.45.refs_0_, f32[64,64]{1,0:T(8,128)S(1)} %copy-done.1, f32[64,128]{1,0:T(8,128)S(1)} %bitcast.10, f32[72,128]{1,0:T(8,128)S(1)} %add.132.refs_3_, ...), custom_call_target="tpu_custom_call" | custom-call | flops 17179869184 | bytes 67108864 | tf_op jit(solution)/shard_map/pallas_call | solution.py:268
  61.0 1.5 %collective-permute-start.30 = (f32[64,128]{1,0:T(8,128)S(1)}, f32[64,128]{1,0:T(8,128)S(1)}, u32[]{:S(2)}, u32[]{:S(2)}) collective-permute-start(f32[64,128]{1,0:T(8,128)S(1)} %get-tuple-element.50), channel_id=1, source_target_pairs={{0,3},{1,2},{2,1},{3,0},{4,7},{5,6},{6,5},{7,4},{8,11},{9,10},{10,... | collective-permute-start | bytes 98312 | tf_op jit(solution)/shard_map/ppermute | solution.py:47
  62.5 0.6 collective-permute-start.29
  63.1 2.3 %collective-permute-start.28 = (f32[64,128]{1,0:T(8,128)S(1)}, f32[64,128]{1,0:T(8,128)S(1)}, u32[]{:S(2)}, u32[]{:S(2)}) collective-permute-start(f32[64,128]{1,0:T(8,128)S(1)} %get-tuple-element.50), channel_id=1, source_target_pairs={{0,1},{1,0},{2,3},{3,2},{4,5},{5,4},{6,7},{7,6},{8,9},{9,8},{10,11... | collective-permute-start | bytes 98312 | tf_op jit(solution)/shard_map/ppermute | solution.py:47
  65.4 1.6 %collective-permute-done.30 = f32[64,128]{1,0:T(8,128)S(1)} collective-permute-done((f32[64,128]{1,0:T(8,128)S(1)}, f32[64,128]{1,0:T(8,128)S(1)}, u32[]{:S(2)}, u32[]{:S(2)}) %collective-permute-start.30) | collective-permute-done | bytes 32800 | tf_op jit(solution)/shard_map/ppermute | solution.py:47
  67.7 1.6 %collective-permute-start.33 = (f32[64,128]{1,0:T(8,128)S(1)}, f32[64,128]{1,0:T(8,128)S(1)}, u32[]{:S(2)}, u32[]{:S(2)}) collective-permute-start(f32[64,128]{1,0:T(8,128)S(1)} %add_add_fusion.11), channel_id=1, source_target_pairs={{0,24},{4,28},{8,16},{12,20},{16,8},{20,12},{24,0},{28,4},{1,25},{... | collective-permute-start | bytes 98312 | tf_op jit(solution)/shard_map/ppermute | solution.py:47
  69.2 0.5 collective-permute-start.32
  69.8 1.5 %collective-permute-start.31 = (f32[64,128]{1,0:T(8,128)S(1)}, f32[64,128]{1,0:T(8,128)S(1)}, u32[]{:S(2)}, u32[]{:S(2)}) collective-permute-start(f32[64,128]{1,0:T(8,128)S(1)} %add_add_fusion.11), channel_id=1, source_target_pairs={{0,8},{4,12},{8,0},{12,4},{16,24},{20,28},{24,16},{28,20},{1,9},{5... | collective-permute-start | bytes 98312 | tf_op jit(solution)/shard_map/ppermute | solution.py:47
  71.2 1.5 %collective-permute-done.33 = f32[64,128]{1,0:T(8,128)S(1)} collective-permute-done((f32[64,128]{1,0:T(8,128)S(1)}, f32[64,128]{1,0:T(8,128)S(1)}, u32[]{:S(2)}, u32[]{:S(2)}) %collective-permute-start.33) | collective-permute-done | bytes 32800 | tf_op jit(solution)/shard_map/ppermute | solution.py:47
  73.8 1.2 %collective-permute-done.34 = f32[64,128]{1,0:T(8,128)S(1)} collective-permute-done((f32[64,128]{1,0:T(8,128)S(1)}, f32[64,128]{1,0:T(8,128)S(1)}, u32[]{:S(2)}, u32[]{:S(2)}) %collective-permute-start.34) | collective-permute-done | bytes 32800 | tf_op jit(solution)/shard_map/ppermute | solution.py:47
  75.0 19.3 %shard_map.50 = (f32[64,128]{1,0:T(8,128)S(1)}, f32[128,64]{1,0:T(8,128)S(1)}, f32[8,128]{1,0:T(8,128)S(1)}) custom-call(f8e4m3fn[128,64,2048]{2,1,0:T(32,128)(4,1)S(1)} %get-tuple-element.45.refs_0_, f32[64,64]{1,0:T(8,128)S(1)} %copy-done.1, f32[128,64]{1,0:T(8,128)S(1)} %get-tuple-element.49.refs_2_, f32[64,128]{1,0:T(8,128)S(1)} %add.139.refs_3_, ...), custom_call_target="tpu_custom_call" | custom-call | flops 17179869184 | bytes 67108864 | tf_op jit(solution)/shard_map/pallas_call | solution.py:268
  94.3 2.3 %collective-permute-start.37 = (f32[64,128]{1,0:T(8,128)S(1)}, f32[64,128]{1,0:T(8,128)S(1)}, u32[]{:S(2)}, u32[]{:S(2)}) collective-permute-start(f32[64,128]{1,0:T(8,128)S(1)} %get-tuple-element.54), channel_id=1, source_target_pairs={{0,3},{1,2},{2,1},{3,0},{4,7},{5,6},{6,5},{7,4},{8,11},{9,10},{10,... | collective-permute-start | bytes 98312 | tf_op jit(solution)/shard_map/ppermute | solution.py:47
  96.6 0.8 collective-permute-start.36
  97.4 1.3 %collective-permute-start.35 = (f32[64,128]{1,0:T(8,128)S(1)}, f32[64,128]{1,0:T(8,128)S(1)}, u32[]{:S(2)}, u32[]{:S(2)}) collective-permute-start(f32[64,128]{1,0:T(8,128)S(1)} %get-tuple-element.54), channel_id=1, source_target_pairs={{0,1},{1,0},{2,3},{3,2},{4,5},{5,4},{6,7},{7,6},{8,9},{9,8},{10,11... | collective-permute-start | bytes 98312 | tf_op jit(solution)/shard_map/ppermute | solution.py:47
  98.7 1.4 %collective-permute-done.37 = f32[64,128]{1,0:T(8,128)S(1)} collective-permute-done((f32[64,128]{1,0:T(8,128)S(1)}, f32[64,128]{1,0:T(8,128)S(1)}, u32[]{:S(2)}, u32[]{:S(2)}) %collective-permute-start.37) | collective-permute-done | bytes 32800 | tf_op jit(solution)/shard_map/ppermute | solution.py:47
  100.1 1.3 %collective-permute-done.36 = f32[64,128]{1,0:T(8,128)S(1)} collective-permute-done((f32[64,128]{1,0:T(8,128)S(1)}, f32[64,128]{1,0:T(8,128)S(1)}, u32[]{:S(2)}, u32[]{:S(2)}) %collective-permute-start.36) | collective-permute-done | bytes 32800 | tf_op jit(solution)/shard_map/ppermute | solution.py:47
  101.7 2.5 %collective-permute-start.40 = (f32[64,128]{1,0:T(8,128)S(1)}, f32[64,128]{1,0:T(8,128)S(1)}, u32[]{:S(2)}, u32[]{:S(2)}) collective-permute-start(f32[64,128]{1,0:T(8,128)S(1)} %add_add_fusion.9), channel_id=1, source_target_pairs={{0,24},{4,28},{8,16},{12,20},{16,8},{20,12},{24,0},{28,4},{1,25},{... | collective-permute-start | bytes 98312 | tf_op jit(solution)/shard_map/ppermute | solution.py:47
  104.7 0.5 collective-permute-start.38
  105.2 1.3 %collective-permute-done.40 = f32[64,128]{1,0:T(8,128)S(1)} collective-permute-done((f32[64,128]{1,0:T(8,128)S(1)}, f32[64,128]{1,0:T(8,128)S(1)}, u32[]{:S(2)}, u32[]{:S(2)}) %collective-permute-start.40) | collective-permute-done | bytes 32800 | tf_op jit(solution)/shard_map/ppermute | solution.py:47
  106.6 1.5 %collective-permute-done.39 = f32[64,128]{1,0:T(8,128)S(1)} collective-permute-done((f32[64,128]{1,0:T(8,128)S(1)}, f32[64,128]{1,0:T(8,128)S(1)}, u32[]{:S(2)}, u32[]{:S(2)}) %collective-permute-start.39) | collective-permute-done | bytes 32800 | tf_op jit(solution)/shard_map/ppermute | solution.py:47
  108.7 1.2 %collective-permute-done.41 = f32[64,128]{1,0:T(8,128)S(1)} collective-permute-done((f32[64,128]{1,0:T(8,128)S(1)}, f32[64,128]{1,0:T(8,128)S(1)}, u32[]{:S(2)}, u32[]{:S(2)}) %collective-permute-start.41) | collective-permute-done | bytes 32800 | tf_op jit(solution)/shard_map/ppermute | solution.py:47
  109.9 0.9 shard_map.51
  (30 shorter events, 4.3 us)
Async XLA Ops:
  0.0 41.6 %copy-start.1 = (f32[64,64]{1,0:T(8,128)S(1)}, f32[64,64]{1,0:T(8,128)}, u32[]{:S(2)}) copy-start(f32[64,64]{1,0:T(8,128)} %refs_1_.5) | copy-start | bytes 49156
  0.0 41.6 %copy-start.2 = (f32[128,64]{0,1:T(8,128)S(1)}, f32[128,64]{0,1:T(8,128)}, u32[]{:S(2)}) copy-start(f32[128,64]{0,1:T(8,128)} %param.7) | copy-start | bytes 98308
  23.3 88.2 %copy-start = (f32[2048,64]{0,1:T(8,128)S(1)}, f32[2048,64]{0,1:T(8,128)}, u32[]{:S(2)}) copy-start(f32[2048,64]{0,1:T(8,128)} %param.8) | copy-start | bytes 1572868
  23.3 7.1 %collective-permute-start.23 = (f32[72,128]{1,0:T(8,128)S(1)}, f32[72,128]{1,0:T(8,128)S(1)}, u32[]{:S(2)}, u32[]{:S(2)}) collective-permute-start(f32[72,128]{1,0:T(8,128)S(1)} %get-tuple-element.46), channel_id=1, source_target_pairs={{0,3},{1,2},{2,1},{3,0},{4,7},{5,6},{6,5},{7,4},{8,11},{9,10},{10,... | collective-permute-start | bytes 110600 | tf_op jit(solution)/shard_map/ppermute | solution.py:47
  28.4 4.9 %collective-permute-start.22 = (f32[72,128]{1,0:T(8,128)S(1)}, f32[72,128]{1,0:T(8,128)S(1)}, u32[]{:S(2)}, u32[]{:S(2)}) collective-permute-start(f32[72,128]{1,0:T(8,128)S(1)} %get-tuple-element.46), channel_id=1, source_target_pairs={{0,2},{1,3},{2,0},{3,1},{4,6},{5,7},{6,4},{7,5},{8,10},{9,11},{10,... | collective-permute-start | bytes 110600 | tf_op jit(solution)/shard_map/ppermute | solution.py:47
  28.4 4.9 %collective-permute-start.21 = (f32[72,128]{1,0:T(8,128)S(1)}, f32[72,128]{1,0:T(8,128)S(1)}, u32[]{:S(2)}, u32[]{:S(2)}) collective-permute-start(f32[72,128]{1,0:T(8,128)S(1)} %get-tuple-element.46), channel_id=1, source_target_pairs={{0,1},{1,0},{2,3},{3,2},{4,5},{5,4},{6,7},{7,6},{8,9},{9,8},{10,11... | collective-permute-start | bytes 110600 | tf_op jit(solution)/shard_map/ppermute | solution.py:47
  33.3 5.2 %collective-permute-start.26 = (f32[72,128]{1,0:T(8,128)S(1)}, f32[72,128]{1,0:T(8,128)S(1)}, u32[]{:S(2)}, u32[]{:S(2)}) collective-permute-start(f32[72,128]{1,0:T(8,128)S(1)} %add_add_fusion.7), channel_id=1, source_target_pairs={{0,24},{4,28},{8,16},{12,20},{16,8},{20,12},{24,0},{28,4},{1,25},{... | collective-permute-start | bytes 110600 | tf_op jit(solution)/shard_map/ppermute | solution.py:47
  35.8 4.0 %collective-permute-start.25 = (f32[72,128]{1,0:T(8,128)S(1)}, f32[72,128]{1,0:T(8,128)S(1)}, u32[]{:S(2)}, u32[]{:S(2)}) collective-permute-start(f32[72,128]{1,0:T(8,128)S(1)} %add_add_fusion.7), channel_id=1, source_target_pairs={{0,16},{4,20},{8,24},{12,28},{16,0},{20,4},{24,8},{28,12},{1,17},{... | collective-permute-start | bytes 110600 | tf_op jit(solution)/shard_map/ppermute | solution.py:47
  36.3 4.0 %collective-permute-start.24 = (f32[72,128]{1,0:T(8,128)S(1)}, f32[72,128]{1,0:T(8,128)S(1)}, u32[]{:S(2)}, u32[]{:S(2)}) collective-permute-start(f32[72,128]{1,0:T(8,128)S(1)} %add_add_fusion.7), channel_id=1, source_target_pairs={{0,8},{4,12},{8,0},{12,4},{16,24},{20,28},{24,16},{28,20},{1,9},{5... | collective-permute-start | bytes 110600 | tf_op jit(solution)/shard_map/ppermute | solution.py:47
  40.3 1.3 %collective-permute-start.27 = (f32[72,128]{1,0:T(8,128)S(1)}, f32[72,128]{1,0:T(8,128)S(1)}, u32[]{:S(2)}, u32[]{:S(2)}) collective-permute-start(f32[72,128]{1,0:T(8,128)S(1)} %add_add_fusion.6), channel_id=1, source_target_pairs={{0,4},{4,0},{8,12},{12,8},{16,20},{20,16},{24,28},{28,24},{1,5},{5... | collective-permute-start | bytes 110600 | tf_op jit(solution)/shard_map/ppermute | solution.py:47
  61.0 6.0 %collective-permute-start.30 = (f32[64,128]{1,0:T(8,128)S(1)}, f32[64,128]{1,0:T(8,128)S(1)}, u32[]{:S(2)}, u32[]{:S(2)}) collective-permute-start(f32[64,128]{1,0:T(8,128)S(1)} %get-tuple-element.50), channel_id=1, source_target_pairs={{0,3},{1,2},{2,1},{3,0},{4,7},{5,6},{6,5},{7,4},{8,11},{9,10},{10,... | collective-permute-start | bytes 98312 | tf_op jit(solution)/shard_map/ppermute | solution.py:47
  62.5 5.0 %collective-permute-start.29 = (f32[64,128]{1,0:T(8,128)S(1)}, f32[64,128]{1,0:T(8,128)S(1)}, u32[]{:S(2)}, u32[]{:S(2)}) collective-permute-start(f32[64,128]{1,0:T(8,128)S(1)} %get-tuple-element.50), channel_id=1, source_target_pairs={{0,2},{1,3},{2,0},{3,1},{4,6},{5,7},{6,4},{7,5},{8,10},{9,11},{10,... | collective-permute-start | bytes 98312 | tf_op jit(solution)/shard_map/ppermute | solution.py:47
  63.1 4.6 %collective-permute-start.28 = (f32[64,128]{1,0:T(8,128)S(1)}, f32[64,128]{1,0:T(8,128)S(1)}, u32[]{:S(2)}, u32[]{:S(2)}) collective-permute-start(f32[64,128]{1,0:T(8,128)S(1)} %get-tuple-element.50), channel_id=1, source_target_pairs={{0,1},{1,0},{2,3},{3,2},{4,5},{5,4},{6,7},{7,6},{8,9},{9,8},{10,11... | collective-permute-start | bytes 98312 | tf_op jit(solution)/shard_map/ppermute | solution.py:47
  67.7 5.1 %collective-permute-start.33 = (f32[64,128]{1,0:T(8,128)S(1)}, f32[64,128]{1,0:T(8,128)S(1)}, u32[]{:S(2)}, u32[]{:S(2)}) collective-permute-start(f32[64,128]{1,0:T(8,128)S(1)} %add_add_fusion.11), channel_id=1, source_target_pairs={{0,24},{4,28},{8,16},{12,20},{16,8},{20,12},{24,0},{28,4},{1,25},{... | collective-permute-start | bytes 98312 | tf_op jit(solution)/shard_map/ppermute | solution.py:47
  69.2 3.9 %collective-permute-start.32 = (f32[64,128]{1,0:T(8,128)S(1)}, f32[64,128]{1,0:T(8,128)S(1)}, u32[]{:S(2)}, u32[]{:S(2)}) collective-permute-start(f32[64,128]{1,0:T(8,128)S(1)} %add_add_fusion.11), channel_id=1, source_target_pairs={{0,16},{4,20},{8,24},{12,28},{16,0},{20,4},{24,8},{28,12},{1,17},{... | collective-permute-start | bytes 98312 | tf_op jit(solution)/shard_map/ppermute | solution.py:47
  69.8 3.9 %collective-permute-start.31 = (f32[64,128]{1,0:T(8,128)S(1)}, f32[64,128]{1,0:T(8,128)S(1)}, u32[]{:S(2)}, u32[]{:S(2)}) collective-permute-start(f32[64,128]{1,0:T(8,128)S(1)} %add_add_fusion.11), channel_id=1, source_target_pairs={{0,8},{4,12},{8,0},{12,4},{16,24},{20,28},{24,16},{28,20},{1,9},{5... | collective-permute-start | bytes 98312 | tf_op jit(solution)/shard_map/ppermute | solution.py:47
  73.7 1.3 %collective-permute-start.34 = (f32[64,128]{1,0:T(8,128)S(1)}, f32[64,128]{1,0:T(8,128)S(1)}, u32[]{:S(2)}, u32[]{:S(2)}) collective-permute-start(f32[64,128]{1,0:T(8,128)S(1)} %add_add_fusion.10), channel_id=1, source_target_pairs={{0,4},{4,0},{8,12},{12,8},{16,20},{20,16},{24,28},{28,24},{1,5},{5... | collective-permute-start | bytes 98312 | tf_op jit(solution)/shard_map/ppermute | solution.py:47
  94.3 5.8 %collective-permute-start.37 = (f32[64,128]{1,0:T(8,128)S(1)}, f32[64,128]{1,0:T(8,128)S(1)}, u32[]{:S(2)}, u32[]{:S(2)}) collective-permute-start(f32[64,128]{1,0:T(8,128)S(1)} %get-tuple-element.54), channel_id=1, source_target_pairs={{0,3},{1,2},{2,1},{3,0},{4,7},{5,6},{6,5},{7,4},{8,11},{9,10},{10,... | collective-permute-start | bytes 98312 | tf_op jit(solution)/shard_map/ppermute | solution.py:47
  96.6 4.9 %collective-permute-start.36 = (f32[64,128]{1,0:T(8,128)S(1)}, f32[64,128]{1,0:T(8,128)S(1)}, u32[]{:S(2)}, u32[]{:S(2)}) collective-permute-start(f32[64,128]{1,0:T(8,128)S(1)} %get-tuple-element.54), channel_id=1, source_target_pairs={{0,2},{1,3},{2,0},{3,1},{4,6},{5,7},{6,4},{7,5},{8,10},{9,11},{10,... | collective-permute-start | bytes 98312 | tf_op jit(solution)/shard_map/ppermute | solution.py:47
  97.4 4.3 %collective-permute-start.35 = (f32[64,128]{1,0:T(8,128)S(1)}, f32[64,128]{1,0:T(8,128)S(1)}, u32[]{:S(2)}, u32[]{:S(2)}) collective-permute-start(f32[64,128]{1,0:T(8,128)S(1)} %get-tuple-element.54), channel_id=1, source_target_pairs={{0,1},{1,0},{2,3},{3,2},{4,5},{5,4},{6,7},{7,6},{8,9},{9,8},{10,11... | collective-permute-start | bytes 98312 | tf_op jit(solution)/shard_map/ppermute | solution.py:47
  101.7 4.9 %collective-permute-start.40 = (f32[64,128]{1,0:T(8,128)S(1)}, f32[64,128]{1,0:T(8,128)S(1)}, u32[]{:S(2)}, u32[]{:S(2)}) collective-permute-start(f32[64,128]{1,0:T(8,128)S(1)} %add_add_fusion.9), channel_id=1, source_target_pairs={{0,24},{4,28},{8,16},{12,20},{16,8},{20,12},{24,0},{28,4},{1,25},{... | collective-permute-start | bytes 98312 | tf_op jit(solution)/shard_map/ppermute | solution.py:47
  104.2 3.9 %collective-permute-start.39 = (f32[64,128]{1,0:T(8,128)S(1)}, f32[64,128]{1,0:T(8,128)S(1)}, u32[]{:S(2)}, u32[]{:S(2)}) collective-permute-start(f32[64,128]{1,0:T(8,128)S(1)} %add_add_fusion.9), channel_id=1, source_target_pairs={{0,16},{4,20},{8,24},{12,28},{16,0},{20,4},{24,8},{28,12},{1,17},{... | collective-permute-start | bytes 98312 | tf_op jit(solution)/shard_map/ppermute | solution.py:47
  104.7 3.9 %collective-permute-start.38 = (f32[64,128]{1,0:T(8,128)S(1)}, f32[64,128]{1,0:T(8,128)S(1)}, u32[]{:S(2)}, u32[]{:S(2)}) collective-permute-start(f32[64,128]{1,0:T(8,128)S(1)} %add_add_fusion.9), channel_id=1, source_target_pairs={{0,8},{4,12},{8,0},{12,4},{16,24},{20,28},{24,16},{28,20},{1,9},{5... | collective-permute-start | bytes 98312 | tf_op jit(solution)/shard_map/ppermute | solution.py:47
  108.6 1.3 %collective-permute-start.41 = (f32[64,128]{1,0:T(8,128)S(1)}, f32[64,128]{1,0:T(8,128)S(1)}, u32[]{:S(2)}, u32[]{:S(2)}) collective-permute-start(f32[64,128]{1,0:T(8,128)S(1)} %add_add_fusion.8), channel_id=1, source_target_pairs={{0,4},{4,0},{8,12},{12,8},{16,20},{20,16},{24,28},{28,24},{1,5},{5... | collective-permute-start | bytes 98312 | tf_op jit(solution)/shard_map/ppermute | solution.py:47

commit v9 on v7

--- a/solution.py
+++ b/solution.py
@@ -113,6 +113,8 @@
         ).T.astype(BF16)
         phi_w[:, 2 * rank:] = jnp.zeros((items, COLUMNS - 2 * rank), BF16)
         factor_s[...] = r["factor_t"][...].T
+        n_item, n_week = (dict(axes)[a] for a in ("item", "week"))
+        r["phi_out"][users // 2:, :] = column_sums(r["item_t"][...], r["week"][...], n_item, n_week)
     else:
         summed = r["summed"][...]
         if iteration == 1:
@@ -172,7 +174,7 @@
                 pltpu.matmul_acc_lhs(total[n], parts[0], None if n else 0)
                 for part in parts[1:]:
                     pltpu.matmul_acc_lhs(total[n], part)
-                if n == len(strips) // 2:
+                if n == 3 * len(strips) // 4:
                     push_phi(chunk + 1)
 
             for chunk in range(chunks):
@@ -185,7 +187,7 @@
                         lhs = operand(after + n)
                         lhs_s[strip, :] = lhs
                     pltpu.matmul_acc_lhs(ahead[n], lhs, None if n else 0)
-                    if n == len(strips) // 2:
+                    if n == len(strips) // 4:
                         push_model(chunk + 2)
                     if stream:
                         count = r["slots"][lax.rem(block, SLOTS), n, :, at]
@@ -225,9 +227,6 @@
 
     pl.run_scoped(matmuls, *[[unit] * tile for unit in units])
     r["phi_out"][: users // 2, :] = pack(phi_s[...])
-    if first:
-        n_item, n_week = (dict(axes)[a] for a in ("item", "week"))
-        r["phi_out"][users // 2:, :] = column_sums(r["item_t"][...], r["week"][...], n_item, n_week)
 
 
 def last_kernel(factor, summed, den, sound, out, sound_out):

time: 112 us -> 113 us (level)
  no operation moved by 1% of the time
where the time goes in v9:
time: 113 us; the launch traced here: 112 us
  Pallas kernels  63.5 us (56%)
  starting transfers between devices  25.4 us (22%)
  waiting for transfers between devices  22.3 us (20%)
    pallas_call x3, Pallas kernels, sweep(): pl.pallas_call(functools.partial(sweep_kernel, iteration, exact, axes, na...  62.6 us
    ppermute x21, starting transfers between devices, sum_over(): parts.append(lax.ppermute(x, axis, partners))  25.4 us
    ppermute x21, waiting for transfers between devices, sum_over(): parts.append(lax.ppermute(x, axis, partners))  22.3 us
  transfers between devices with their start and end apart: 21, of which 20 were waited for; matrix products, arithmetic and copies ran while one was open for 0% of the time, Pallas kernels for 0%

profile of v9, /device:TPU:0, one launch (start us, length us, event | category | flops | bytes accessed | tf_op | source)
XLA Modules:
  0.0 112.4 jit_solution(2199436396238564746)
XLA Ops:
  0.0 23.1 %shard_map.48 = (f32[72,128]{1,0:T(8,128)S(1)}, bf16[256,2048]{1,0:T(8,128)(2,1)S(1)}, bf16[2048,256]{1,0:T(8,128)(2,1)S(1)}, f8e4m3fn[128,64,2048]{2,1,0:T(32,128)(4,1)S(1)}) custom-call(s32[128,64,2048]{2,1,0:T(8,128)} %refs_0_.1, f32[64,64]{1,0:T(8,128)} %refs_1_.5, f32[64,128]{1,0:T(8,128)} %bitcast.9, f32[64,2048]{1,0:T(8,128)} %bitcast.7), custom_call_target="tpu_custom_call" | custom-call | flops 17179869184 | bytes 67108864 | tf_op jit(solution)/shard_map/pallas_call | solution.py:265
  23.1 5.1 %collective-permute-start.23 = (f32[72,128]{1,0:T(8,128)S(1)}, f32[72,128]{1,0:T(8,128)S(1)}, u32[]{:S(2)}, u32[]{:S(2)}) collective-permute-start(f32[72,128]{1,0:T(8,128)S(1)} %get-tuple-element.46), channel_id=1, source_target_pairs={{0,3},{1,2},{2,1},{3,0},{4,7},{5,6},{6,5},{7,4},{8,11},{9,10},{10,... | collective-permute-start | bytes 110600 | tf_op jit(solution)/shard_map/ppermute | solution.py:47
  28.3 0.6 collective-permute-start.21
  28.9 1.3 %collective-permute-done.23 = f32[72,128]{1,0:T(8,128)S(1)} collective-permute-done((f32[72,128]{1,0:T(8,128)S(1)}, f32[72,128]{1,0:T(8,128)S(1)}, u32[]{:S(2)}, u32[]{:S(2)}) %collective-permute-start.23) | collective-permute-done | bytes 36896 | tf_op jit(solution)/shard_map/ppermute | solution.py:47
  30.2 2.9 %collective-permute-done.22 = f32[72,128]{1,0:T(8,128)S(1)} collective-permute-done((f32[72,128]{1,0:T(8,128)S(1)}, f32[72,128]{1,0:T(8,128)S(1)}, u32[]{:S(2)}, u32[]{:S(2)}) %collective-permute-start.22) | collective-permute-done | bytes 36896 | tf_op jit(solution)/shard_map/ppermute | solution.py:47
  33.1 2.5 %collective-permute-start.26 = (f32[72,128]{1,0:T(8,128)S(1)}, f32[72,128]{1,0:T(8,128)S(1)}, u32[]{:S(2)}, u32[]{:S(2)}) collective-permute-start(f32[72,128]{1,0:T(8,128)S(1)} %add_add_fusion.7), channel_id=1, source_target_pairs={{0,24},{4,28},{8,16},{12,20},{16,8},{20,12},{24,0},{28,4},{1,25},{... | collective-permute-start | bytes 110600 | tf_op jit(solution)/shard_map/ppermute | solution.py:47
  36.2 0.5 collective-permute-start.24
  36.7 1.6 %collective-permute-done.26 = f32[72,128]{1,0:T(8,128)S(1)} collective-permute-done((f32[72,128]{1,0:T(8,128)S(1)}, f32[72,128]{1,0:T(8,128)S(1)}, u32[]{:S(2)}, u32[]{:S(2)}) %collective-permute-start.26) | collective-permute-done | bytes 36896 | tf_op jit(solution)/shard_map/ppermute | solution.py:47
  38.3 1.3 %collective-permute-done.25 = f32[72,128]{1,0:T(8,128)S(1)} collective-permute-done((f32[72,128]{1,0:T(8,128)S(1)}, f32[72,128]{1,0:T(8,128)S(1)}, u32[]{:S(2)}, u32[]{:S(2)}) %collective-permute-start.25) | collective-permute-done | bytes 36896 | tf_op jit(solution)/shard_map/ppermute | solution.py:47
  40.2 1.2 %collective-permute-done.27 = f32[72,128]{1,0:T(8,128)S(1)} collective-permute-done((f32[72,128]{1,0:T(8,128)S(1)}, f32[72,128]{1,0:T(8,128)S(1)}, u32[]{:S(2)}, u32[]{:S(2)}) %collective-permute-start.27) | collective-permute-done | bytes 36896 | tf_op jit(solution)/shard_map/ppermute | solution.py:47
  41.4 19.8 %shard_map.49 = (f32[64,128]{1,0:T(8,128)S(1)}, f32[128,64]{1,0:T(8,128)S(1)}, f32[8,128]{1,0:T(8,128)S(1)}, f32[8,64]{1,0:T(8,128)S(1)}) custom-call(f8e4m3fn[128,64,2048]{2,1,0:T(32,128)(4,1)S(1)} %get-tuple-element.45.refs_0_, f32[64,64]{1,0:T(8,128)S(1)} %copy-done.1, f32[64,128]{1,0:T(8,128)S(1)} %bitcast.10, f32[72,128]{1,0:T(8,128)S(1)} %add.132.refs_3_, ...), custom_call_target="tpu_custom_call" | custom-call | flops 17179869184 | bytes 67108864 | tf_op jit(solution)/shard_map/pallas_call | solution.py:265
  61.2 1.5 %collective-permute-start.30 = (f32[64,128]{1,0:T(8,128)S(1)}, f32[64,128]{1,0:T(8,128)S(1)}, u32[]{:S(2)}, u32[]{:S(2)}) collective-permute-start(f32[64,128]{1,0:T(8,128)S(1)} %get-tuple-element.50), channel_id=1, source_target_pairs={{0,3},{1,2},{2,1},{3,0},{4,7},{5,6},{6,5},{7,4},{8,11},{9,10},{10,... | collective-permute-start | bytes 98312 | tf_op jit(solution)/shard_map/ppermute | solution.py:47
  62.7 0.6 collective-permute-start.29
  63.3 2.3 %collective-permute-start.28 = (f32[64,128]{1,0:T(8,128)S(1)}, f32[64,128]{1,0:T(8,128)S(1)}, u32[]{:S(2)}, u32[]{:S(2)}) collective-permute-start(f32[64,128]{1,0:T(8,128)S(1)} %get-tuple-element.50), channel_id=1, source_target_pairs={{0,1},{1,0},{2,3},{3,2},{4,5},{5,4},{6,7},{7,6},{8,9},{9,8},{10,11... | collective-permute-start | bytes 98312 | tf_op jit(solution)/shard_map/ppermute | solution.py:47
  65.6 1.6 %collective-permute-done.30 = f32[64,128]{1,0:T(8,128)S(1)} collective-permute-done((f32[64,128]{1,0:T(8,128)S(1)}, f32[64,128]{1,0:T(8,128)S(1)}, u32[]{:S(2)}, u32[]{:S(2)}) %collective-permute-start.30) | collective-permute-done | bytes 32800 | tf_op jit(solution)/shard_map/ppermute | solution.py:47
  67.9 1.6 %collective-permute-start.33 = (f32[64,128]{1,0:T(8,128)S(1)}, f32[64,128]{1,0:T(8,128)S(1)}, u32[]{:S(2)}, u32[]{:S(2)}) collective-permute-start(f32[64,128]{1,0:T(8,128)S(1)} %add_add_fusion.11), channel_id=1, source_target_pairs={{0,24},{4,28},{8,16},{12,20},{16,8},{20,12},{24,0},{28,4},{1,25},{... | collective-permute-start | bytes 98312 | tf_op jit(solution)/shard_map/ppermute | solution.py:47
  69.5 0.5 collective-permute-start.32
  70.0 1.5 %collective-permute-start.31 = (f32[64,128]{1,0:T(8,128)S(1)}, f32[64,128]{1,0:T(8,128)S(1)}, u32[]{:S(2)}, u32[]{:S(2)}) collective-permute-start(f32[64,128]{1,0:T(8,128)S(1)} %add_add_fusion.11), channel_id=1, source_target_pairs={{0,8},{4,12},{8,0},{12,4},{16,24},{20,28},{24,16},{28,20},{1,9},{5... | collective-permute-start | bytes 98312 | tf_op jit(solution)/shard_map/ppermute | solution.py:47
  71.5 1.5 %collective-permute-done.33 = f32[64,128]{1,0:T(8,128)S(1)} collective-permute-done((f32[64,128]{1,0:T(8,128)S(1)}, f32[64,128]{1,0:T(8,128)S(1)}, u32[]{:S(2)}, u32[]{:S(2)}) %collective-permute-start.33) | collective-permute-done | bytes 32800 | tf_op jit(solution)/shard_map/ppermute | solution.py:47
  74.0 1.2 %collective-permute-done.34 = f32[64,128]{1,0:T(8,128)S(1)} collective-permute-done((f32[64,128]{1,0:T(8,128)S(1)}, f32[64,128]{1,0:T(8,128)S(1)}, u32[]{:S(2)}, u32[]{:S(2)}) %collective-permute-start.34) | collective-permute-done | bytes 32800 | tf_op jit(solution)/shard_map/ppermute | solution.py:47
  75.2 19.7 %shard_map.50 = (f32[64,128]{1,0:T(8,128)S(1)}, f32[128,64]{1,0:T(8,128)S(1)}, f32[8,128]{1,0:T(8,128)S(1)}) custom-call(f8e4m3fn[128,64,2048]{2,1,0:T(32,128)(4,1)S(1)} %get-tuple-element.45.refs_0_, f32[64,64]{1,0:T(8,128)S(1)} %copy-done.1, f32[128,64]{1,0:T(8,128)S(1)} %get-tuple-element.49.refs_2_, f32[64,128]{1,0:T(8,128)S(1)} %add.139.refs_3_, ...), custom_call_target="tpu_custom_call" | custom-call | flops 17179869184 | bytes 67108864 | tf_op jit(solution)/shard_map/pallas_call | solution.py:265
  94.9 2.3 %collective-permute-start.37 = (f32[64,128]{1,0:T(8,128)S(1)}, f32[64,128]{1,0:T(8,128)S(1)}, u32[]{:S(2)}, u32[]{:S(2)}) collective-permute-start(f32[64,128]{1,0:T(8,128)S(1)} %get-tuple-element.54), channel_id=1, source_target_pairs={{0,3},{1,2},{2,1},{3,0},{4,7},{5,6},{6,5},{7,4},{8,11},{9,10},{10,... | collective-permute-start | bytes 98312 | tf_op jit(solution)/shard_map/ppermute | solution.py:47
  97.2 0.8 collective-permute-start.36
  98.0 1.3 %collective-permute-start.35 = (f32[64,128]{1,0:T(8,128)S(1)}, f32[64,128]{1,0:T(8,128)S(1)}, u32[]{:S(2)}, u32[]{:S(2)}) collective-permute-start(f32[64,128]{1,0:T(8,128)S(1)} %get-tuple-element.54), channel_id=1, source_target_pairs={{0,1},{1,0},{2,3},{3,2},{4,5},{5,4},{6,7},{7,6},{8,9},{9,8},{10,11... | collective-permute-start | bytes 98312 | tf_op jit(solution)/shard_map/ppermute | solution.py:47
  99.3 1.5 %collective-permute-done.37 = f32[64,128]{1,0:T(8,128)S(1)} collective-permute-done((f32[64,128]{1,0:T(8,128)S(1)}, f32[64,128]{1,0:T(8,128)S(1)}, u32[]{:S(2)}, u32[]{:S(2)}) %collective-permute-start.37) | collective-permute-done | bytes 32800 | tf_op jit(solution)/shard_map/ppermute | solution.py:47
  100.7 1.3 %collective-permute-done.36 = f32[64,128]{1,0:T(8,128)S(1)} collective-permute-done((f32[64,128]{1,0:T(8,128)S(1)}, f32[64,128]{1,0:T(8,128)S(1)}, u32[]{:S(2)}, u32[]{:S(2)}) %collective-permute-start.36) | collective-permute-done | bytes 32800 | tf_op jit(solution)/shard_map/ppermute | solution.py:47
  102.3 2.5 %collective-permute-start.40 = (f32[64,128]{1,0:T(8,128)S(1)}, f32[64,128]{1,0:T(8,128)S(1)}, u32[]{:S(2)}, u32[]{:S(2)}) collective-permute-start(f32[64,128]{1,0:T(8,128)S(1)} %add_add_fusion.9), channel_id=1, source_target_pairs={{0,24},{4,28},{8,16},{12,20},{16,8},{20,12},{24,0},{28,4},{1,25},{... | collective-permute-start | bytes 98312 | tf_op jit(solution)/shard_map/ppermute | solution.py:47
  105.3 0.5 collective-permute-start.38
  105.8 1.3 %collective-permute-done.40 = f32[64,128]{1,0:T(8,128)S(1)} collective-permute-done((f32[64,128]{1,0:T(8,128)S(1)}, f32[64,128]{1,0:T(8,128)S(1)}, u32[]{:S(2)}, u32[]{:S(2)}) %collective-permute-start.40) | collective-permute-done | bytes 32800 | tf_op jit(solution)/shard_map/ppermute | solution.py:47
  107.2 1.5 %collective-permute-done.39 = f32[64,128]{1,0:T(8,128)S(1)} collective-permute-done((f32[64,128]{1,0:T(8,128)S(1)}, f32[64,128]{1,0:T(8,128)S(1)}, u32[]{:S(2)}, u32[]{:S(2)}) %collective-permute-start.39) | collective-permute-done | bytes 32800 | tf_op jit(solution)/shard_map/ppermute | solution.py:47
  109.3 1.2 %collective-permute-done.41 = f32[64,128]{1,0:T(8,128)S(1)} collective-permute-done((f32[64,128]{1,0:T(8,128)S(1)}, f32[64,128]{1,0:T(8,128)S(1)}, u32[]{:S(2)}, u32[]{:S(2)}) %collective-permute-start.41) | collective-permute-done | bytes 32800 | tf_op jit(solution)/shard_map/ppermute | solution.py:47
  110.5 0.9 shard_map.51
  (30 shorter events, 4.3 us)
Async XLA Ops:
  0.0 41.4 %copy-start.1 = (f32[64,64]{1,0:T(8,128)S(1)}, f32[64,64]{1,0:T(8,128)}, u32[]{:S(2)}) copy-start(f32[64,64]{1,0:T(8,128)} %refs_1_.5) | copy-start | bytes 49156
  0.0 41.4 %copy-start.2 = (f32[128,64]{0,1:T(8,128)S(1)}, f32[128,64]{0,1:T(8,128)}, u32[]{:S(2)}) copy-start(f32[128,64]{0,1:T(8,128)} %param.7) | copy-start | bytes 98308
  23.1 89.0 %copy-start = (f32[2048,64]{0,1:T(8,128)S(1)}, f32[2048,64]{0,1:T(8,128)}, u32[]{:S(2)}) copy-start(f32[2048,64]{0,1:T(8,128)} %param.8) | copy-start | bytes 1572868
  23.1 7.1 %collective-permute-start.23 = (f32[72,128]{1,0:T(8,128)S(1)}, f32[72,128]{1,0:T(8,128)S(1)}, u32[]{:S(2)}, u32[]{:S(2)}) collective-permute-start(f32[72,128]{1,0:T(8,128)S(1)} %get-tuple-element.46), channel_id=1, source_target_pairs={{0,3},{1,2},{2,1},{3,0},{4,7},{5,6},{6,5},{7,4},{8,11},{9,10},{10,... | collective-permute-start | bytes 110600 | tf_op jit(solution)/shard_map/ppermute | solution.py:47
  28.3 4.9 %collective-permute-start.22 = (f32[72,128]{1,0:T(8,128)S(1)}, f32[72,128]{1,0:T(8,128)S(1)}, u32[]{:S(2)}, u32[]{:S(2)}) collective-permute-start(f32[72,128]{1,0:T(8,128)S(1)} %get-tuple-element.46), channel_id=1, source_target_pairs={{0,2},{1,3},{2,0},{3,1},{4,6},{5,7},{6,4},{7,5},{8,10},{9,11},{10,... | collective-permute-start | bytes 110600 | tf_op jit(solution)/shard_map/ppermute | solution.py:47
  28.3 4.9 %collective-permute-start.21 = (f32[72,128]{1,0:T(8,128)S(1)}, f32[72,128]{1,0:T(8,128)S(1)}, u32[]{:S(2)}, u32[]{:S(2)}) collective-permute-start(f32[72,128]{1,0:T(8,128)S(1)} %get-tuple-element.46), channel_id=1, source_target_pairs={{0,1},{1,0},{2,3},{3,2},{4,5},{5,4},{6,7},{7,6},{8,9},{9,8},{10,11... | collective-permute-start | bytes 110600 | tf_op jit(solution)/shard_map/ppermute | solution.py:47
  33.1 5.2 %collective-permute-start.26 = (f32[72,128]{1,0:T(8,128)S(1)}, f32[72,128]{1,0:T(8,128)S(1)}, u32[]{:S(2)}, u32[]{:S(2)}) collective-permute-start(f32[72,128]{1,0:T(8,128)S(1)} %add_add_fusion.7), channel_id=1, source_target_pairs={{0,24},{4,28},{8,16},{12,20},{16,8},{20,12},{24,0},{28,4},{1,25},{... | collective-permute-start | bytes 110600 | tf_op jit(solution)/shard_map/ppermute | solution.py:47
  35.7 4.0 %collective-permute-start.25 = (f32[72,128]{1,0:T(8,128)S(1)}, f32[72,128]{1,0:T(8,128)S(1)}, u32[]{:S(2)}, u32[]{:S(2)}) collective-permute-start(f32[72,128]{1,0:T(8,128)S(1)} %add_add_fusion.7), channel_id=1, source_target_pairs={{0,16},{4,20},{8,24},{12,28},{16,0},{20,4},{24,8},{28,12},{1,17},{... | collective-permute-start | bytes 110600 | tf_op jit(solution)/shard_map/ppermute | solution.py:47
  36.2 4.0 %collective-permute-start.24 = (f32[72,128]{1,0:T(8,128)S(1)}, f32[72,128]{1,0:T(8,128)S(1)}, u32[]{:S(2)}, u32[]{:S(2)}) collective-permute-start(f32[72,128]{1,0:T(8,128)S(1)} %add_add_fusion.7), channel_id=1, source_target_pairs={{0,8},{4,12},{8,0},{12,4},{16,24},{20,28},{24,16},{28,20},{1,9},{5... | collective-permute-start | bytes 110600 | tf_op jit(solution)/shard_map/ppermute | solution.py:47
  40.1 1.3 %collective-permute-start.27 = (f32[72,128]{1,0:T(8,128)S(1)}, f32[72,128]{1,0:T(8,128)S(1)}, u32[]{:S(2)}, u32[]{:S(2)}) collective-permute-start(f32[72,128]{1,0:T(8,128)S(1)} %add_add_fusion.6), channel_id=1, source_target_pairs={{0,4},{4,0},{8,12},{12,8},{16,20},{20,16},{24,28},{28,24},{1,5},{5... | collective-permute-start | bytes 110600 | tf_op jit(solution)/shard_map/ppermute | solution.py:47
  61.2 6.0 %collective-permute-start.30 = (f32[64,128]{1,0:T(8,128)S(1)}, f32[64,128]{1,0:T(8,128)S(1)}, u32[]{:S(2)}, u32[]{:S(2)}) collective-permute-start(f32[64,128]{1,0:T(8,128)S(1)} %get-tuple-element.50), channel_id=1, source_target_pairs={{0,3},{1,2},{2,1},{3,0},{4,7},{5,6},{6,5},{7,4},{8,11},{9,10},{10,... | collective-permute-start | bytes 98312 | tf_op jit(solution)/shard_map/ppermute | solution.py:47
  62.7 5.0 %collective-permute-start.29 = (f32[64,128]{1,0:T(8,128)S(1)}, f32[64,128]{1,0:T(8,128)S(1)}, u32[]{:S(2)}, u32[]{:S(2)}) collective-permute-start(f32[64,128]{1,0:T(8,128)S(1)} %get-tuple-element.50), channel_id=1, source_target_pairs={{0,2},{1,3},{2,0},{3,1},{4,6},{5,7},{6,4},{7,5},{8,10},{9,11},{10,... | collective-permute-start | bytes 98312 | tf_op jit(solution)/shard_map/ppermute | solution.py:47
  63.3 4.6 %collective-permute-start.28 = (f32[64,128]{1,0:T(8,128)S(1)}, f32[64,128]{1,0:T(8,128)S(1)}, u32[]{:S(2)}, u32[]{:S(2)}) collective-permute-start(f32[64,128]{1,0:T(8,128)S(1)} %get-tuple-element.50), channel_id=1, source_target_pairs={{0,1},{1,0},{2,3},{3,2},{4,5},{5,4},{6,7},{7,6},{8,9},{9,8},{10,11... | collective-permute-start | bytes 98312 | tf_op jit(solution)/shard_map/ppermute | solution.py:47
  67.9 5.1 %collective-permute-start.33 = (f32[64,128]{1,0:T(8,128)S(1)}, f32[64,128]{1,0:T(8,128)S(1)}, u32[]{:S(2)}, u32[]{:S(2)}) collective-permute-start(f32[64,128]{1,0:T(8,128)S(1)} %add_add_fusion.11), channel_id=1, source_target_pairs={{0,24},{4,28},{8,16},{12,20},{16,8},{20,12},{24,0},{28,4},{1,25},{... | collective-permute-start | bytes 98312 | tf_op jit(solution)/shard_map/ppermute | solution.py:47
  69.5 3.9 %collective-permute-start.32 = (f32[64,128]{1,0:T(8,128)S(1)}, f32[64,128]{1,0:T(8,128)S(1)}, u32[]{:S(2)}, u32[]{:S(2)}) collective-permute-start(f32[64,128]{1,0:T(8,128)S(1)} %add_add_fusion.11), channel_id=1, source_target_pairs={{0,16},{4,20},{8,24},{12,28},{16,0},{20,4},{24,8},{28,12},{1,17},{... | collective-permute-start | bytes 98312 | tf_op jit(solution)/shard_map/ppermute | solution.py:47
  70.0 3.9 %collective-permute-start.31 = (f32[64,128]{1,0:T(8,128)S(1)}, f32[64,128]{1,0:T(8,128)S(1)}, u32[]{:S(2)}, u32[]{:S(2)}) collective-permute-start(f32[64,128]{1,0:T(8,128)S(1)} %add_add_fusion.11), channel_id=1, source_target_pairs={{0,8},{4,12},{8,0},{12,4},{16,24},{20,28},{24,16},{28,20},{1,9},{5... | collective-permute-start | bytes 98312 | tf_op jit(solution)/shard_map/ppermute | solution.py:47
  73.9 1.3 %collective-permute-start.34 = (f32[64,128]{1,0:T(8,128)S(1)}, f32[64,128]{1,0:T(8,128)S(1)}, u32[]{:S(2)}, u32[]{:S(2)}) collective-permute-start(f32[64,128]{1,0:T(8,128)S(1)} %add_add_fusion.10), channel_id=1, source_target_pairs={{0,4},{4,0},{8,12},{12,8},{16,20},{20,16},{24,28},{28,24},{1,5},{5... | collective-permute-start | bytes 98312 | tf_op jit(solution)/shard_map/ppermute | solution.py:47
  94.9 5.8 %collective-permute-start.37 = (f32[64,128]{1,0:T(8,128)S(1)}, f32[64,128]{1,0:T(8,128)S(1)}, u32[]{:S(2)}, u32[]{:S(2)}) collective-permute-start(f32[64,128]{1,0:T(8,128)S(1)} %get-tuple-element.54), channel_id=1, source_target_pairs={{0,3},{1,2},{2,1},{3,0},{4,7},{5,6},{6,5},{7,4},{8,11},{9,10},{10,... | collective-permute-start | bytes 98312 | tf_op jit(solution)/shard_map/ppermute | solution.py:47
  97.2 4.9 %collective-permute-start.36 = (f32[64,128]{1,0:T(8,128)S(1)}, f32[64,128]{1,0:T(8,128)S(1)}, u32[]{:S(2)}, u32[]{:S(2)}) collective-permute-start(f32[64,128]{1,0:T(8,128)S(1)} %get-tuple-element.54), channel_id=1, source_target_pairs={{0,2},{1,3},{2,0},{3,1},{4,6},{5,7},{6,4},{7,5},{8,10},{9,11},{10,... | collective-permute-start | bytes 98312 | tf_op jit(solution)/shard_map/ppermute | solution.py:47
  98.0 4.3 %collective-permute-start.35 = (f32[64,128]{1,0:T(8,128)S(1)}, f32[64,128]{1,0:T(8,128)S(1)}, u32[]{:S(2)}, u32[]{:S(2)}) collective-permute-start(f32[64,128]{1,0:T(8,128)S(1)} %get-tuple-element.54), channel_id=1, source_target_pairs={{0,1},{1,0},{2,3},{3,2},{4,5},{5,4},{6,7},{7,6},{8,9},{9,8},{10,11... | collective-permute-start | bytes 98312 | tf_op jit(solution)/shard_map/ppermute | solution.py:47
  102.3 4.9 %collective-permute-start.40 = (f32[64,128]{1,0:T(8,128)S(1)}, f32[64,128]{1,0:T(8,128)S(1)}, u32[]{:S(2)}, u32[]{:S(2)}) collective-permute-start(f32[64,128]{1,0:T(8,128)S(1)} %add_add_fusion.9), channel_id=1, source_target_pairs={{0,24},{4,28},{8,16},{12,20},{16,8},{20,12},{24,0},{28,4},{1,25},{... | collective-permute-start | bytes 98312 | tf_op jit(solution)/shard_map/ppermute | solution.py:47
  104.8 3.9 %collective-permute-start.39 = (f32[64,128]{1,0:T(8,128)S(1)}, f32[64,128]{1,0:T(8,128)S(1)}, u32[]{:S(2)}, u32[]{:S(2)}) collective-permute-start(f32[64,128]{1,0:T(8,128)S(1)} %add_add_fusion.9), channel_id=1, source_target_pairs={{0,16},{4,20},{8,24},{12,28},{16,0},{20,4},{24,8},{28,12},{1,17},{... | collective-permute-start | bytes 98312 | tf_op jit(solution)/shard_map/ppermute | solution.py:47
  105.3 3.9 %collective-permute-start.38 = (f32[64,128]{1,0:T(8,128)S(1)}, f32[64,128]{1,0:T(8,128)S(1)}, u32[]{:S(2)}, u32[]{:S(2)}) collective-permute-start(f32[64,128]{1,0:T(8,128)S(1)} %add_add_fusion.9), channel_id=1, source_target_pairs={{0,8},{4,12},{8,0},{12,4},{16,24},{20,28},{24,16},{28,20},{1,9},{5... | collective-permute-start | bytes 98312 | tf_op jit(solution)/shard_map/ppermute | solution.py:47
  109.2 1.3 %collective-permute-start.41 = (f32[64,128]{1,0:T(8,128)S(1)}, f32[64,128]{1,0:T(8,128)S(1)}, u32[]{:S(2)}, u32[]{:S(2)}) collective-permute-start(f32[64,128]{1,0:T(8,128)S(1)} %add_add_fusion.8), channel_id=1, source_target_pairs={{0,4},{4,0},{8,12},{12,8},{16,20},{20,16},{24,28},{28,24},{1,5},{5... | collective-permute-start | bytes 98312 | tf_op jit(solution)/shard_map/ppermute | solution.py:47
